TPU v7x, 256 devices: a whole 4x4x8 slice. The times are simulated.
256 devices in a mesh: fsdp: 32 (over x, y, core), rep: 8 (over z).
Axes of the slice: x: 4, y: 4, z: 8, core: 2. Of those that a mesh axis runs over, the one named last changes fastest.
Arguments:
- gradient: bfloat16 [32, 1024, 1024], P(None, 'fsdp'), may hold values from -6 to 6
- block_owner: int32 [32], replicated, may hold values from 0 to 31, as said below
- block_slot: int32 [32], replicated, may hold values from 0 to 2
- left_state: float32 [32, 3, 1024, 1024], P('fsdp', None, 'rep'), may hold values from -6 to 6
- right_state: float32 [32, 3, 1024, 1024], P('fsdp', None, None, 'rep'), may hold values from -6 to 6
- left_root: bfloat16 [32, 3, 1024, 1024], P('fsdp', None, 'rep'), may hold values from -0.2 to 1.4
- right_root: bfloat16 [32, 3, 1024, 1024], P('fsdp', None, None, 'rep'), may hold values from -0.2 to 1.4
Outputs:
- update: bfloat16 [32, 1024, 1024], P(None, 'fsdp')
- left_factor: float32 [32, 3, 1024, 1024], P('fsdp', None, 'rep')
- right_factor: float32 [32, 3, 1024, 1024], P('fsdp', None, None, 'rep')
Inputs may be any that keep to these rules, and one draw needn't show every extreme that they name: The pairs (block_owner[i], block_slot[i]) are distinct; some owner holds blocks in all 3 of its slots.
All inputs are finite; a program needn't handle non-finite values.
Results may differ from a plain program's by a relative error of at most 0.0049.
Values may be sent and summed in bfloat16 or wider, within the bound.
No kernel may reach another device: no remote copies, remote signals or barrier semaphores. Data moves between devices by JAX's collectives and lax.ppermute only.
A program may use at most 128 MiB of HBM per device.

v0:
```python
import jax
import jax.numpy as jnp
from jax import lax
from jax.sharding import PartitionSpec as P

decay_rate = 0.95
epsilon = 1e-06


def local(gradient, block_owner, block_slot, left_state, right_state, left_root, right_root):
    owners_count = lax.axis_size("fsdp")
    replicas = lax.axis_size("rep")
    block_count, row_share, block_order = gradient.shape
    slot_count = left_state.shape[1]
    part_width = block_order // replicas
    rep_index = lax.axis_index("rep")
    positions = owners_count * slot_count
    flat_index = block_owner * slot_count + block_slot
    matches = flat_index[None, :] == jnp.arange(positions, dtype=jnp.int32)[:, None]
    occupied = jnp.any(matches, axis=1)
    sources = jnp.sum(
        jnp.where(matches, jnp.arange(block_count, dtype=jnp.int32)[None, :], 0), axis=1
    )
    packed = jnp.take(gradient, sources, axis=0) * occupied[:, None, None].astype(gradient.dtype)
    packed = packed.reshape(owners_count, slot_count, row_share, block_order)
    blocks = lax.all_to_all(packed, "fsdp", split_axis=0, concat_axis=2, tiled=True)
    blocks = blocks[0]
    own_rows = lax.dynamic_slice_in_dim(blocks, rep_index * part_width, part_width, 1)
    own_cols = lax.dynamic_slice_in_dim(blocks, rep_index * part_width, part_width, 2)
    left_products = jnp.einsum("kij,kmj->kim", own_rows, blocks, preferred_element_type=jnp.float32)
    right_products = jnp.einsum(
        "kji,kjc->kic", blocks, own_cols, preferred_element_type=jnp.float32
    )
    left_factor = decay_rate * left_state[0] + (1.0 - decay_rate) * left_products
    right_factor = decay_rate * right_state[0] + (1.0 - decay_rate) * right_products
    rooted = jnp.einsum(
        "kij,kjc->kic", blocks, right_root[0], preferred_element_type=jnp.float32
    ).astype(jnp.bfloat16)
    precond = jnp.einsum(
        "kij,kjc->kic",
        lax.all_gather(left_root[0], "rep", axis=1, tiled=True),
        rooted,
        preferred_element_type=jnp.float32,
    )
    pre_part = jnp.sum(precond * precond, axis=(1, 2))
    grad_squares = jnp.sum(jnp.square(blocks.astype(jnp.float32)), axis=(1, 2))
    pre_squares = lax.psum(pre_part, "rep")
    graft_scale = jnp.sqrt(grad_squares) / jnp.sqrt(pre_squares + epsilon)
    update_part = (precond * graft_scale[:, None, None]).astype(jnp.bfloat16)
    assembled = lax.all_gather(update_part, "rep", axis=2, tiled=True)
    outgoing = assembled.reshape(1, slot_count, owners_count, row_share, block_order)
    arrived = lax.all_to_all(outgoing, "fsdp", split_axis=2, concat_axis=0, tiled=True)
    arrived = arrived.reshape(positions, row_share, block_order)
    update = jnp.take(arrived, flat_index, axis=0)
    return (update, left_factor[None], right_factor[None])


def solution(mesh):
    in_specs = (
        P(None, "fsdp", None),
        P(),
        P(),
        P("fsdp", None, "rep", None),
        P("fsdp", None, None, "rep"),
        P("fsdp", None, "rep", None),
        P("fsdp", None, None, "rep"),
    )
    out_specs = (P(None, "fsdp", None), P("fsdp", None, "rep", None), P("fsdp", None, None, "rep"))
    return jax.shard_map(local, mesh=mesh, in_specs=in_specs, out_specs=out_specs, check_vma=False)
```

profile of v0, /device:TPU:8, one launch (start us, length us, event | category | flops | bytes accessed | tf_op | source)
XLA Modules:
  0.0 328.7 jit_solution(9790014694183485610)
XLA Ops:
  7.2 0.0 copy-start
  7.2 0.0 all-gather.6.cloned.1.call-start
  7.2 0.7 all-gather.6.cloned.1.call-update
  7.9 0.0 all-gather.4.cloned.1.call-start
  8.0 0.7 compare_and_fusion.1
  8.6 0.1 fusion.10
  8.7 0.1 reshape.58
  8.9 0.1 select_reduce_fusion
  9.0 0.1 reduce_sum.32
  9.1 0.0 copy-done
  9.1 5.9 %gather_fusion = bf16[96,32,1024]{2,1,0:T(8,128)(2,1)} fusion(bf16[32,32,1024]{2,1,0:T(8,128)(2,1)S(1)} %copy-done, s32[1024]{0:T(1024)S(1)} %pad_clamp_fusion.1), kind=kCustom, calls=%fused_computation | custom fusion | bytes 12583296 | tf_op jit(solution)/shard_map/jit(_take)/gather | solution.py:24
  15.1 3.5 %select_multiply_fusion = bf16[32,3,32,1024]{3,2,1,0:T(8,128)(2,1)S(1)} fusion(bf16[32,3,32,1024]{3,2,1,0:T(8,128)(2,1)} %bitcast.49, pred[32,3]{1,0:T(8,128)(4,1)S(1)} %compare_and_fusion, bf16[32,3]{1,0:T(8,128)(2,1)S(1)} %reshape.58), kind=kLoop, calls=%fused_computation.5 | loop fusion | flops 6291456 | bytes 12583200 | tf_op jit(solution)/shard_map/mul | solution.py:24
  18.5 79.1 %all_to_all.30 = bf16[32,3,32,1024]{3,2,1,0:T(8,128)(2,1)S(1)} all-to-all(bf16[32,3,32,1024]{3,2,1,0:T(8,128)(2,1)S(1)} %select_multiply_fusion), channel_id=1, replica_groups=mesh['fsdp'=32,'rep'=8] {'fsdp'}, dimensions={0} | all-to-all | bytes 12582912 | tf_op jit(solution)/shard_map/all_to_all | solution.py:26
  97.6 3.4 %copy.25 = bf16[1,3,32,32,1024]{4,3,2,1,0:T(8,128)(2,1)} copy(bf16[1,3,32,32,1024]{4,3,1,2,0:T(8,128)(2,1)S(1)} %bitcast.48) | data formatting | bytes 12582912 | tf_op jit(solution)/shard_map/all_to_all | solution.py:26
  101.0 0.0 copy-start.3
  101.0 1.6 multiply_reduce_fusion
  102.6 0.0 all-gather.6.cloned.1.call-done
  102.6 0.0 copy-done.3
  102.6 8.4 %multiply_reduce_fusion.1 = (f32[3]{0:T(128)S(1)}, f32[3,128,1024]{2,1,0:T(8,128)S(1)}) fusion(bf16[1,3,1024,1024]{3,2,1,0:T(8,128)(2,1)} %all-gather.6.cloned.1.call-done, bf16[3,1024,1024]{2,1,0:T(8,128)(2,1)} %bitcast.45, bf16[1,3,1024,128]{3,2,1,0:T(8,128)(2,1)S(1)} %copy-done.3), kind=kOutput, calls=%fused_computation.12 | convolution fusion | flops 1611792384 | bytes 14942220 | tf_op jit(solution)/shard_map/kij,kjc->kic/dot_general | solution.py:39
  111.0 20.0 %psum.7 = f32[3]{0:T(128)S(1)} all-reduce(f32[3]{0:T(128)S(1)} %get-tuple-element.5), channel_id=1, replica_groups=mesh['fsdp'=32,'rep'=8] {'rep'}, use_global_device_ids=true, to_apply=%region_4.5 | all-reduce | flops 3 | bytes 24 | tf_op jit(solution)/shard_map/psum | solution.py:47
  131.0 1.1 fusion.4
  132.1 0.0 all-gather.4.cloned.1.call-update
  132.1 70.5 %all-gather.4.cloned.1.call-done = bf16[3,1024,1024]{1,2,0:T(8,128)(2,1)} async-done(((bf16[3,1024,128]{1,2,0:T(8,128)(2,1)}), bf16[3,1024,1024]{1,2,0:T(8,128)(2,1)}) %all-gather.4.cloned.1.call-update) | async-done | bytes 6291472 | tf_op jit(solution)/shard_map/all_gather | solution.py:50
  202.6 8.7 %copy.27 = bf16[3,1024,1024]{2,1,0:T(8,128)(2,1)} copy(bf16[3,1024,1024]{1,2,0:T(8,128)(2,1)} %all-gather.4.cloned.1.call-done) | data formatting | bytes 12582912 | tf_op jit(solution)/shard_map/all_gather | solution.py:50
  211.3 6.8 %copy.28 = bf16[1,3,32,32,1024]{4,3,1,0,2:T(8,128)(2,1)} copy(bf16[1,3,32,32,1024]{4,3,2,1,0:T(8,128)(2,1)} %bitcast.50) | data formatting | bytes 12582912 | tf_op jit(solution)/shard_map/reshape | solution.py:51
  218.1 0.0 copy-start.2
  218.1 7.6 %all-to-all-start.1 = ((bf16[1,3,32,32,1024]{4,3,1,0,2:T(8,128)(2,1)}), bf16[1,3,32,32,1024]{4,3,1,0,2:T(8,128)(2,1)}, u32[]{:S(2)}, u32[]{:S(2)}) async-start(bf16[1,3,32,32,1024]{4,3,1,0,2:T(8,128)(2,1)} %copy.28), calls=%async_computation.1 | async-start | bytes 12582912 | tf_op jit(solution)/shard_map/all_to_all | solution.py:52
  225.7 0.0 copy-done.2
  225.7 6.5 %fusion.3 = f32[1,3,128,1024]{3,2,1,0:T(8,128)} fusion(f32[1,3,128,1024]{3,2,1,0:T(8,128)S(1)} %copy-done.2, bf16[3,1024,1024]{2,1,0:T(8,128)(2,1)} %bitcast.46, s32[]{:T(128)S(6)} %select_n.45), kind=kOutput, calls=%fused_computation.10 | convolution fusion | flops 806486016 | bytes 10223620 | tf_op jit(solution)/shard_map/kij,kmj->kim/dot_general | solution.py:30
  232.2 0.0 copy-start.1
  232.2 7.0 %fusion.2 = f32[1,3,1024,128]{3,2,1,0:T(8,128)} fusion(f32[1,3,1024,128]{3,2,1,0:T(8,128)} %param.11, bf16[3,1024,1024]{2,1,0:T(8,128)(2,1)} %bitcast.47, s32[]{:T(128)S(6)} %select_n.45), kind=kOutput, calls=%fused_computation.8 | convolution fusion | flops 806486016 | bytes 10223620 | tf_op jit(solution)/shard_map/kji,kjc->kic/dot_general | solution.py:31
  239.2 74.7 %all-to-all-done.1 = bf16[1,3,32,32,1024]{4,3,1,0,2:T(8,128)(2,1)} async-done(((bf16[1,3,32,32,1024]{4,3,1,0,2:T(8,128)(2,1)}), bf16[1,3,32,32,1024]{4,3,1,0,2:T(8,128)(2,1)}, u32[]{:S(2)}, u32[]{:S(2)}) %all-to-all-start.1) | async-done | bytes 6291488 | tf_op jit(solution)/shard_map/all_to_all | solution.py:52
  313.9 4.8 %gather_fusion.1 = bf16[32,32,1024]{2,1,0:T(8,128)(2,1)} fusion(bf16[96,32,1024]{2,1,0:T(8,128)(2,1)} %bitcast.13, s32[1024]{0:T(1024)S(1)} %pad_clamp_fusion), kind=kCustom, calls=%fused_computation.1 | custom fusion | bytes 4194432 | tf_op jit(solution)/shard_map/jit(_take)/gather | solution.py:54
  318.7 3.2 broadcast_select_fusion
  321.8 0.0 copy-done.1
  (7 shorter events, 0.0 us)
Async XLA Ops:
  7.2 1.9 copy-start
  7.2 95.4 %all-gather.6.cloned.1.call-start = ((), (), s32[]{:S(2)}) async-start(), calls=%async_computation.3 | async-start | bytes 7077888 | tf_op jit(solution)/shard_map/all_gather | solution.py:41
  7.9 194.7 %all-gather.4.cloned.1.call-start = ((), (), s32[]{:S(2)}) async-start(), calls=%async_computation.2 | async-start | bytes 7077888 | tf_op jit(solution)/shard_map/all_gather | solution.py:50
  101.0 1.7 copy-start.3
  218.1 7.6 %copy-start.2 = (f32[1,3,128,1024]{3,2,1,0:T(8,128)S(1)}, f32[1,3,128,1024]{3,2,1,0:T(8,128)}, u32[]{:S(2)}) copy-start(f32[1,3,128,1024]{3,2,1,0:T(8,128)} %param.10) | copy-start | bytes 4718596
  218.1 95.8 %all-to-all-start.1 = ((bf16[1,3,32,32,1024]{4,3,1,0,2:T(8,128)(2,1)}), bf16[1,3,32,32,1024]{4,3,1,0,2:T(8,128)(2,1)}, u32[]{:S(2)}, u32[]{:S(2)}) async-start(bf16[1,3,32,32,1024]{4,3,1,0,2:T(8,128)(2,1)} %copy.28), calls=%async_computation.1 | async-start | bytes 12582912 | tf_op jit(solution)/shard_map/all_to_all | solution.py:52
  232.2 89.7 %copy-start.1 = (bf16[32,32,1024]{2,1,0:T(8,128)(2,1)S(1)}, bf16[32,32,1024]{2,1,0:T(8,128)(2,1)}, u32[]{:S(2)}) copy-start(bf16[32,32,1024]{2,1,0:T(8,128)(2,1)} %param.7) | copy-start | bytes 6291460
Sparse Core Ops, SparseCore 0:
  9.8 77.3 all-gather.5
  132.2 70.3 all-gather.3
where the time goes:
time: 329 us
  waiting for transfers between devices  146 us (44%)
  blocking collectives  99 us (30%)
  local copies, waits for them, and re-layouts  29.8 us (9%)
  matrix products  21.9 us (7%)
  between operations  14.1 us (4%)
  other arithmetic  10.3 us (3%)
  starting transfers between devices  7.67 us (2%)
    all_to_all x1, blocking collectives, local(): lax.all_to_all(packed, 'fsdp', split_axis=0, concat_axis=2, tiled=True)  79.1 us
    all_to_all x1, waiting for transfers between devices, local(): lax.all_to_all(outgoing, 'fsdp', split_axis=2, concat_axis=0, tiled=True)  74.7 us
    all_gather x1, waiting for transfers between devices, local(): assembled = lax.all_gather(update_part, 'rep', axis=2, tiled=True)  70.5 us
    psum x1, blocking collectives, local(): pre_squares = lax.psum(pre_part, 'rep')  20 us
    all_gather x1, local copies, waits for them, and re-layouts, local(): assembled = lax.all_gather(update_part, 'rep', axis=2, tiled=True)  8.71 us
    dot_general x1, matrix products, local(): jnp.einsum('kij,kjc->kic', lax.all_gather(left_root[0], 'rep', axis=1, ti...  8.37 us
    all_to_all x1, starting transfers between devices, local(): lax.all_to_all(outgoing, 'fsdp', split_axis=2, concat_axis=0, tiled=True)  7.59 us
    dot_general x1, matrix products, local(): jnp.einsum('kji,kjc->kic', blocks, own_cols, preferred_element_type=jnp.f...  7.03 us
  transfers between devices with their start and end apart: 3, of which 2 were waited for; matrix products, arithmetic and copies ran while one was open for 9% of the time, Pallas kernels for 0%

commit v1 on v0

v1 whole, which is shorter than its diff:
```python
import jax
import jax.numpy as jnp
from jax import lax
from jax.experimental import pallas as pl
from jax.experimental.pallas import tpu as pltpu
from jax.sharding import PartitionSpec as P

decay_rate = 0.95
epsilon = 1e-06

F32 = jnp.float32
BF16 = jnp.bfloat16
LANES = 128
STRIDE = 8
VMEM_LIMIT = 48 * 1024 * 1024


def split_three(value):
    high = value.astype(BF16).astype(F32)
    rest = value - high
    middle = rest.astype(BF16).astype(F32)
    return high, middle, (rest - middle).astype(BF16).astype(F32)


def update_kernel(rep_ref, blocks_ref, left_ref, right_ref, out_ref, sums_ref):
    slot = pl.program_id(0)
    slots = pl.num_programs(0)
    pieces, rows, order = blocks_ref.shape
    width = right_ref.shape[1]
    block = blocks_ref[...].reshape(pieces * rows, order)
    rooted = jnp.dot(block, right_ref[...], preferred_element_type=F32).astype(BF16)
    precond = jnp.dot(left_ref[...], rooted, preferred_element_type=F32)
    start = pl.multiple_of(slot * rows, rows)
    out_ref[:, pl.ds(start, rows), :] = precond.astype(BF16).reshape(pieces, rows, width)
    columns = pl.multiple_of(rep_ref[0] * width, width)
    own = blocks_ref[:, :, pl.ds(columns, width)].astype(F32)
    lane = lax.broadcasted_iota(jnp.int32, sums_ref.shape, 1)

    @pl.when(slot == 0)
    def _():
        sums_ref[...] = jnp.zeros_like(sums_ref)

    total = sums_ref[...]
    parts = split_three(jnp.sum(precond * precond, keepdims=True))
    parts += split_three(jnp.sum(own * own, keepdims=True).reshape(1, 1))
    for index, part in enumerate(parts):
        total = jnp.where(lane == slot * STRIDE + index, part, total)
    sums_ref[...] = total

    @pl.when(slot == slots - 1)
    def _():
        tail = sums_ref[...].astype(BF16)
        out_ref[:, slots * rows :, :] = jnp.broadcast_to(tail, (pieces,) + tail.shape)


def precondition(rep, blocks, left, right):
    pieces, slots, rows, order = blocks.shape
    width = right.shape[-1]
    tail = 16
    return pl.pallas_call(
        update_kernel,
        grid_spec=pltpu.PrefetchScalarGridSpec(
            num_scalar_prefetch=1,
            grid=(slots,),
            in_specs=[
                pl.BlockSpec((pieces, None, rows, order), lambda k, rep: (0, k, 0, 0)),
                pl.BlockSpec((None, order, order), lambda k, rep: (k, 0, 0)),
                pl.BlockSpec((None, order, width), lambda k, rep: (k, 0, 0)),
            ],
            out_specs=pl.BlockSpec(
                (pieces, slots * rows + tail, width), lambda k, rep: (0, 0, 0)
            ),
            scratch_shapes=[pltpu.VMEM((tail, width), F32)],
        ),
        out_shape=jax.ShapeDtypeStruct((pieces, slots * rows + tail, width), BF16),
        compiler_params=pltpu.CompilerParams(vmem_limit_bytes=VMEM_LIMIT),
        cost_estimate=pl.CostEstimate(
            flops=slots * 4 * order * order * width,
            bytes_accessed=slots * 4 * order * order,
            transcendentals=0,
        ),
        name="precondition",
    )(rep, blocks, left, right)


def select_kernel(owner_ref, slot_ref, arrived_ref, out_ref):
    count, rows, width = out_ref.shape
    count -= 1
    slots_rows = arrived_ref.shape[1] - 16
    line = lax.broadcasted_iota(jnp.int32, (rows, width), 0)
    sums = jnp.zeros((rows, width), F32)
    for index in range(count):
        owner = owner_ref[index]
        start = pl.multiple_of(slot_ref[index] * rows, rows)
        out_ref[index] = arrived_ref[owner, pl.ds(start, rows), :]
        tail = arrived_ref[owner, slots_rows : slots_rows + 16, :].astype(F32)
        sums = jnp.where(line == index, jnp.concatenate([tail, tail], axis=0), sums)
    out_ref[count] = sums.astype(BF16)


def select(owner, slot, arrived):
    count, rows = owner.shape[0], (arrived.shape[1] - 16) // 3
    width = arrived.shape[2]
    return pl.pallas_call(
        select_kernel,
        grid_spec=pltpu.PrefetchScalarGridSpec(
            num_scalar_prefetch=2,
            grid=(1,),
            in_specs=[pl.BlockSpec(arrived.shape, lambda i, o, s: (0, 0, 0))],
            out_specs=pl.BlockSpec((count + 1, rows, width), lambda i, o, s: (0, 0, 0)),
        ),
        out_shape=jax.ShapeDtypeStruct((count + 1, rows, width), BF16),
        compiler_params=pltpu.CompilerParams(vmem_limit_bytes=VMEM_LIMIT),
        name="select",
    )(owner, slot, arrived)


def finish_kernel(rep_ref, slot_ref, *refs):
    out_ref, scale_ref = refs[-2:]
    shares = refs[:-2]
    count, rows, order = out_ref.shape
    width = shares[0].shape[2]
    half = shares[7].shape[0]
    replicas = order // width
    sums = shares[8][count - half].astype(F32)
    for share in shares[:7]:
        sums += share[count].astype(F32)
    lane = lax.broadcasted_iota(jnp.int32, (rows, width), 1) - slot_ref[...] * STRIDE
    pre = jnp.sum(jnp.where((lane >= 0) & (lane < 3), sums, 0.0), axis=1, keepdims=True)
    grad = jnp.sum(jnp.where((lane >= 3) & (lane < 6), sums, 0.0), axis=1, keepdims=True)
    scale = jnp.sqrt(grad) / jnp.sqrt(pre + epsilon)
    scale_ref[...] = jnp.broadcast_to(scale, (rows, width))

    def place(index, share, column):
        factor = scale_ref[pl.ds(index, 1), :]
        start = pl.multiple_of(column * width, width)
        out_ref[index, :, pl.ds(start, width)] = (share.astype(F32) * factor).astype(BF16)

    distances = (0, 1, 2, 3, -1, -2, -3)
    for index in range(count):
        for share, distance in zip(shares[:7], distances):
            place(index, share[index], lax.rem(rep_ref[0] - distance + replicas, replicas))
        far = lax.rem(rep_ref[0] + replicas // 2, replicas)
        share = shares[7][index] if index < half else shares[8][index - half]
        place(index, share, far)


def finish(rep, slot, shares, count, rows, order):
    slot_rows = jnp.broadcast_to(slot[:, None], (count, LANES))
    return pl.pallas_call(
        finish_kernel,
        in_specs=[pl.BlockSpec(memory_space=pltpu.SMEM)]
        + [pl.BlockSpec(memory_space=pltpu.VMEM)] * (1 + len(shares)),
        out_specs=pl.BlockSpec(memory_space=pltpu.VMEM),
        out_shape=jax.ShapeDtypeStruct((count, rows, order), BF16),
        scratch_shapes=[pltpu.VMEM((count, LANES), F32)],
        compiler_params=pltpu.CompilerParams(vmem_limit_bytes=VMEM_LIMIT),
        name="finish",
    )(rep, slot_rows, *shares)


def factor_kernel(rep_ref, occupied_ref, blocks_ref, left_ref, right_ref, left_out, right_out):
    slot = pl.program_id(0)
    pieces, rows, order = blocks_ref.shape
    width = right_ref.shape[1]
    rep = rep_ref[0]
    weight = (1.0 - decay_rate) * occupied_ref[slot].astype(F32)
    block = blocks_ref[...].reshape(pieces * rows, order)
    share = width // rows
    own_rows = blocks_ref[pl.ds(rep * share, share)].reshape(width, order)
    columns = pl.multiple_of(rep * width, width)
    own_columns = blocks_ref[:, :, pl.ds(columns, width)].reshape(order, width)
    left = lax.dot_general(
        own_rows, block, (((1,), (1,)), ((), ())), preferred_element_type=F32
    )
    left_out[...] = decay_rate * left_ref[...] + weight * left
    right = jnp.dot(own_columns.T, block, preferred_element_type=F32).T
    right_out[...] = decay_rate * right_ref[...] + weight * right


def factors(rep, occupied, blocks, left, right):
    pieces, slots, rows, order = blocks.shape
    width = right.shape[-1]
    left_spec = pl.BlockSpec((None, None, width, order), lambda k, a, b: (0, k, 0, 0))
    right_spec = pl.BlockSpec((None, None, order, width), lambda k, a, b: (0, k, 0, 0))
    return pl.pallas_call(
        factor_kernel,
        grid_spec=pltpu.PrefetchScalarGridSpec(
            num_scalar_prefetch=2,
            grid=(slots,),
            in_specs=[
                pl.BlockSpec((pieces, None, rows, order), lambda k, a, b: (0, k, 0, 0)),
                left_spec,
                right_spec,
            ],
            out_specs=[left_spec, right_spec],
        ),
        out_shape=[
            jax.ShapeDtypeStruct(left.shape, F32),
            jax.ShapeDtypeStruct(right.shape, F32),
        ],
        compiler_params=pltpu.CompilerParams(vmem_limit_bytes=VMEM_LIMIT),
        cost_estimate=pl.CostEstimate(
            flops=slots * 4 * order * order * width,
            bytes_accessed=slots * 6 * order * order,
            transcendentals=0,
        ),
        name="factors",
    )(rep, occupied, blocks, left, right)


def ring_gather(share, axis):
    size = lax.axis_size(axis)
    half = share.shape[0] // 2

    def shift(value, by):
        return lax.ppermute(value, axis, [(i, (i + by) % size) for i in range(size)])

    up, down = [share], [share]
    for _ in range(size // 2 - 1):
        up.append(shift(up[-1], 1))
        down.append(shift(down[-1], -1))
    far_up = shift(up[-1][:half], 1)
    far_down = shift(down[-1][half:], -1)
    return up + down[1:] + [far_up, far_down]


def local(gradient, block_owner, block_slot, left_state, right_state, left_root, right_root):
    owners_count = lax.axis_size("fsdp")
    block_count, row_share, block_order = gradient.shape
    slot_count = left_state.shape[1]
    rep = lax.axis_index("rep").astype(jnp.int32).reshape(1)
    positions = owners_count * slot_count
    flat_index = block_owner * slot_count + block_slot
    matches = flat_index[None, :] == jnp.arange(positions, dtype=jnp.int32)[:, None]
    occupied = jnp.any(matches, axis=1).astype(jnp.int32)
    sources = jnp.sum(
        jnp.where(matches, jnp.arange(block_count, dtype=jnp.int32)[None, :], 0), axis=1
    )
    mine = lax.dynamic_slice_in_dim(
        occupied, lax.axis_index("fsdp") * slot_count, slot_count, 0
    )
    left_full = lax.all_gather(left_root[0], "rep", axis=1, tiled=True)
    packed = gradient.at[sources].get(mode="promise_in_bounds")
    packed = packed.reshape(owners_count, slot_count, row_share, block_order)
    blocks = lax.all_to_all(packed, "fsdp", split_axis=0, concat_axis=0, tiled=True)
    outgoing = precondition(rep, blocks, left_full, right_root[0])
    arrived = lax.all_to_all(outgoing, "fsdp", split_axis=0, concat_axis=0, tiled=True)
    named = select(block_owner, block_slot, arrived)
    left_factor, right_factor = factors(rep, mine, blocks, left_state, right_state)
    shares = ring_gather(named, "rep")
    update = finish(rep, block_slot, shares, block_count, row_share, block_order)
    return (update, left_factor, right_factor)


def solution(mesh):
    in_specs = (
        P(None, "fsdp", None),
        P(),
        P(),
        P("fsdp", None, "rep", None),
        P("fsdp", None, None, "rep"),
        P("fsdp", None, "rep", None),
        P("fsdp", None, None, "rep"),
    )
    out_specs = (P(None, "fsdp", None), P("fsdp", None, "rep", None), P("fsdp", None, None, "rep"))
    return jax.shard_map(local, mesh=mesh, in_specs=in_specs, out_specs=out_specs, check_vma=False)
```

time: 329 us -> 194 us (0.59)
  blocking collectives: 99 us -> 18.9 us
  waiting for transfers between devices: 146 us -> 103 us
  matrix products: 21.9 us -> 0 us
  local copies, waits for them, and re-layouts: 29.8 us -> 8.92 us
  Pallas kernels: 0 us -> 20.7 us
  starting transfers between devices: 7.67 us -> 24.9 us
  other arithmetic: 10.3 us -> 0.88 us
    all_gather x2 -> x1, waiting for transfers between devices: 70.5 us -> 0.01 us  [local(): left_full = lax.all_gather(left_root[0], 'rep', axis=1, tiled=True)]
    all_to_all x1, blocking collectives: 79.1 us -> 18.9 us  [local(): lax.all_to_all(outgoing, 'fsdp', split_axis=0, concat_axis=0, tiled=True)]
    dot_general x3 -> x0, matrix products: 21.9 us -> none  [the longest x1 8.37 us: local(): jnp.einsum('kij,kjc->kic', lax.all_gather(left_root[0], 'rep', axis=1, ti...]
    pallas_call x0 -> x4, Pallas kernels: none -> 20.7 us  [the longest x1 10 us: precondition(): pl.pallas_call(update_kernel, grid_spec=pltpu.PrefetchScalarGridSpec(num_...]
    psum x1 -> x0, blocking collectives: 20 us -> none  [local(): pre_squares = lax.psum(pre_part, 'rep')]
    ppermute x0 -> x8, starting transfers between devices: none -> 17.2 us  [shift(): lax.ppermute(value, axis, [(i, (i + by) % size) for i in range(size)])]
    ppermute x0 -> x8, waiting for transfers between devices: none -> 14.4 us  [shift(): lax.ppermute(value, axis, [(i, (i + by) % size) for i in range(size)])]
    all_to_all x1, waiting for transfers between devices: 74.7 us -> 87.6 us  [local(): lax.all_to_all(packed, 'fsdp', split_axis=0, concat_axis=0, tiled=True)]
  transfers between devices with their start and end apart: 3 -> 10, of which waited for: 2 -> 4; matrix products, arithmetic and copies ran while one was open for 9% -> 4% of each run, Pallas kernels for 0% -> 4%
where the time goes in v1:
time: 194 us; the launch traced here: 191 us
  waiting for transfers between devices  103 us (53%)
  starting transfers between devices  24.9 us (13%)
  Pallas kernels  20.7 us (11%)
  blocking collectives  18.9 us (10%)
  between operations  14.1 us (7%)
  local copies, waits for them, and re-layouts  8.92 us (5%)
    all_to_all x1, waiting for transfers between devices, local(): lax.all_to_all(packed, 'fsdp', split_axis=0, concat_axis=0, tiled=True)  87.6 us
    all_to_all x1, blocking collectives, local(): lax.all_to_all(outgoing, 'fsdp', split_axis=0, concat_axis=0, tiled=True)  18.9 us
    ppermute x8, starting transfers between devices, shift(): lax.ppermute(value, axis, [(i, (i + by) % size) for i in range(size)])  17.2 us
    ppermute x8, waiting for transfers between devices, shift(): lax.ppermute(value, axis, [(i, (i + by) % size) for i in range(size)])  14.4 us
    pallas_call x1, Pallas kernels, precondition(): pl.pallas_call(update_kernel, grid_spec=pltpu.PrefetchScalarGridSpec(num_...  10 us
    all_to_all x1, starting transfers between devices, local(): lax.all_to_all(packed, 'fsdp', split_axis=0, concat_axis=0, tiled=True)  7.72 us
    pallas_call x1, Pallas kernels, factors(): pl.pallas_call(factor_kernel, grid_spec=pltpu.PrefetchScalarGridSpec(num_...  7.23 us
    gather x1, local copies, waits for them, and re-layouts, local(): packed = gradient.at[sources].get(mode='promise_in_bounds')  5.87 us
  transfers between devices with their start and end apart: 10, of which 4 were waited for; matrix products, arithmetic and copies ran while one was open for 4% of the time, Pallas kernels for 4%

profile of v1, /device:TPU:8, one launch (start us, length us, event | category | flops | bytes accessed | tf_op | source)
XLA Modules:
  0.0 191.2 jit_solution(13117809214597819256)
XLA Ops:
  7.2 0.0 copy-start
  7.2 0.0 all-gather.3.cloned.1.call-start
  7.2 0.7 all-gather.3.cloned.1.call-update
  7.9 0.7 multiply_add_fusion
  8.6 0.1 select_reduce_fusion
  8.7 0.1 copy-done
  8.8 5.9 %gather_fusion = bf16[96,32,1024]{2,1,0:T(8,128)(2,1)} fusion(bf16[32,32,1024]{2,1,0:T(8,128)(2,1)S(1)} %copy-done, s32[1024]{0:T(1024)S(1)} %pad_clamp_fusion), kind=kCustom, calls=%fused_computation | custom fusion | bytes 12583296 | tf_op jit(solution)/shard_map/gather | solution.py:244
  14.6 0.0 copy-start.3
  14.6 7.7 %all-to-all-start = ((bf16[32,3,32,1024]{3,2,1,0:T(8,128)(2,1)}), bf16[32,3,32,1024]{3,2,1,0:T(8,128)(2,1)}, u32[]{:S(2)}, u32[]{:S(2)}) async-start(bf16[32,3,32,1024]{3,2,1,0:T(8,128)(2,1)} %bitcast.9), calls=%async_computation | async-start | bytes 12582912 | tf_op jit(solution)/shard_map/all_to_all | solution.py:246
  22.4 87.6 %all-to-all-done.blocks_ref = bf16[32,3,32,1024]{3,2,1,0:T(8,128)(2,1)} async-done(((bf16[32,3,32,1024]{3,2,1,0:T(8,128)(2,1)}), bf16[32,3,32,1024]{3,2,1,0:T(8,128)(2,1)}, u32[]{:S(2)}, u32[]{:S(2)}) %all-to-all-start) | async-done | bytes 6291488 | tf_op jit(solution)/shard_map/all_to_all | solution.py:246
  109.9 0.0 all-gather.3.cloned.1.call-done
  109.9 0.0 copy-done.3
  109.9 0.0 copy-start.4
  109.9 0.0 copy-start.5
  110.0 10.0 %precondition.1 = bf16[32,112,128]{2,1,0:T(8,128)(2,1)S(1)} custom-call(s32[1]{0:T(128)} %bitcast.rep_ref, bf16[32,3,32,1024]{3,2,1,0:T(8,128)(2,1)} %all-to-all-done.blocks_ref, bf16[3,1024,1024]{2,1,0:T(8,128)(2,1)} %bitcast.10, bf16[3,1024,128]{2,1,0:T(8,128)(2,1)S(1)} %bitcast.8), custom_call_target="tpu_custom_call" | custom-call | flops 1610612736 | bytes 12582912 | tf_op jit(solution)/shard_map/precondition/pallas_call | solution.py:60
  120.0 18.9 %all_to_all.10.arrived_ref = bf16[32,112,128]{2,1,0:T(8,128)(2,1)S(1)} all-to-all(bf16[32,112,128]{2,1,0:T(8,128)(2,1)S(1)} %precondition.1), channel_id=1, replica_groups=mesh['fsdp'=32,'rep'=8] {'fsdp'}, dimensions={0} | all-to-all | bytes 1835008 | tf_op jit(solution)/shard_map/all_to_all | solution.py:248
  138.9 0.0 copy-done.4
  138.9 0.0 copy-done.5
  138.9 0.6 select.1.refs_0_
  139.6 5.9 %collective-permute-start.3 = (bf16[33,32,128]{2,1,0:T(8,128)(2,1)S(1)}, bf16[33,32,128]{2,1,0:T(8,128)(2,1)S(1)}, u32[]{:S(2)}, u32[]{:S(2)}) collective-permute-start(bf16[33,32,128]{2,1,0:T(8,128)(2,1)S(1)} %select.1.refs_0_), channel_id=1, source_target_pairs={{0,7},{1,0},{2,1},{3,2},{4,3},{5,4},{6,5},{7,6},{8,15},{9,8},{10,9... | collective-permute-start | bytes 811016 | tf_op jit(solution)/shard_map/ppermute | solution.py:217
  145.5 0.0 collective-permute-start
  145.5 5.6 %collective-permute-done.3.refs_4_ = bf16[33,32,128]{2,1,0:T(8,128)(2,1)S(1)} collective-permute-done((bf16[33,32,128]{2,1,0:T(8,128)(2,1)S(1)}, bf16[33,32,128]{2,1,0:T(8,128)(2,1)S(1)}, u32[]{:S(2)}, u32[]{:S(2)}) %collective-permute-start.3) | collective-permute-done | bytes 270368 | tf_op jit(solution)/shard_map/ppermute | solution.py:217
  151.1 3.7 %collective-permute-start.4 = (bf16[33,32,128]{2,1,0:T(8,128)(2,1)S(1)}, bf16[33,32,128]{2,1,0:T(8,128)(2,1)}, u32[]{:S(2)}, u32[]{:S(2)}) collective-permute-start(bf16[33,32,128]{2,1,0:T(8,128)(2,1)S(1)} %collective-permute-done.3.refs_4_), channel_id=1, source_target_pairs={{0,7},{1,0},{2,1},{3,2},{4,3},{5,4},{6,5},{7,6},{8,15},{9,8},{10,9... | collective-permute-start | bytes 811016 | tf_op jit(solution)/shard_map/ppermute | solution.py:217
  154.8 0.0 collective-permute-done.refs_1_
  154.8 0.0 collective-permute-start.1
  154.8 4.7 %collective-permute-done.4.refs_5_ = bf16[33,32,128]{2,1,0:T(8,128)(2,1)} collective-permute-done((bf16[33,32,128]{2,1,0:T(8,128)(2,1)S(1)}, bf16[33,32,128]{2,1,0:T(8,128)(2,1)}, u32[]{:S(2)}, u32[]{:S(2)}) %collective-permute-start.4) | collective-permute-done | bytes 270368 | tf_op jit(solution)/shard_map/ppermute | solution.py:217
  159.4 3.8 %collective-permute-start.5 = (bf16[33,32,128]{2,1,0:T(8,128)(2,1)}, bf16[33,32,128]{2,1,0:T(8,128)(2,1)S(1)}, u32[]{:S(2)}, u32[]{:S(2)}) collective-permute-start(bf16[33,32,128]{2,1,0:T(8,128)(2,1)} %collective-permute-done.4.refs_5_), channel_id=1, source_target_pairs={{0,7},{1,0},{2,1},{3,2},{4,3},{5,4},{6,5},{7,6},{8,15},{9,8},{10,9... | collective-permute-start | bytes 811016 | tf_op jit(solution)/shard_map/ppermute | solution.py:217
  163.2 0.0 collective-permute-done.1.refs_2_
  163.3 0.0 collective-permute-start.2
  163.3 0.1 fusion
  163.4 0.1 dynamic_slice.3.occupied_ref
  163.4 4.1 %collective-permute-done.5.refs_6_ = bf16[33,32,128]{2,1,0:T(8,128)(2,1)S(1)} collective-permute-done((bf16[33,32,128]{2,1,0:T(8,128)(2,1)}, bf16[33,32,128]{2,1,0:T(8,128)(2,1)S(1)}, u32[]{:S(2)}, u32[]{:S(2)}) %collective-permute-start.5) | collective-permute-done | bytes 270368 | tf_op jit(solution)/shard_map/ppermute | solution.py:217
  167.6 3.7 %collective-permute-start.7 = (bf16[17,32,128]{2,1,0:T(8,128)(2,1)S(1)}, bf16[17,32,128]{2,1,0:T(8,128)(2,1)S(1)}, u32[]{:S(2)}, u32[]{:S(2)}) collective-permute-start(bf16[17,32,128]{2,1,0:T(8,128)(2,1)S(1)} %slice.11), channel_id=1, source_target_pairs={{0,7},{1,0},{2,1},{3,2},{4,3},{5,4},{6,5},{7,6},{8,15},{9,8},{10,9... | collective-permute-start | bytes 417800 | tf_op jit(solution)/shard_map/ppermute | solution.py:217
  171.2 0.0 collective-permute-done.2.refs_3_
  171.2 0.1 collective-permute-start.6
  171.3 0.0 copy-start.1
  171.3 1.4 copy-done.1
  172.7 0.0 copy-start.2
  172.7 1.4 copy-done.2
  174.1 7.2 %factors.1 = (f32[1,3,128,1024]{3,2,1,0:T(8,128)}, f32[1,3,1024,128]{3,2,1,0:T(8,128)}) custom-call(s32[1]{0:T(128)} %bitcast.rep_ref, s32[3]{0:T(128)S(1)} %dynamic_slice.3.occupied_ref, bf16[32,3,32,1024]{3,2,1,0:T(8,128)(2,1)} %all-to-all-done.blocks_ref, f32[1,3,128,1024]{3,2,1,0:T(8,128)S(1)} %copy-done.1, f32[1,3,1024,128]{3,2,1,0:T(8,128)S(1)} %copy-done.2), custom_call_target="tpu_custom_call" | custom-call | flops 1610612736 | bytes 18874368 | tf_op jit(solution)/shard_map/factors/pallas_call | solution.py:186
  181.4 0.0 collective-permute-done.6.refs_7_
  181.4 0.0 collective-permute-done.7.refs_8_
  181.4 0.1 broadcast_in_dim.14.slot_ref
  181.5 2.9 %finish.1 = bf16[32,32,1024]{2,1,0:T(8,128)(2,1)} custom-call(s32[1]{0:T(128)} %bitcast.rep_ref, s32[32,128]{1,0:T(8,128)S(1)} %broadcast_in_dim.14.slot_ref, bf16[33,32,128]{2,1,0:T(8,128)(2,1)S(1)} %select.1.refs_0_, bf16[33,32,128]{2,1,0:T(8,128)(2,1)S(1)} %collective-permute-done.refs_1_, bf16[33,32,128]{2,1,0:T(8,128)(2,1)} %collective-permute-done.1.refs_2_, ...), custom_call_target="tpu_custom_call" | custom-call | tf_op jit(solution)/shard_map/finish/pallas_call | solution.py:150
  (5 shorter events, 0.0 us)
Async XLA Ops:
  7.2 1.6 copy-start
  7.2 102.8 %all-gather.3.cloned.1.call-start = ((), (), s32[]{:S(2)}) async-start(), calls=%async_computation.2 | async-start | bytes 7077888 | tf_op jit(solution)/shard_map/all_gather | solution.py:243
  14.6 95.3 %copy-start.3 = (bf16[1,3,1024,128]{3,2,1,0:T(8,128)(2,1)S(1)}, bf16[1,3,1024,128]{3,2,1,0:T(8,128)(2,1)}, u32[]{:S(2)}) copy-start(bf16[1,3,1024,128]{3,2,1,0:T(8,128)(2,1)} %param.13) | copy-start | bytes 2359300
  14.6 95.3 %all-to-all-start = ((bf16[32,3,32,1024]{3,2,1,0:T(8,128)(2,1)}), bf16[32,3,32,1024]{3,2,1,0:T(8,128)(2,1)}, u32[]{:S(2)}, u32[]{:S(2)}) async-start(bf16[32,3,32,1024]{3,2,1,0:T(8,128)(2,1)} %bitcast.9), calls=%async_computation | async-start | bytes 12582912 | tf_op jit(solution)/shard_map/all_to_all | solution.py:246
  109.9 29.0 %copy-start.4 = (s32[32]{0:T(128)S(1)}, s32[32]{0:T(128)}, u32[]{:S(2)}) copy-start(s32[32]{0:T(128)} %slot_ref.1) | copy-start | bytes 388
  109.9 29.0 %copy-start.5 = (s32[32]{0:T(128)S(1)}, s32[32]{0:T(128)}, u32[]{:S(2)}) copy-start(s32[32]{0:T(128)} %owner_ref.1) | copy-start | bytes 388
  139.6 11.5 %collective-permute-start.3 = (bf16[33,32,128]{2,1,0:T(8,128)(2,1)S(1)}, bf16[33,32,128]{2,1,0:T(8,128)(2,1)S(1)}, u32[]{:S(2)}, u32[]{:S(2)}) collective-permute-start(bf16[33,32,128]{2,1,0:T(8,128)(2,1)S(1)} %select.1.refs_0_), channel_id=1, source_target_pairs={{0,7},{1,0},{2,1},{3,2},{4,3},{5,4},{6,5},{7,6},{8,15},{9,8},{10,9... | collective-permute-start | bytes 811016 | tf_op jit(solution)/shard_map/ppermute | solution.py:217
  145.5 9.3 %collective-permute-start = (bf16[33,32,128]{2,1,0:T(8,128)(2,1)S(1)}, bf16[33,32,128]{2,1,0:T(8,128)(2,1)S(1)}, u32[]{:S(2)}, u32[]{:S(2)}) collective-permute-start(bf16[33,32,128]{2,1,0:T(8,128)(2,1)S(1)} %select.1.refs_0_), channel_id=1, source_target_pairs={{0,1},{1,2},{2,3},{3,4},{4,5},{5,6},{6,7},{7,0},{8,9},{9,10},{10,1... | collective-permute-start | bytes 811016 | tf_op jit(solution)/shard_map/ppermute | solution.py:217
  151.1 8.4 %collective-permute-start.4 = (bf16[33,32,128]{2,1,0:T(8,128)(2,1)S(1)}, bf16[33,32,128]{2,1,0:T(8,128)(2,1)}, u32[]{:S(2)}, u32[]{:S(2)}) collective-permute-start(bf16[33,32,128]{2,1,0:T(8,128)(2,1)S(1)} %collective-permute-done.3.refs_4_), channel_id=1, source_target_pairs={{0,7},{1,0},{2,1},{3,2},{4,3},{5,4},{6,5},{7,6},{8,15},{9,8},{10,9... | collective-permute-start | bytes 811016 | tf_op jit(solution)/shard_map/ppermute | solution.py:217
  154.8 8.5 %collective-permute-start.1 = (bf16[33,32,128]{2,1,0:T(8,128)(2,1)S(1)}, bf16[33,32,128]{2,1,0:T(8,128)(2,1)}, u32[]{:S(2)}, u32[]{:S(2)}) collective-permute-start(bf16[33,32,128]{2,1,0:T(8,128)(2,1)S(1)} %collective-permute-done.refs_1_), channel_id=1, source_target_pairs={{0,1},{1,2},{2,3},{3,4},{4,5},{5,6},{6,7},{7,0},{8,9},{9,10},{10,1... | collective-permute-start | bytes 811016 | tf_op jit(solution)/shard_map/ppermute | solution.py:217
  159.4 8.1 %collective-permute-start.5 = (bf16[33,32,128]{2,1,0:T(8,128)(2,1)}, bf16[33,32,128]{2,1,0:T(8,128)(2,1)S(1)}, u32[]{:S(2)}, u32[]{:S(2)}) collective-permute-start(bf16[33,32,128]{2,1,0:T(8,128)(2,1)} %collective-permute-done.4.refs_5_), channel_id=1, source_target_pairs={{0,7},{1,0},{2,1},{3,2},{4,3},{5,4},{6,5},{7,6},{8,15},{9,8},{10,9... | collective-permute-start | bytes 811016 | tf_op jit(solution)/shard_map/ppermute | solution.py:217
  163.3 8.0 %collective-permute-start.2 = (bf16[33,32,128]{2,1,0:T(8,128)(2,1)}, bf16[33,32,128]{2,1,0:T(8,128)(2,1)S(1)}, u32[]{:S(2)}, u32[]{:S(2)}) collective-permute-start(bf16[33,32,128]{2,1,0:T(8,128)(2,1)} %collective-permute-done.1.refs_2_), channel_id=1, source_target_pairs={{0,1},{1,2},{2,3},{3,4},{4,5},{5,6},{6,7},{7,0},{8,9},{9,10},{10,1... | collective-permute-start | bytes 811016 | tf_op jit(solution)/shard_map/ppermute | solution.py:217
  167.6 13.8 %collective-permute-start.7 = (bf16[17,32,128]{2,1,0:T(8,128)(2,1)S(1)}, bf16[17,32,128]{2,1,0:T(8,128)(2,1)S(1)}, u32[]{:S(2)}, u32[]{:S(2)}) collective-permute-start(bf16[17,32,128]{2,1,0:T(8,128)(2,1)S(1)} %slice.11), channel_id=1, source_target_pairs={{0,7},{1,0},{2,1},{3,2},{4,3},{5,4},{6,5},{7,6},{8,15},{9,8},{10,9... | collective-permute-start | bytes 417800 | tf_op jit(solution)/shard_map/ppermute | solution.py:217
  171.2 10.1 %collective-permute-start.6 = (bf16[16,32,128]{2,1,0:T(8,128)(2,1)S(1)}, bf16[16,32,128]{2,1,0:T(8,128)(2,1)S(1)}, u32[]{:S(2)}, u32[]{:S(2)}) collective-permute-start(bf16[16,32,128]{2,1,0:T(8,128)(2,1)S(1)} %slice.10), channel_id=1, source_target_pairs={{0,1},{1,2},{2,3},{3,4},{4,5},{5,6},{6,7},{7,0},{8,9},{9,10},{10,1... | collective-permute-start | bytes 393224 | tf_op jit(solution)/shard_map/ppermute | solution.py:217
  171.3 1.4 copy-start.1
  172.7 1.4 copy-start.2
Sparse Core Ops, SparseCore 0:
  9.8 77.3 all-gather.2

commit v2 on v0

v2 whole, which is shorter than its diff:
```python
import jax
import jax.numpy as jnp
from jax import lax
from jax.experimental import pallas as pl
from jax.experimental.pallas import tpu as pltpu
from jax.sharding import PartitionSpec as P

decay_rate = 0.95
epsilon = 1e-06

F32 = jnp.float32
BF16 = jnp.bfloat16
ROWS = 32
TILE = 16
LANES = 128
VMEM_LIMIT = 48 * 1024 * 1024
DISTANCES = (0, 1, 2, 3, -1, -2, -3)


def params():
    return pltpu.CompilerParams(vmem_limit_bytes=VMEM_LIMIT)


def whole(shape):
    return pl.BlockSpec(shape, lambda *_: (0,) * len(shape))


def row_piece(index):
    per_line = 1024 // (2 * LANES)
    return TILE * (index // per_line), 2 * LANES * (index % per_line)


def split_three(value):
    high = value.astype(BF16).astype(F32)
    rest = value - high
    middle = rest.astype(BF16).astype(F32)
    return high, middle, (rest - middle).astype(BF16).astype(F32)


def pack_kernel(left_ref, right_ref, out_ref):
    for slot in range(left_ref.shape[0]):
        base = 2 * ROWS * slot
        for index in range(out_ref.shape[0]):
            row, column = row_piece(index)
            rows = pl.ds(row, TILE)
            out_ref[index, base : base + TILE] = left_ref[slot, rows, column : column + LANES]
            out_ref[index, base + TILE : base + ROWS] = left_ref[
                slot, rows, column + LANES : column + 2 * LANES
            ]
            out_ref[index, base + ROWS : base + 2 * ROWS] = right_ref[
                slot, ROWS * index : ROWS * (index + 1)
            ]


def pack(left, right, pieces):
    return pl.pallas_call(
        pack_kernel,
        out_shape=jax.ShapeDtypeStruct((pieces, left.shape[0] * 2 * ROWS, LANES), BF16),
        compiler_params=params(),
        name="pack",
    )(left, right)


def route_kernel(owner_ref, slot_ref, arrived_ref, out_ref):
    for index in range(out_ref.shape[0]):
        start = pl.multiple_of(slot_ref[index] * (2 * ROWS), 2 * ROWS)
        out_ref[index] = arrived_ref[owner_ref[index], pl.ds(start, 2 * ROWS), :]


def route(owner, slot, arrived):
    shape = (owner.shape[0], 2 * ROWS, LANES)
    return pl.pallas_call(
        route_kernel,
        grid_spec=pltpu.PrefetchScalarGridSpec(
            num_scalar_prefetch=2,
            grid=(1,),
            in_specs=[whole(arrived.shape)],
            out_specs=whole(shape),
        ),
        out_shape=jax.ShapeDtypeStruct(shape, BF16),
        compiler_params=params(),
        name="route",
    )(owner, slot, arrived)


def block_kernel(rep_ref, block_ref, roots_ref, *refs):
    shares, (out_ref, left_ref) = refs[:-2], refs[-2:]
    pieces, rows, order = block_ref.shape
    width = LANES
    replicas = order // width
    rep = rep_ref[0]
    half = shares[7].shape[0]

    def place(index, share, start):
        row, column = row_piece(index)
        lines = pl.ds(pl.multiple_of(start + row, TILE), TILE)
        left_ref[lines, column : column + width] = share[:TILE]
        left_ref[lines, column + width : column + 2 * width] = share[TILE:]

    for share, distance in zip(shares[:7], DISTANCES):
        start = lax.rem(rep - distance + replicas, replicas) * width
        for index in range(pieces):
            place(index, share[index], start)
    start = lax.rem(rep + replicas // 2, replicas) * width
    for index in range(pieces):
        share = shares[7][index] if index < half else shares[8][index - half]
        place(index, share, start)

    block = block_ref[...].reshape(order, order)
    right_root = roots_ref[:, ROWS:, :].reshape(order, width)
    rooted = jnp.dot(block, right_root, preferred_element_type=F32).astype(BF16)
    precond = jnp.dot(left_ref[...], rooted, preferred_element_type=F32)
    out_ref[:, :ROWS, :] = precond.astype(BF16).reshape(pieces, rows, width)

    columns = pl.multiple_of(rep * width, width)
    own_columns = block_ref[:, :, pl.ds(columns, width)].reshape(order, width)
    own_rows = block_ref[pl.ds(rep * (width // rows), width // rows)].reshape(width, order)
    left = lax.dot_general(
        own_rows, block, (((1,), (1,)), ((), ())), preferred_element_type=F32
    ).astype(BF16)
    for index in range(pieces):
        row, column = row_piece(index)
        out_ref[index, ROWS : ROWS + TILE] = left[row : row + TILE, column : column + width]
        out_ref[index, ROWS + TILE : 2 * ROWS] = left[
            row : row + TILE, column + width : column + 2 * width
        ]
    right = jnp.dot(own_columns.T, block, preferred_element_type=F32).T
    out_ref[:, 2 * ROWS : 3 * ROWS, :] = right.astype(BF16).reshape(pieces, rows, width)

    own = own_columns.astype(F32)
    lane = lax.broadcasted_iota(jnp.int32, (TILE, width), 1)
    total = jnp.zeros((TILE, width), F32)
    parts = split_three(jnp.sum(precond * precond, keepdims=True))
    parts += split_three(jnp.sum(own * own, keepdims=True))
    for index, part in enumerate(parts):
        total = jnp.where(lane == index, part, total)
    out_ref[:, 3 * ROWS :, :] = jnp.broadcast_to(total.astype(BF16), (pieces, TILE, width))


def block_shares(rep, block, roots, shares):
    pieces, _, order = block.shape
    out = (pieces, 3 * ROWS + TILE, LANES)
    return pl.pallas_call(
        block_kernel,
        in_specs=[pl.BlockSpec(memory_space=pltpu.SMEM)]
        + [pl.BlockSpec(memory_space=pltpu.VMEM)] * (2 + len(shares)),
        out_specs=pl.BlockSpec(memory_space=pltpu.VMEM),
        out_shape=jax.ShapeDtypeStruct(out, BF16),
        scratch_shapes=[pltpu.VMEM((order, order), BF16)],
        compiler_params=params(),
        name="block_shares",
    )(rep, block, roots, *shares)


def deal_kernel(sources_ref, arrived_ref, update_ref, products_ref):
    count = arrived_ref.shape[0]
    line = lax.broadcasted_iota(jnp.int32, (ROWS, LANES), 0)
    sums = jnp.zeros((ROWS, LANES), F32)
    for index in range(count):
        update_ref[index] = arrived_ref[index, :ROWS, :]
        tail = arrived_ref[index, 3 * ROWS :, :].astype(F32)
        sums = jnp.where(line == index, jnp.concatenate([tail, tail], axis=0), sums)
    update_ref[count] = sums.astype(BF16)
    slots = products_ref.shape[1] // (2 * ROWS)
    for owner in range(products_ref.shape[0]):
        for slot in range(slots):
            source = sources_ref[owner * slots + slot]
            products_ref[owner, 2 * ROWS * slot : 2 * ROWS * (slot + 1)] = arrived_ref[
                source, ROWS : 3 * ROWS, :
            ]


def deal(sources, arrived, owners):
    count = arrived.shape[0]
    shapes = [
        (count + 1, ROWS, LANES),
        (owners, sources.shape[0] // owners * 2 * ROWS, LANES),
    ]
    return pl.pallas_call(
        deal_kernel,
        grid_spec=pltpu.PrefetchScalarGridSpec(
            num_scalar_prefetch=1,
            grid=(1,),
            in_specs=[whole(arrived.shape)],
            out_specs=[whole(shape) for shape in shapes],
        ),
        out_shape=[jax.ShapeDtypeStruct(shape, BF16) for shape in shapes],
        compiler_params=params(),
        name="deal",
    )(sources, arrived)


def finish_kernel(rep_ref, *refs):
    shares, (out_ref, scale_ref) = refs[:-2], refs[-2:]
    count, rows, order = out_ref.shape
    width = LANES
    half = shares[7].shape[0]
    replicas = order // width
    sums = shares[8][count - half].astype(F32)
    for share in shares[:7]:
        sums += share[count].astype(F32)
    lane = lax.broadcasted_iota(jnp.int32, (rows, width), 1)
    pre = jnp.sum(jnp.where(lane < 3, sums, 0.0), axis=1, keepdims=True)
    grad = jnp.sum(jnp.where((lane >= 3) & (lane < 6), sums, 0.0), axis=1, keepdims=True)
    scale = jnp.sqrt(grad) / jnp.sqrt(pre + epsilon)
    scale_ref[...] = jnp.broadcast_to(scale, (rows, width))

    def place(index, share, column):
        factor = scale_ref[pl.ds(index, 1), :]
        start = pl.multiple_of(column * width, width)
        out_ref[index, :, pl.ds(start, width)] = (share.astype(F32) * factor).astype(BF16)

    for index in range(count):
        for share, distance in zip(shares[:7], DISTANCES):
            place(index, share[index], lax.rem(rep_ref[0] - distance + replicas, replicas))
        far = lax.rem(rep_ref[0] + replicas // 2, replicas)
        share = shares[7][index] if index < half else shares[8][index - half]
        place(index, share, far)


def finish(rep, shares, count, rows, order):
    return pl.pallas_call(
        finish_kernel,
        in_specs=[pl.BlockSpec(memory_space=pltpu.SMEM)]
        + [pl.BlockSpec(memory_space=pltpu.VMEM)] * len(shares),
        out_specs=pl.BlockSpec(memory_space=pltpu.VMEM),
        out_shape=jax.ShapeDtypeStruct((count, rows, order), BF16),
        scratch_shapes=[pltpu.VMEM((count, LANES), F32)],
        compiler_params=params(),
        name="finish",
    )(rep, *shares)


def factor_kernel(occupied_ref, products_ref, left_ref, right_ref, left_out, right_out):
    pieces = products_ref.shape[0]
    order, width = right_ref.shape
    occupied = occupied_ref[pl.program_id(0)]
    weight = (1.0 - decay_rate) * occupied.astype(F32)
    for index in range(pieces):
        row, column = row_piece(index)
        piece = products_ref[index].astype(F32)
        for part in range(2):
            at = (pl.ds(row, TILE), pl.ds(column + part * width, width))
            product = piece[part * TILE : (part + 1) * TILE]
            left_out[at] = decay_rate * left_ref[at] + weight * product
        at = pl.ds(ROWS * index, ROWS)
        right_out[at, :] = decay_rate * right_ref[at, :] + weight * piece[ROWS:]


def factors(occupied, products, left, right):
    slots, width, order = left.shape[1:]
    left_spec = pl.BlockSpec((None, None, width, order), lambda k, a: (0, k, 0, 0))
    right_spec = pl.BlockSpec((None, None, order, width), lambda k, a: (0, k, 0, 0))
    pieces = products.shape[0]
    return pl.pallas_call(
        factor_kernel,
        grid_spec=pltpu.PrefetchScalarGridSpec(
            num_scalar_prefetch=1,
            grid=(slots,),
            in_specs=[
                pl.BlockSpec((pieces, 2 * ROWS, LANES), lambda k, a: (0, k, 0)),
                left_spec,
                right_spec,
            ],
            out_specs=[left_spec, right_spec],
        ),
        out_shape=[
            jax.ShapeDtypeStruct(left.shape, F32),
            jax.ShapeDtypeStruct(right.shape, F32),
        ],
        compiler_params=params(),
        name="factors",
    )(occupied, products, left, right)


def ring_gather(share, axis):
    size = lax.axis_size(axis)
    half = share.shape[0] // 2

    def shift(value, by):
        return lax.ppermute(value, axis, [(i, (i + by) % size) for i in range(size)])

    up, down = [share], [share]
    for _ in range(size // 2 - 1):
        up.append(shift(up[-1], 1))
        down.append(shift(down[-1], -1))
    far_up = shift(up[-1][:half], 1)
    far_down = shift(down[-1][half:], -1)
    return up + down[1:] + [far_up, far_down]


def exchange(value):
    return lax.all_to_all(value, "fsdp", split_axis=0, concat_axis=0, tiled=True)


def local(gradient, block_owner, block_slot, left_state, right_state, left_root, right_root):
    owners = lax.axis_size("fsdp")
    count, rows, order = gradient.shape
    slots = left_state.shape[1]
    rep = lax.axis_index("rep").astype(jnp.int32).reshape(1)
    flat_index = block_owner * slots + block_slot
    matches = flat_index[None, :] == jnp.arange(owners * slots, dtype=jnp.int32)[:, None]
    occupied = jnp.any(matches, axis=1).astype(jnp.int32)
    numbers = jnp.arange(count, dtype=jnp.int32)
    sources = jnp.sum(jnp.where(matches, numbers[None, :], 0), axis=1)
    mine = lax.dynamic_slice_in_dim(occupied, lax.axis_index("fsdp") * slots, slots, 0)

    spread = exchange(pack(left_root[0], right_root[0], owners))
    roots = exchange(route(block_owner, block_slot, spread))
    roots, gradient = lax.optimization_barrier((roots, gradient))
    left_shares = ring_gather(roots[:, :ROWS, :], "rep")
    block = exchange(gradient)

    arrived = exchange(block_shares(rep, block, roots, left_shares))
    named, products = deal(sources, arrived, owners)
    products = exchange(products)
    update = finish(rep, ring_gather(named, "rep"), count, rows, order)
    left_factor, right_factor = factors(mine, products, left_state, right_state)
    return (update, left_factor, right_factor)


def solution(mesh):
    in_specs = (
        P(None, "fsdp", None),
        P(),
        P(),
        P("fsdp", None, "rep", None),
        P("fsdp", None, None, "rep"),
        P("fsdp", None, "rep", None),
        P("fsdp", None, None, "rep"),
    )
    out_specs = (P(None, "fsdp", None), P("fsdp", None, "rep", None), P("fsdp", None, None, "rep"))
    return jax.shard_map(local, mesh=mesh, in_specs=in_specs, out_specs=out_specs, check_vma=False)
```

time: 329 us -> 180 us (0.55)
  waiting for transfers between devices: 146 us -> 54 us
  blocking collectives: 99 us -> 43.8 us
  starting transfers between devices: 7.67 us -> 45.7 us
  matrix products: 21.9 us -> 0 us
  Pallas kernels: 0 us -> 13.5 us
  between operations: 14.1 us -> 0.79 us
  other arithmetic: 10.3 us -> 0.19 us
  local copies, waits for them, and re-layouts: 29.8 us -> 21.5 us
    all_gather x2 -> x0, waiting for transfers between devices: 70.5 us -> none  [the longest x1 70.5 us: local(): assembled = lax.all_gather(update_part, 'rep', axis=2, tiled=True)]
    all_to_all x1 -> x3, waiting for transfers between devices: 74.7 us -> 14.1 us  [exchange(): lax.all_to_all(value, 'fsdp', split_axis=0, concat_axis=0, tiled=True)]
    ppermute x0 -> x16, waiting for transfers between devices: none -> 39.8 us  [shift(): lax.ppermute(value, axis, [(i, (i + by) % size) for i in range(size)])]
    all_to_all x1 -> x2, blocking collectives: 79.1 us -> 43.8 us  [exchange(): lax.all_to_all(value, 'fsdp', split_axis=0, concat_axis=0, tiled=True)]
    ppermute x0 -> x16, starting transfers between devices: none -> 28 us  [shift(): lax.ppermute(value, axis, [(i, (i + by) % size) for i in range(size)])]
    dot_general x3 -> x0, matrix products: 21.9 us -> none  [the longest x1 8.37 us: local(): jnp.einsum('kij,kjc->kic', lax.all_gather(left_root[0], 'rep', axis=1, ti...]
    psum x1 -> x0, blocking collectives: 20 us -> none  [local(): pre_squares = lax.psum(pre_part, 'rep')]
    unnamed x8 -> x54, local copies, waits for them, and re-layouts: 0.02 us -> 18.1 us
  transfers between devices with their start and end apart: 3 -> 19, of which waited for: 2 -> 10; matrix products, arithmetic and copies ran while one was open for 9% -> 2% of each run, Pallas kernels for 0% -> 2%
where the time goes in v2:
time: 180 us; the launch traced here: 179 us
  waiting for transfers between devices  54 us (30%)
  starting transfers between devices  45.7 us (25%)
  blocking collectives  43.8 us (24%)
  local copies, waits for them, and re-layouts  21.5 us (12%)
  Pallas kernels  13.5 us (8%)
    all_to_all x2, blocking collectives, exchange(): lax.all_to_all(value, 'fsdp', split_axis=0, concat_axis=0, tiled=True)  43.8 us
    ppermute x16, waiting for transfers between devices, shift(): lax.ppermute(value, axis, [(i, (i + by) % size) for i in range(size)])  39.8 us
    ppermute x16, starting transfers between devices, shift(): lax.ppermute(value, axis, [(i, (i + by) % size) for i in range(size)])  28 us
    unnamed x54, local copies, waits for them, and re-layouts  18.1 us
    all_to_all x3, starting transfers between devices, exchange(): lax.all_to_all(value, 'fsdp', split_axis=0, concat_axis=0, tiled=True)  17.7 us
    all_to_all x3, waiting for transfers between devices, exchange(): lax.all_to_all(value, 'fsdp', split_axis=0, concat_axis=0, tiled=True)  14.1 us
    pallas_call x1, Pallas kernels, block_shares(): pl.pallas_call(block_kernel, in_specs=[pl.BlockSpec(memory_space=pltpu.SM...  5.25 us
  transfers between devices with their start and end apart: 19, of which 10 were waited for; matrix products, arithmetic and copies ran while one was open for 2% of the time, Pallas kernels for 2%

profile of v2, /device:TPU:8, one launch (start us, length us, event | category | flops | bytes accessed | tf_op | source)
XLA Modules:
  0.0 179.4 jit_solution(8906760107566838259)
XLA Ops:
  0.6 1.1 copy-done.2
  1.8 1.1 copy-done.3
  2.9 0.2 pack.1
  3.1 0.0 copy-start.25
  3.1 0.0 copy-start.26
  3.1 28.7 %all_to_all.25.arrived_ref = bf16[32,192,128]{2,1,0:T(8,128)(2,1)S(1)} all-to-all(bf16[32,192,128]{2,1,0:T(8,128)(2,1)S(1)} %pack.1), channel_id=1, replica_groups=mesh['fsdp'=32,'rep'=8] {'fsdp'}, dimensions={0} | all-to-all | bytes 3145728 | tf_op jit(solution)/shard_map/all_to_all | solution.py:293
  31.8 0.6 route.1
  32.4 15.1 %all_to_all.26.roots_ref = bf16[32,64,128]{2,1,0:T(8,128)(2,1)S(1)} all-to-all(bf16[32,64,128]{2,1,0:T(8,128)(2,1)S(1)} %route.1), channel_id=1, replica_groups=mesh['fsdp'=32,'rep'=8] {'fsdp'}, dimensions={0} | all-to-all | bytes 1048576 | tf_op jit(solution)/shard_map/all_to_all | solution.py:293
  47.5 5.1 %all-to-all-start.2 = ((bf16[32,32,1024]{2,1,0:T(8,128)(2,1)}), bf16[32,32,1024]{2,1,0:T(8,128)(2,1)S(1)}, u32[]{:S(2)}, u32[]{:S(2)}) async-start(bf16[32,32,1024]{2,1,0:T(8,128)(2,1)} %param.7), calls=%async_computation.2 | async-start | bytes 4194304 | tf_op jit(solution)/shard_map/all_to_all | solution.py:293
  52.6 5.9 %collective-permute-start.3 = (bf16[32,32,128]{2,1,0:T(8,128)(2,1)S(1)}, bf16[32,32,128]{2,1,0:T(8,128)(2,1)S(1)}, u32[]{:S(2)}, u32[]{:S(2)}) collective-permute-start(bf16[32,32,128]{2,1,0:T(8,128)(2,1)S(1)} %slice.15.refs_0_), channel_id=1, source_target_pairs={{0,7},{1,0},{2,1},{3,2},{4,3},{5,4},{6,5},{7,6},{8,15},{9,8},{10,9... | collective-permute-start | bytes 786440 | tf_op jit(solution)/shard_map/ppermute | solution.py:281
  58.6 5.9 %collective-permute-done.3.refs_4_ = bf16[32,32,128]{2,1,0:T(8,128)(2,1)S(1)} collective-permute-done((bf16[32,32,128]{2,1,0:T(8,128)(2,1)S(1)}, bf16[32,32,128]{2,1,0:T(8,128)(2,1)S(1)}, u32[]{:S(2)}, u32[]{:S(2)}) %collective-permute-start.3) | collective-permute-done | bytes 262176 | tf_op jit(solution)/shard_map/ppermute | solution.py:281
  64.4 3.7 %collective-permute-start.4 = (bf16[32,32,128]{2,1,0:T(8,128)(2,1)S(1)}, bf16[32,32,128]{2,1,0:T(8,128)(2,1)S(1)}, u32[]{:S(2)}, u32[]{:S(2)}) collective-permute-start(bf16[32,32,128]{2,1,0:T(8,128)(2,1)S(1)} %collective-permute-done.3.refs_4_), channel_id=1, source_target_pairs={{0,7},{1,0},{2,1},{3,2},{4,3},{5,4},{6,5},{7,6},{8,15},{9,8},{10,9... | collective-permute-start | bytes 786440 | tf_op jit(solution)/shard_map/ppermute | solution.py:281
  68.1 0.7 copy-done.16
  68.8 0.7 copy-done.18
  69.5 3.6 %collective-permute-done.4.refs_5_ = bf16[32,32,128]{2,1,0:T(8,128)(2,1)S(1)} collective-permute-done((bf16[32,32,128]{2,1,0:T(8,128)(2,1)S(1)}, bf16[32,32,128]{2,1,0:T(8,128)(2,1)S(1)}, u32[]{:S(2)}, u32[]{:S(2)}) %collective-permute-start.4) | collective-permute-done | bytes 262176 | tf_op jit(solution)/shard_map/ppermute | solution.py:281
  73.2 3.7 %collective-permute-start.5 = (bf16[32,32,128]{2,1,0:T(8,128)(2,1)S(1)}, bf16[32,32,128]{2,1,0:T(8,128)(2,1)S(1)}, u32[]{:S(2)}, u32[]{:S(2)}) collective-permute-start(bf16[32,32,128]{2,1,0:T(8,128)(2,1)S(1)} %collective-permute-done.4.refs_5_), channel_id=1, source_target_pairs={{0,7},{1,0},{2,1},{3,2},{4,3},{5,4},{6,5},{7,6},{8,15},{9,8},{10,9... | collective-permute-start | bytes 786440 | tf_op jit(solution)/shard_map/ppermute | solution.py:281
  76.9 0.7 copy-done.20
  77.6 0.0 collective-permute-done.1.refs_2_
  77.6 3.4 %collective-permute-done.5.refs_6_ = bf16[32,32,128]{2,1,0:T(8,128)(2,1)S(1)} collective-permute-done((bf16[32,32,128]{2,1,0:T(8,128)(2,1)S(1)}, bf16[32,32,128]{2,1,0:T(8,128)(2,1)S(1)}, u32[]{:S(2)}, u32[]{:S(2)}) %collective-permute-start.5) | collective-permute-done | bytes 262176 | tf_op jit(solution)/shard_map/ppermute | solution.py:281
  81.0 0.7 slice.21
  81.6 3.7 %collective-permute-start.7 = (bf16[16,32,128]{2,1,0:T(8,128)(2,1)}, bf16[16,32,128]{2,1,0:T(8,128)(2,1)S(1)}, u32[]{:S(2)}, u32[]{:S(2)}) collective-permute-start(bf16[16,32,128]{2,1,0:T(8,128)(2,1)} %slice.21), channel_id=1, source_target_pairs={{0,7},{1,0},{2,1},{3,2},{4,3},{5,4},{6,5},{7,6},{8,15},{9,8},{10,9... | collective-permute-start | bytes 393224 | tf_op jit(solution)/shard_map/ppermute | solution.py:281
  85.3 0.0 collective-permute-done.2.refs_3_
  85.3 0.7 slice.20
  86.0 2.2 %collective-permute-done.7.refs_8_ = bf16[16,32,128]{2,1,0:T(8,128)(2,1)S(1)} collective-permute-done((bf16[16,32,128]{2,1,0:T(8,128)(2,1)}, bf16[16,32,128]{2,1,0:T(8,128)(2,1)S(1)}, u32[]{:S(2)}, u32[]{:S(2)}) %collective-permute-start.7) | collective-permute-done | bytes 131104 | tf_op jit(solution)/shard_map/ppermute | solution.py:281
  88.2 4.3 %collective-permute-done.6.refs_7_ = bf16[16,32,128]{2,1,0:T(8,128)(2,1)} collective-permute-done((bf16[16,32,128]{2,1,0:T(8,128)(2,1)}, bf16[16,32,128]{2,1,0:T(8,128)(2,1)}, u32[]{:S(2)}, u32[]{:S(2)}) %collective-permute-start.6) | collective-permute-done | bytes 131104 | tf_op jit(solution)/shard_map/ppermute | solution.py:281
  92.5 0.9 copy-done.17
  93.5 0.9 copy-done.19
  94.4 0.9 copy-done.21
  95.4 0.9 copy-done.23
  96.3 5.2 %block_shares.1 = bf16[32,112,128]{2,1,0:T(8,128)(2,1)} custom-call(s32[1]{0:T(128)} %bitcast.rep_ref, bf16[32,32,1024]{2,1,0:T(8,128)(2,1)S(1)} %all-to-all-done.2.block_ref, bf16[32,64,128]{2,1,0:T(8,128)(2,1)S(1)} %all_to_all.26.roots_ref, bf16[32,32,128]{2,1,0:T(8,128)(2,1)S(1)} %slice.15.refs_0_, bf16[32,32,128]{2,1,0:T(8,128)(2,1)S(1)} %copy-done.19, ...), custom_call_target="tpu_custom_call" | custom-call | tf_op jit(solution)/shard_map/block_shares/pallas_call | solution.py:143
  101.5 7.4 %all-to-all-start.3 = ((bf16[32,112,128]{2,1,0:T(8,128)(2,1)}), bf16[32,112,128]{2,1,0:T(8,128)(2,1)S(1)}, u32[]{:S(2)}, u32[]{:S(2)}) async-start(bf16[32,112,128]{2,1,0:T(8,128)(2,1)} %block_shares.1), calls=%async_computation.3 | async-start | bytes 1835008 | tf_op jit(solution)/shard_map/all_to_all | solution.py:293
  108.9 0.1 select_reduce_fusion.sources_ref
  109.0 14.1 %all-to-all-done.3.arrived_ref = bf16[32,112,128]{2,1,0:T(8,128)(2,1)S(1)} async-done(((bf16[32,112,128]{2,1,0:T(8,128)(2,1)}), bf16[32,112,128]{2,1,0:T(8,128)(2,1)S(1)}, u32[]{:S(2)}, u32[]{:S(2)}) %all-to-all-start.3) | async-done | bytes 917536 | tf_op jit(solution)/shard_map/all_to_all | solution.py:293
  123.2 1.8 %deal.1 = (bf16[33,32,128]{2,1,0:T(8,128)(2,1)S(1)}, bf16[32,192,128]{2,1,0:T(8,128)(2,1)}) custom-call(s32[96]{0:T(128)S(1)} %select_reduce_fusion.sources_ref, bf16[32,112,128]{2,1,0:T(8,128)(2,1)S(1)} %all-to-all-done.3.arrived_ref), custom_call_target="tpu_custom_call" | custom-call | tf_op jit(solution)/shard_map/deal/pallas_call | solution.py:179
  125.0 5.2 %all-to-all-start.4 = ((bf16[32,192,128]{2,1,0:T(8,128)(2,1)}), bf16[32,192,128]{2,1,0:T(8,128)(2,1)S(1)}, u32[]{:S(2)}, u32[]{:S(2)}) async-start(bf16[32,192,128]{2,1,0:T(8,128)(2,1)} %get-tuple-element.12), calls=%async_computation.4 | async-start | bytes 3145728 | tf_op jit(solution)/shard_map/all_to_all | solution.py:293
  130.2 0.3 collective-permute-start.11
  130.5 2.0 %collective-permute-start.8 = (bf16[33,32,128]{2,1,0:T(8,128)(2,1)S(1)}, bf16[33,32,128]{2,1,0:T(8,128)(2,1)S(1)}, u32[]{:S(2)}, u32[]{:S(2)}) collective-permute-start(bf16[33,32,128]{2,1,0:T(8,128)(2,1)S(1)} %get-tuple-element.11.refs_0_), channel_id=1, source_target_pairs={{0,1},{1,2},{2,3},{3,4},{4,5},{5,6},{6,7},{7,0},{8,9},{9,10},{10,1... | collective-permute-start | bytes 811016 | tf_op jit(solution)/shard_map/ppermute | solution.py:281
  132.5 6.5 %collective-permute-done.11.refs_4_ = bf16[33,32,128]{2,1,0:T(8,128)(2,1)S(1)} collective-permute-done((bf16[33,32,128]{2,1,0:T(8,128)(2,1)S(1)}, bf16[33,32,128]{2,1,0:T(8,128)(2,1)S(1)}, u32[]{:S(2)}, u32[]{:S(2)}) %collective-permute-start.11) | collective-permute-done | bytes 270368 | tf_op jit(solution)/shard_map/ppermute | solution.py:281
  139.0 1.5 collective-permute-start.12
  140.5 0.7 copy-done.8
  141.2 0.0 collective-permute-done.8.refs_1_
  141.2 0.5 collective-permute-start.9
  141.8 5.0 %collective-permute-done.12.refs_5_ = bf16[33,32,128]{2,1,0:T(8,128)(2,1)S(1)} collective-permute-done((bf16[33,32,128]{2,1,0:T(8,128)(2,1)S(1)}, bf16[33,32,128]{2,1,0:T(8,128)(2,1)S(1)}, u32[]{:S(2)}, u32[]{:S(2)}) %collective-permute-start.12) | collective-permute-done | bytes 270368 | tf_op jit(solution)/shard_map/ppermute | solution.py:281
  146.7 3.0 %collective-permute-start.13 = (bf16[33,32,128]{2,1,0:T(8,128)(2,1)S(1)}, bf16[33,32,128]{2,1,0:T(8,128)(2,1)S(1)}, u32[]{:S(2)}, u32[]{:S(2)}) collective-permute-start(bf16[33,32,128]{2,1,0:T(8,128)(2,1)S(1)} %collective-permute-done.12.refs_5_), channel_id=1, source_target_pairs={{0,7},{1,0},{2,1},{3,2},{4,3},{5,4},{6,5},{7,6},{8,15},{9,8},{10,9... | collective-permute-start | bytes 811016 | tf_op jit(solution)/shard_map/ppermute | solution.py:281
  149.7 0.7 copy-done.12
  150.5 0.0 collective-permute-done.9.refs_2_
  150.5 0.7 copy-done.14
  151.2 3.2 %collective-permute-done.13.refs_6_ = bf16[33,32,128]{2,1,0:T(8,128)(2,1)S(1)} collective-permute-done((bf16[33,32,128]{2,1,0:T(8,128)(2,1)S(1)}, bf16[33,32,128]{2,1,0:T(8,128)(2,1)S(1)}, u32[]{:S(2)}, u32[]{:S(2)}) %collective-permute-start.13) | collective-permute-done | bytes 270368 | tf_op jit(solution)/shard_map/ppermute | solution.py:281
  154.4 0.7 slice.23
  155.1 3.7 %collective-permute-start.15 = (bf16[17,32,128]{2,1,0:T(8,128)(2,1)}, bf16[17,32,128]{2,1,0:T(8,128)(2,1)S(1)}, u32[]{:S(2)}, u32[]{:S(2)}) collective-permute-start(bf16[17,32,128]{2,1,0:T(8,128)(2,1)} %slice.23), channel_id=1, source_target_pairs={{0,7},{1,0},{2,1},{3,2},{4,3},{5,4},{6,5},{7,6},{8,15},{9,8},{10,9... | collective-permute-start | bytes 417800 | tf_op jit(solution)/shard_map/ppermute | solution.py:281
  158.8 0.7 slice.22
  159.5 0.1 fusion
  159.6 0.7 dynamic_slice.3.occupied_ref
  160.3 5.7 %collective-permute-done.14.refs_7_ = bf16[16,32,128]{2,1,0:T(8,128)(2,1)} collective-permute-done((bf16[16,32,128]{2,1,0:T(8,128)(2,1)}, bf16[16,32,128]{2,1,0:T(8,128)(2,1)}, u32[]{:S(2)}, u32[]{:S(2)}) %collective-permute-start.14) | collective-permute-done | bytes 131104 | tf_op jit(solution)/shard_map/ppermute | solution.py:281
  166.0 1.0 copy-done.5
  166.9 1.0 copy-done.7
  167.9 1.0 copy-done.9
  168.8 1.0 copy-done.11
  169.8 1.0 copy-done.13
  170.7 1.0 copy-done.15
  171.7 2.7 %finish.1 = bf16[32,32,1024]{2,1,0:T(8,128)(2,1)} custom-call(s32[1]{0:T(128)} %bitcast.rep_ref, bf16[33,32,128]{2,1,0:T(8,128)(2,1)S(1)} %copy-done.7, bf16[33,32,128]{2,1,0:T(8,128)(2,1)S(1)} %copy-done.11, bf16[33,32,128]{2,1,0:T(8,128)(2,1)S(1)} %copy-done.15, bf16[33,32,128]{2,1,0:T(8,128)(2,1)S(1)} %copy-done.5, bf16[33,32,128]{2,1,0:T(8,128)(2,1)S(1)} %copy-done.9, ...), custom_call_target="tpu_custom_call" | custom-call | tf_op jit(solution)/shard_map/finish/pallas_call | solution.py:222
  174.5 1.4 copy-done.1
  175.9 0.7 copy-done.24
  176.5 2.9 %factors.1 = (f32[1,3,128,1024]{3,2,1,0:T(8,128)}, f32[1,3,1024,128]{3,2,1,0:T(8,128)}) custom-call(s32[3]{0:T(128)S(1)} %copy-done.24, bf16[32,192,128]{2,1,0:T(8,128)(2,1)S(1)} %all-to-all-done.4.products_ref, f32[1,3,128,1024]{3,2,1,0:T(8,128)S(1)} %copy-done, f32[1,3,1024,128]{3,2,1,0:T(8,128)S(1)} %copy-done.1), custom_call_target="tpu_custom_call" | custom-call | tf_op jit(solution)/shard_map/factors/pallas_call | solution.py:255
  (46 shorter events, 0.1 us)
Async XLA Ops:
  0.6 1.1 copy-start.2
  1.8 1.1 copy-start.3
  3.1 28.7 %copy-start.25 = (s32[32]{0:T(128)S(1)}, s32[32]{0:T(128)}, u32[]{:S(2)}) copy-start(s32[32]{0:T(128)} %slot_ref.1) | copy-start | bytes 388
  3.1 28.7 %copy-start.26 = (s32[32]{0:T(128)S(1)}, s32[32]{0:T(128)}, u32[]{:S(2)}) copy-start(s32[32]{0:T(128)} %owner_ref.1) | copy-start | bytes 388
  47.5 45.0 %all-to-all-start.2 = ((bf16[32,32,1024]{2,1,0:T(8,128)(2,1)}), bf16[32,32,1024]{2,1,0:T(8,128)(2,1)S(1)}, u32[]{:S(2)}, u32[]{:S(2)}) async-start(bf16[32,32,1024]{2,1,0:T(8,128)(2,1)} %param.7), calls=%async_computation.2 | async-start | bytes 4194304 | tf_op jit(solution)/shard_map/all_to_all | solution.py:293
  52.6 11.8 %collective-permute-start.3 = (bf16[32,32,128]{2,1,0:T(8,128)(2,1)S(1)}, bf16[32,32,128]{2,1,0:T(8,128)(2,1)S(1)}, u32[]{:S(2)}, u32[]{:S(2)}) collective-permute-start(bf16[32,32,128]{2,1,0:T(8,128)(2,1)S(1)} %slice.15.refs_0_), channel_id=1, source_target_pairs={{0,7},{1,0},{2,1},{3,2},{4,3},{5,4},{6,5},{7,6},{8,15},{9,8},{10,9... | collective-permute-start | bytes 786440 | tf_op jit(solution)/shard_map/ppermute | solution.py:281
  58.6 10.3 %collective-permute-start = (bf16[32,32,128]{2,1,0:T(8,128)(2,1)S(1)}, bf16[32,32,128]{2,1,0:T(8,128)(2,1)S(1)}, u32[]{:S(2)}, u32[]{:S(2)}) collective-permute-start(bf16[32,32,128]{2,1,0:T(8,128)(2,1)S(1)} %slice.15.refs_0_), channel_id=1, source_target_pairs={{0,1},{1,2},{2,3},{3,4},{4,5},{5,6},{6,7},{7,0},{8,9},{9,10},{10,1... | collective-permute-start | bytes 786440 | tf_op jit(solution)/shard_map/ppermute | solution.py:281
  64.4 8.7 %collective-permute-start.4 = (bf16[32,32,128]{2,1,0:T(8,128)(2,1)S(1)}, bf16[32,32,128]{2,1,0:T(8,128)(2,1)S(1)}, u32[]{:S(2)}, u32[]{:S(2)}) collective-permute-start(bf16[32,32,128]{2,1,0:T(8,128)(2,1)S(1)} %collective-permute-done.3.refs_4_), channel_id=1, source_target_pairs={{0,7},{1,0},{2,1},{3,2},{4,3},{5,4},{6,5},{7,6},{8,15},{9,8},{10,9... | collective-permute-start | bytes 786440 | tf_op jit(solution)/shard_map/ppermute | solution.py:281
  68.1 0.7 copy-start.16
  68.8 8.7 %collective-permute-start.1 = (bf16[32,32,128]{2,1,0:T(8,128)(2,1)S(1)}, bf16[32,32,128]{2,1,0:T(8,128)(2,1)S(1)}, u32[]{:S(2)}, u32[]{:S(2)}) collective-permute-start(bf16[32,32,128]{2,1,0:T(8,128)(2,1)S(1)} %collective-permute-done.refs_1_), channel_id=1, source_target_pairs={{0,1},{1,2},{2,3},{3,4},{4,5},{5,6},{6,7},{7,0},{8,9},{9,10},{10,1... | collective-permute-start | bytes 786440 | tf_op jit(solution)/shard_map/ppermute | solution.py:281
  68.8 0.7 copy-start.18
  73.2 7.8 %collective-permute-start.5 = (bf16[32,32,128]{2,1,0:T(8,128)(2,1)S(1)}, bf16[32,32,128]{2,1,0:T(8,128)(2,1)S(1)}, u32[]{:S(2)}, u32[]{:S(2)}) collective-permute-start(bf16[32,32,128]{2,1,0:T(8,128)(2,1)S(1)} %collective-permute-done.4.refs_5_), channel_id=1, source_target_pairs={{0,7},{1,0},{2,1},{3,2},{4,3},{5,4},{6,5},{7,6},{8,15},{9,8},{10,9... | collective-permute-start | bytes 786440 | tf_op jit(solution)/shard_map/ppermute | solution.py:281
  76.9 0.7 copy-start.20
  77.6 7.8 %copy-start.22 = (bf16[32,32,128]{2,1,0:T(8,128)(2,1)}, bf16[32,32,128]{2,1,0:T(8,128)(2,1)S(1)}, u32[]{:S(2)}) copy-start(bf16[32,32,128]{2,1,0:T(8,128)(2,1)S(1)} %collective-permute-done.1.refs_2_) | copy-start | bytes 786436
  77.6 7.8 %collective-permute-start.2 = (bf16[32,32,128]{2,1,0:T(8,128)(2,1)S(1)}, bf16[32,32,128]{2,1,0:T(8,128)(2,1)S(1)}, u32[]{:S(2)}, u32[]{:S(2)}) collective-permute-start(bf16[32,32,128]{2,1,0:T(8,128)(2,1)S(1)} %collective-permute-done.1.refs_2_), channel_id=1, source_target_pairs={{0,1},{1,2},{2,3},{3,4},{4,5},{5,6},{6,7},{7,0},{8,9},{9,10},{10,1... | collective-permute-start | bytes 786440 | tf_op jit(solution)/shard_map/ppermute | solution.py:281
  81.6 6.5 %collective-permute-start.7 = (bf16[16,32,128]{2,1,0:T(8,128)(2,1)}, bf16[16,32,128]{2,1,0:T(8,128)(2,1)S(1)}, u32[]{:S(2)}, u32[]{:S(2)}) collective-permute-start(bf16[16,32,128]{2,1,0:T(8,128)(2,1)} %slice.21), channel_id=1, source_target_pairs={{0,7},{1,0},{2,1},{3,2},{4,3},{5,4},{6,5},{7,6},{8,15},{9,8},{10,9... | collective-permute-start | bytes 393224 | tf_op jit(solution)/shard_map/ppermute | solution.py:281
  86.0 6.5 %collective-permute-start.6 = (bf16[16,32,128]{2,1,0:T(8,128)(2,1)}, bf16[16,32,128]{2,1,0:T(8,128)(2,1)}, u32[]{:S(2)}, u32[]{:S(2)}) collective-permute-start(bf16[16,32,128]{2,1,0:T(8,128)(2,1)} %slice.20), channel_id=1, source_target_pairs={{0,1},{1,2},{2,3},{3,4},{4,5},{5,6},{6,7},{7,0},{8,9},{9,10},{10,1... | collective-permute-start | bytes 393224 | tf_op jit(solution)/shard_map/ppermute | solution.py:281
  92.5 1.0 copy-start.17
  93.5 0.9 copy-start.19
  94.4 0.9 copy-start.21
  95.4 0.9 copy-start.23
  101.5 21.6 %all-to-all-start.3 = ((bf16[32,112,128]{2,1,0:T(8,128)(2,1)}), bf16[32,112,128]{2,1,0:T(8,128)(2,1)S(1)}, u32[]{:S(2)}, u32[]{:S(2)}) async-start(bf16[32,112,128]{2,1,0:T(8,128)(2,1)} %block_shares.1), calls=%async_computation.3 | async-start | bytes 1835008 | tf_op jit(solution)/shard_map/all_to_all | solution.py:293
  125.0 5.5 %copy-start.6 = (bf16[33,32,128]{2,1,0:T(8,128)(2,1)}, bf16[33,32,128]{2,1,0:T(8,128)(2,1)S(1)}, u32[]{:S(2)}) copy-start(bf16[33,32,128]{2,1,0:T(8,128)(2,1)S(1)} %get-tuple-element.11.refs_0_) | copy-start | bytes 811012
  125.0 49.5 %all-to-all-start.4 = ((bf16[32,192,128]{2,1,0:T(8,128)(2,1)}), bf16[32,192,128]{2,1,0:T(8,128)(2,1)S(1)}, u32[]{:S(2)}, u32[]{:S(2)}) async-start(bf16[32,192,128]{2,1,0:T(8,128)(2,1)} %get-tuple-element.12), calls=%async_computation.4 | async-start | bytes 3145728 | tf_op jit(solution)/shard_map/all_to_all | solution.py:293
  130.2 8.8 %collective-permute-start.11 = (bf16[33,32,128]{2,1,0:T(8,128)(2,1)S(1)}, bf16[33,32,128]{2,1,0:T(8,128)(2,1)S(1)}, u32[]{:S(2)}, u32[]{:S(2)}) collective-permute-start(bf16[33,32,128]{2,1,0:T(8,128)(2,1)S(1)} %get-tuple-element.11.refs_0_), channel_id=1, source_target_pairs={{0,7},{1,0},{2,1},{3,2},{4,3},{5,4},{6,5},{7,6},{8,15},{9,8},{10,9... | collective-permute-start | bytes 811016 | tf_op jit(solution)/shard_map/ppermute | solution.py:281
  130.5 10.7 %collective-permute-start.8 = (bf16[33,32,128]{2,1,0:T(8,128)(2,1)S(1)}, bf16[33,32,128]{2,1,0:T(8,128)(2,1)S(1)}, u32[]{:S(2)}, u32[]{:S(2)}) collective-permute-start(bf16[33,32,128]{2,1,0:T(8,128)(2,1)S(1)} %get-tuple-element.11.refs_0_), channel_id=1, source_target_pairs={{0,1},{1,2},{2,3},{3,4},{4,5},{5,6},{6,7},{7,0},{8,9},{9,10},{10,1... | collective-permute-start | bytes 811016 | tf_op jit(solution)/shard_map/ppermute | solution.py:281
  139.0 7.7 %collective-permute-start.12 = (bf16[33,32,128]{2,1,0:T(8,128)(2,1)S(1)}, bf16[33,32,128]{2,1,0:T(8,128)(2,1)S(1)}, u32[]{:S(2)}, u32[]{:S(2)}) collective-permute-start(bf16[33,32,128]{2,1,0:T(8,128)(2,1)S(1)} %collective-permute-done.11.refs_4_), channel_id=1, source_target_pairs={{0,7},{1,0},{2,1},{3,2},{4,3},{5,4},{6,5},{7,6},{8,15},{9,8},{10,9... | collective-permute-start | bytes 811016 | tf_op jit(solution)/shard_map/ppermute | solution.py:281
  140.5 0.7 copy-start.8
  141.2 18.4 %copy-start.10 = (bf16[33,32,128]{2,1,0:T(8,128)(2,1)}, bf16[33,32,128]{2,1,0:T(8,128)(2,1)S(1)}, u32[]{:S(2)}) copy-start(bf16[33,32,128]{2,1,0:T(8,128)(2,1)S(1)} %collective-permute-done.8.refs_1_) | copy-start | bytes 811012
  141.2 9.2 %collective-permute-start.9 = (bf16[33,32,128]{2,1,0:T(8,128)(2,1)S(1)}, bf16[33,32,128]{2,1,0:T(8,128)(2,1)S(1)}, u32[]{:S(2)}, u32[]{:S(2)}) collective-permute-start(bf16[33,32,128]{2,1,0:T(8,128)(2,1)S(1)} %collective-permute-done.8.refs_1_), channel_id=1, source_target_pairs={{0,1},{1,2},{2,3},{3,4},{4,5},{5,6},{6,7},{7,0},{8,9},{9,10},{10,1... | collective-permute-start | bytes 811016 | tf_op jit(solution)/shard_map/ppermute | solution.py:281
  146.7 7.7 %collective-permute-start.13 = (bf16[33,32,128]{2,1,0:T(8,128)(2,1)S(1)}, bf16[33,32,128]{2,1,0:T(8,128)(2,1)S(1)}, u32[]{:S(2)}, u32[]{:S(2)}) collective-permute-start(bf16[33,32,128]{2,1,0:T(8,128)(2,1)S(1)} %collective-permute-done.12.refs_5_), channel_id=1, source_target_pairs={{0,7},{1,0},{2,1},{3,2},{4,3},{5,4},{6,5},{7,6},{8,15},{9,8},{10,9... | collective-permute-start | bytes 811016 | tf_op jit(solution)/shard_map/ppermute | solution.py:281
  149.7 0.7 copy-start.12
  150.5 8.3 %collective-permute-start.10 = (bf16[33,32,128]{2,1,0:T(8,128)(2,1)S(1)}, bf16[33,32,128]{2,1,0:T(8,128)(2,1)S(1)}, u32[]{:S(2)}, u32[]{:S(2)}) collective-permute-start(bf16[33,32,128]{2,1,0:T(8,128)(2,1)S(1)} %collective-permute-done.9.refs_2_), channel_id=1, source_target_pairs={{0,1},{1,2},{2,3},{3,4},{4,5},{5,6},{6,7},{7,0},{8,9},{9,10},{10,1... | collective-permute-start | bytes 811016 | tf_op jit(solution)/shard_map/ppermute | solution.py:281
  150.5 0.7 copy-start.14
  155.1 10.9 %collective-permute-start.15 = (bf16[17,32,128]{2,1,0:T(8,128)(2,1)}, bf16[17,32,128]{2,1,0:T(8,128)(2,1)S(1)}, u32[]{:S(2)}, u32[]{:S(2)}) collective-permute-start(bf16[17,32,128]{2,1,0:T(8,128)(2,1)} %slice.23), channel_id=1, source_target_pairs={{0,7},{1,0},{2,1},{3,2},{4,3},{5,4},{6,5},{7,6},{8,15},{9,8},{10,9... | collective-permute-start | bytes 417800 | tf_op jit(solution)/shard_map/ppermute | solution.py:281
  158.8 0.8 copy-start.4
  159.5 6.5 %collective-permute-start.14 = (bf16[16,32,128]{2,1,0:T(8,128)(2,1)}, bf16[16,32,128]{2,1,0:T(8,128)(2,1)}, u32[]{:S(2)}, u32[]{:S(2)}) collective-permute-start(bf16[16,32,128]{2,1,0:T(8,128)(2,1)} %slice.22), channel_id=1, source_target_pairs={{0,1},{1,2},{2,3},{3,4},{4,5},{5,6},{6,7},{7,0},{8,9},{9,10},{10,1... | collective-permute-start | bytes 393224 | tf_op jit(solution)/shard_map/ppermute | solution.py:281
  160.3 14.2 %copy-start = (f32[1,3,128,1024]{3,2,1,0:T(8,128)S(1)}, f32[1,3,128,1024]{3,2,1,0:T(8,128)}, u32[]{:S(2)}) copy-start(f32[1,3,128,1024]{3,2,1,0:T(8,128)} %left_ref.1) | copy-start | bytes 4718596
  166.0 1.0 copy-start.5
  166.9 1.0 copy-start.7
  167.9 1.0 copy-start.9
  168.8 1.0 copy-start.11
  169.8 1.0 copy-start.13
  170.7 1.0 copy-start.15
  174.4 1.4 copy-start.1
  175.9 0.7 copy-start.24

commit v3 on v2

v3 whole, which is shorter than its diff:
```python
import jax
import jax.numpy as jnp
from jax import lax
from jax.experimental import pallas as pl
from jax.experimental.pallas import tpu as pltpu
from jax.sharding import PartitionSpec as P

decay_rate = 0.95
epsilon = 1e-06

F32 = jnp.float32
BF16 = jnp.bfloat16
ROWS = 32
TILE = 16
LANES = 128
DISTANCES = (0, 1, 2, 3, -1, -2, -3)


def params(mebibytes):
    return pltpu.CompilerParams(vmem_limit_bytes=mebibytes * 1024 * 1024)


def in_hbm(*arrays):
    return [pltpu.with_memory_space_constraint(array, pltpu.HBM) for array in arrays]


def cost(flops, accessed):
    return pl.CostEstimate(flops=flops, bytes_accessed=accessed, transcendentals=0)


def whole(shape):
    return pl.BlockSpec(shape, lambda *_: (0,) * len(shape))


def row_piece(index):
    per_line = 1024 // (2 * LANES)
    return TILE * (index // per_line), 2 * LANES * (index % per_line)


def split_three(value):
    high = value.astype(BF16).astype(F32)
    rest = value - high
    middle = rest.astype(BF16).astype(F32)
    return high, middle, (rest - middle).astype(BF16).astype(F32)


SOURCE = 0
HOME_BLOCK = 96
HOME_ORIGIN = 128
SPARE_HOME = 160
PLAN = 256


def plan_kernel(owner_ref, slot_ref, plan_ref, list_ref):
    owners = HOME_ORIGIN - HOME_BLOCK
    slots = (HOME_BLOCK - SOURCE) // owners

    def clear(index, carry):
        plan_ref[SOURCE + index] = -1
        return carry

    def clear_spare(index, carry):
        plan_ref[SPARE_HOME + index] = 0
        return carry

    def enter(index, carry):
        plan_ref[SOURCE + owner_ref[index] * slots + slot_ref[index]] = index
        return carry

    def walk(owner, carry):
        spare, idle = carry
        count = 0
        for slot in range(slots):
            block = plan_ref[SOURCE + owner * slots + slot]
            named = block >= 0

            @pl.when(named & (count == 0))
            def _():
                plan_ref[HOME_BLOCK + owner] = block
                plan_ref[HOME_ORIGIN + owner] = -1

            @pl.when(named & (count > 0))
            def _():
                list_ref[0, spare] = block
                list_ref[1, spare] = owner * 2 + count - 1

            spare += (named & (count > 0)).astype(jnp.int32)
            count += named.astype(jnp.int32)

        @pl.when(count == 0)
        def _():
            list_ref[2, idle] = owner

        return spare, idle + (count == 0).astype(jnp.int32)

    def assign(index, carry):
        home = list_ref[2, index]
        origin = list_ref[1, index]
        plan_ref[HOME_BLOCK + home] = list_ref[0, index]
        plan_ref[HOME_ORIGIN + home] = origin
        plan_ref[SPARE_HOME + origin] = home
        return carry

    zero = jnp.int32(0)
    lax.fori_loop(0, owners * slots, clear, zero)
    lax.fori_loop(0, 2 * owners, clear_spare, zero)
    lax.fori_loop(0, owner_ref.shape[0], enter, zero)
    _, idle = lax.fori_loop(0, owners, walk, (zero, zero))
    lax.fori_loop(0, idle, assign, zero)


def make_plan(owner, slot):
    smem = pl.BlockSpec(memory_space=pltpu.SMEM)
    return pl.pallas_call(
        plan_kernel,
        in_specs=[smem, smem],
        out_specs=smem,
        out_shape=jax.ShapeDtypeStruct((PLAN,), jnp.int32),
        scratch_shapes=[pltpu.SMEM((3, 32), jnp.int32)],
        compiler_params=params(4),
        name="make_plan",
    )(owner, slot)


def cut(left_ref, right_ref, slot, out_ref, base):
    for index in range(out_ref.shape[0]):
        row, column = row_piece(index)
        rows = pl.ds(row, TILE)
        out_ref[index, base : base + TILE] = left_ref[slot, rows, column : column + LANES]
        out_ref[index, base + TILE : base + ROWS] = left_ref[
            slot, rows, column + LANES : column + 2 * LANES
        ]
        out_ref[index, base + ROWS : base + 2 * ROWS] = right_ref[
            slot, ROWS * index : ROWS * (index + 1)
        ]


def pack_kernel(
    place_ref, owner_hbm, slot_hbm, left_hbm, right_hbm, spare_hbm, *scratch
):
    owner_ref, slot_ref, left_ref, right_ref, spare_ref, sems = scratch
    spares = left_ref.shape[0]
    roots = []
    for spare in range(spares):
        pair = (
            pltpu.make_async_copy(left_hbm.at[spare + 1], left_ref.at[spare], sems.at[0, spare]),
            pltpu.make_async_copy(right_hbm.at[spare + 1], right_ref.at[spare], sems.at[1, spare]),
        )
        roots.append(pair)
    names = (
        pltpu.make_async_copy(owner_hbm, owner_ref, sems.at[2, 0]),
        pltpu.make_async_copy(slot_hbm, slot_ref, sems.at[2, 1]),
    )
    for copy in names + roots[1] + roots[0]:
        copy.start()
    for copy in names:
        copy.wait()

    def look(index, found):
        own = owner_ref[index] == place_ref[1]
        return found + (own & (slot_ref[index] < spares)).astype(jnp.int32)

    found = lax.fori_loop(0, owner_ref.shape[0], look, jnp.int32(0), unroll=4)
    second = jnp.where(found == spares, 0, 1)
    for copy in roots[1]:
        copy.wait()
    writes = []
    for spare in (1, 0):
        if spare == 0:
            for copy in roots[0]:
                copy.wait()
        cut(left_ref, right_ref, 1 if spare else second, spare_ref, 2 * ROWS * spare)
        part = (slice(None), pl.ds(2 * ROWS * spare, 2 * ROWS))
        copy = pltpu.make_async_copy(spare_ref.at[part], spare_hbm.at[part], sems.at[3, spare])
        copy.start()
        writes.append(copy)
    for copy in writes:
        copy.wait()


def pack(place, owner, slot, left, right, pieces):
    hbm = pl.BlockSpec(memory_space=pltpu.HBM)
    spares = left.shape[0] - 1
    shape = (pieces, spares * 2 * ROWS, LANES)
    return pl.pallas_call(
        pack_kernel,
        in_specs=[pl.BlockSpec(memory_space=pltpu.SMEM)] + [hbm] * 4,
        out_specs=hbm,
        out_shape=pltpu.HBM(shape, BF16),
        scratch_shapes=[
            pltpu.SMEM(owner.shape, jnp.int32),
            pltpu.SMEM(slot.shape, jnp.int32),
            pltpu.VMEM((spares,) + left.shape[1:], BF16),
            pltpu.VMEM((spares,) + right.shape[1:], BF16),
            pltpu.VMEM(shape, BF16),
            pltpu.SemaphoreType.DMA((4, 2)),
        ],
        compiler_params=params(8),
        name="pack",
    )(place, *in_hbm(owner, slot, left, right))


def keep_kernel(place_ref, plan_ref, left_hbm, right_hbm, kept_ref, left_ref, right_ref, sems):
    slots = left_hbm.shape[0]
    first = jnp.int32(slots - 1)
    for slot in reversed(range(slots - 1)):
        first = jnp.where(plan_ref[SOURCE + place_ref[1] * slots + slot] >= 0, slot, first)
    copies = (
        pltpu.make_async_copy(left_hbm.at[first], left_ref.at[0], sems.at[0]),
        pltpu.make_async_copy(right_hbm.at[first], right_ref.at[0], sems.at[1]),
    )
    for copy in copies:
        copy.start()
    for copy in copies:
        copy.wait()
    cut(left_ref, right_ref, 0, kept_ref, 0)


def keep(place, plan, left, right, pieces):
    smem = pl.BlockSpec(memory_space=pltpu.SMEM)
    hbm = pl.BlockSpec(memory_space=pltpu.HBM)
    return pl.pallas_call(
        keep_kernel,
        in_specs=[smem, smem, hbm, hbm],
        out_specs=pl.BlockSpec(memory_space=pltpu.VMEM),
        out_shape=jax.ShapeDtypeStruct((pieces, 2 * ROWS, LANES), BF16),
        scratch_shapes=[
            pltpu.VMEM((1,) + left.shape[1:], BF16),
            pltpu.VMEM((1,) + right.shape[1:], BF16),
            pltpu.SemaphoreType.DMA((2,)),
        ],
        compiler_params=params(8),
        name="keep",
    )(place, plan, *in_hbm(left, right))


def route_kernel(plan_ref, arrived_ref, out_hbm, sems):
    copies = []
    for home in range(out_hbm.shape[0]):
        origin = jnp.maximum(plan_ref[HOME_ORIGIN + home], 0)
        start = pl.multiple_of(lax.rem(origin, 2) * (2 * ROWS), 2 * ROWS)
        source = arrived_ref.at[lax.div(origin, 2), pl.ds(start, 2 * ROWS)]
        copies.append(pltpu.make_async_copy(source, out_hbm.at[home], sems.at[home]))
        copies[-1].start()
    for copy in copies:
        copy.wait()


def route(plan, arrived):
    homes = arrived.shape[0]
    return pl.pallas_call(
        route_kernel,
        in_specs=[
            pl.BlockSpec(memory_space=pltpu.SMEM),
            pl.BlockSpec(memory_space=pltpu.VMEM),
        ],
        out_specs=pl.BlockSpec(memory_space=pltpu.HBM),
        out_shape=pltpu.HBM((homes, 2 * ROWS, LANES), BF16),
        scratch_shapes=[pltpu.SemaphoreType.DMA((homes,))],
        compiler_params=params(8),
        name="route",
    )(plan, arrived)


def pick_kernel(place_ref, plan_ref, kept_ref, roots_ref, left_ref, both_hbm, sem):
    own = plan_ref[HOME_ORIGIN + place_ref[1]] < 0

    def take(source_ref):
        copy = pltpu.make_async_copy(source_ref, both_hbm, sem)
        copy.start()
        left_ref[...] = source_ref[:, :ROWS]
        copy.wait()

    @pl.when(own)
    def _():
        take(kept_ref)

    @pl.when(jnp.logical_not(own))
    def _():
        take(roots_ref)


def pick(place, plan, kept, roots):
    smem = pl.BlockSpec(memory_space=pltpu.SMEM)
    vmem = pl.BlockSpec(memory_space=pltpu.VMEM)
    return pl.pallas_call(
        pick_kernel,
        in_specs=[smem, smem, vmem, vmem],
        out_specs=[vmem, pl.BlockSpec(memory_space=pltpu.HBM)],
        out_shape=[
            jax.ShapeDtypeStruct((kept.shape[0], ROWS, LANES), BF16),
            pltpu.HBM(kept.shape, BF16),
        ],
        scratch_shapes=[pltpu.SemaphoreType.DMA],
        compiler_params=params(8),
        name="pick",
    )(place, plan, kept, roots)


def gather_kernel(plan_ref, gradient_ref, out_ref):
    for home in range(out_ref.shape[0]):
        out_ref[home] = gradient_ref[plan_ref[HOME_BLOCK + home]]


def gather(plan, gradient):
    return pl.pallas_call(
        gather_kernel,
        in_specs=[
            pl.BlockSpec(memory_space=pltpu.SMEM),
            pl.BlockSpec(memory_space=pltpu.VMEM),
        ],
        out_shape=jax.ShapeDtypeStruct(gradient.shape, BF16),
        compiler_params=params(8),
        name="gather",
    )(plan, gradient)


def block_kernel(rep_ref, block_hbm, both_hbm, *refs):
    shares, (out_ref, own_ref, block_ref, both_ref, left_ref, sems) = refs[:-6], refs[-6:]
    pieces, rows, order = block_ref.shape
    width = LANES
    replicas = order // width
    rep = rep_ref[0]
    half = shares[6].shape[0]
    roots = pltpu.make_async_copy(both_hbm, both_ref, sems.at[0])
    roots.start()
    parts = 4
    blocks = []
    for part in range(parts):
        lines = pl.ds(part * (pieces // parts), pieces // parts)
        copy = pltpu.make_async_copy(
            block_hbm.at[lines], block_ref.at[lines], sems.at[1 + part]
        )
        copy.start()
        blocks.append(copy)

    def place(index, share, start):
        row, column = row_piece(index)
        lines = pl.ds(pl.multiple_of(start + row, TILE), TILE)
        left_ref[lines, column : column + width] = share[:TILE]
        left_ref[lines, column + width : column + 2 * width] = share[TILE:]

    for share, distance in zip(shares[:6], DISTANCES[1:]):
        start = lax.rem(rep - distance + replicas, replicas) * width
        for index in range(pieces):
            place(index, share[index], start)
    start = lax.rem(rep + replicas // 2, replicas) * width
    for index in range(pieces):
        share = shares[6][index] if index < half else shares[7][index - half]
        place(index, share, start)
    roots.wait()
    for index in range(pieces):
        place(index, both_ref[index, :ROWS], rep * width)

    right_root = both_ref[:, ROWS:].reshape(order, width)
    rooted = []
    for part, copy in enumerate(blocks):
        copy.wait()
        lines = block_ref[part * (pieces // parts) : (part + 1) * (pieces // parts)]
        rooted.append(
            jnp.dot(
                lines.reshape(order // parts, order), right_root, preferred_element_type=F32
            ).astype(BF16)
        )
    rooted = jnp.concatenate(rooted, axis=0)
    precond = jnp.dot(left_ref[...], rooted, preferred_element_type=F32)
    out_ref[:, :ROWS, :] = precond.astype(BF16).reshape(pieces, rows, width)

    block = block_ref[...].reshape(order, order)
    columns = pl.multiple_of(rep * width, width)
    own_columns = block_ref[:, :, pl.ds(columns, width)].reshape(order, width)
    own_rows = block_ref[pl.ds(rep * (width // rows), width // rows)].reshape(width, order)
    left = lax.dot_general(
        own_rows, block, (((1,), (1,)), ((), ())), preferred_element_type=F32
    ).astype(BF16)
    for index in range(pieces):
        row, column = row_piece(index)
        for at, first in enumerate((column, column + width)):
            tile = left[row : row + TILE, first : first + width]
            base = ROWS + at * TILE
            out_ref[index, base : base + TILE] = tile
            own_ref[index, at * TILE : (at + 1) * TILE] = tile
    right = jnp.dot(own_columns.T, block, preferred_element_type=F32).T
    right = right.astype(BF16).reshape(pieces, rows, width)
    out_ref[:, 2 * ROWS : 3 * ROWS, :] = right
    own_ref[:, ROWS:, :] = right

    own = own_columns.astype(F32)
    lane = lax.broadcasted_iota(jnp.int32, (TILE, width), 1)
    total = jnp.zeros((TILE, width), F32)
    values = split_three(jnp.sum(precond * precond, keepdims=True))
    values += split_three(jnp.sum(own * own, keepdims=True))
    for index, value in enumerate(values):
        total = jnp.where(lane == index, value, total)
    out_ref[:, 3 * ROWS :, :] = jnp.broadcast_to(total.astype(BF16), (pieces, TILE, width))


def block_shares(rep, block, both, shares):
    pieces, _, order = block.shape
    vmem = pl.BlockSpec(memory_space=pltpu.VMEM)
    hbm = pl.BlockSpec(memory_space=pltpu.HBM)
    return pl.pallas_call(
        block_kernel,
        in_specs=[pl.BlockSpec(memory_space=pltpu.SMEM), hbm, hbm] + [vmem] * len(shares),
        out_specs=[vmem, vmem],
        out_shape=[
            jax.ShapeDtypeStruct((pieces, 3 * ROWS + TILE, LANES), BF16),
            jax.ShapeDtypeStruct((pieces, 2 * ROWS, LANES), BF16),
        ],
        scratch_shapes=[
            pltpu.VMEM(block.shape, BF16),
            pltpu.VMEM(both.shape, BF16),
            pltpu.VMEM((order, order), BF16),
            pltpu.SemaphoreType.DMA((5,)),
        ],
        compiler_params=params(20),
        cost_estimate=cost(8 * order * order * LANES, 6 * order * order),
        name="block_shares",
    )(rep, *in_hbm(block, both), *shares)


def named_kernel(arrived_ref, update_ref):
    count = arrived_ref.shape[0]
    line = lax.broadcasted_iota(jnp.int32, (ROWS, LANES), 0)
    sums = jnp.zeros((ROWS, LANES), F32)
    for index in range(count):
        update_ref[index] = arrived_ref[index, :ROWS, :]
        tail = arrived_ref[index, 3 * ROWS :, :].astype(F32)
        sums = jnp.where(line == index, jnp.concatenate([tail, tail], axis=0), sums)
    update_ref[count] = sums.astype(BF16)


def named(arrived):
    return pl.pallas_call(
        named_kernel,
        out_shape=jax.ShapeDtypeStruct((arrived.shape[0] + 1, ROWS, LANES), BF16),
        compiler_params=params(8),
        name="named",
    )(arrived)


def deal_kernel(plan_ref, arrived_ref, products_ref):
    spares = products_ref.shape[1] // (2 * ROWS)
    for owner in range(products_ref.shape[0]):
        for spare in range(spares):
            home = plan_ref[SPARE_HOME + owner * spares + spare]
            products_ref[owner, 2 * ROWS * spare : 2 * ROWS * (spare + 1)] = arrived_ref[
                home, ROWS : 3 * ROWS, :
            ]


def deal(plan, arrived, spares):
    shape = (arrived.shape[0], spares * 2 * ROWS, LANES)
    return pl.pallas_call(
        deal_kernel,
        in_specs=[
            pl.BlockSpec(memory_space=pltpu.SMEM),
            pl.BlockSpec(memory_space=pltpu.VMEM),
        ],
        out_shape=jax.ShapeDtypeStruct(shape, BF16),
        compiler_params=params(8),
        name="deal",
    )(plan, arrived)


def finish_kernel(rep_ref, plan_ref, *refs):
    shares, (out_hbm, out_ref, scale_ref, sems) = refs[:-4], refs[-4:]
    count, rows, order = out_ref.shape
    width = LANES
    half = shares[7].shape[0]
    replicas = order // width
    sums = shares[8][count - half].astype(F32)
    for share in shares[:7]:
        sums += share[count].astype(F32)
    lane = lax.broadcasted_iota(jnp.int32, (rows, width), 1)
    pre = jnp.sum(jnp.where(lane < 3, sums, 0.0), axis=1, keepdims=True)
    grad = jnp.sum(jnp.where((lane >= 3) & (lane < 6), sums, 0.0), axis=1, keepdims=True)
    scale = jnp.sqrt(grad) / jnp.sqrt(pre + epsilon)
    scale_ref[...] = jnp.broadcast_to(scale, (rows, width))

    def place(index, share, column):
        factor = scale_ref[pl.ds(index, 1), :]
        start = pl.multiple_of(column * width, width)
        out_ref[index, :, pl.ds(start, width)] = (share.astype(F32) * factor).astype(BF16)

    copies = []
    for index in range(count):
        for share, distance in zip(shares[:7], DISTANCES):
            place(index, share[index], lax.rem(rep_ref[0] - distance + replicas, replicas))
        far = lax.rem(rep_ref[0] + replicas // 2, replicas)
        share = shares[7][index] if index < half else shares[8][index - half]
        place(index, share, far)
        block = plan_ref[HOME_BLOCK + index]
        copies.append(pltpu.make_async_copy(out_ref.at[index], out_hbm.at[block], sems.at[index]))
        copies[-1].start()
    for copy in copies:
        copy.wait()


def finish(rep, plan, shares, count, rows, order):
    shape = (count, rows, order)
    return pl.pallas_call(
        finish_kernel,
        in_specs=[pl.BlockSpec(memory_space=pltpu.SMEM)] * 2
        + [pl.BlockSpec(memory_space=pltpu.VMEM)] * len(shares),
        out_specs=pl.BlockSpec(memory_space=pltpu.HBM),
        out_shape=jax.ShapeDtypeStruct(shape, BF16),
        scratch_shapes=[
            pltpu.VMEM(shape, BF16),
            pltpu.VMEM((count, LANES), F32),
            pltpu.SemaphoreType.DMA((count,)),
        ],
        compiler_params=params(12),
        name="finish",
    )(rep, plan, *shares)


def factor_kernel(
    plan_ref,
    place_ref,
    own_ref,
    products_ref,
    left_hbm,
    right_hbm,
    left_out,
    right_out,
    *scratch,
):
    left_ref, right_ref, left_new, right_new, held_ref, sems = scratch
    pieces = products_ref.shape[0]
    slots, order, width = right_ref.shape
    reads, writes = [], []
    for slot in range(slots):
        reads.append(
            (
                pltpu.make_async_copy(left_hbm.at[0, slot], left_ref.at[slot], sems.at[0, slot]),
                pltpu.make_async_copy(right_hbm.at[0, slot], right_ref.at[slot], sems.at[1, slot]),
            )
        )
        writes.append(
            (
                pltpu.make_async_copy(left_new.at[slot], left_out.at[0, slot], sems.at[2, slot]),
                pltpu.make_async_copy(right_new.at[slot], right_out.at[0, slot], sems.at[3, slot]),
            )
        )
        for copy in reads[slot]:
            copy.start()
    held_ref[0] = own_ref[...]
    for spare in range(slots - 1):
        held_ref[spare + 1] = products_ref[:, 2 * ROWS * spare : 2 * ROWS * (spare + 1)]
    which = jnp.int32(0)
    for slot in range(slots):
        named = plan_ref[SOURCE + place_ref[1] * slots + slot] >= 0
        weight = jnp.where(named, 1.0 - decay_rate, 0.0).astype(F32)
        for copy in reads[slot]:
            copy.wait()
        at_most = jnp.minimum(which, slots - 1)
        for index in range(pieces):
            row, column = row_piece(index)
            piece = held_ref[at_most, index].astype(F32)
            for part in range(2):
                at = (slot, pl.ds(row, TILE), pl.ds(column + part * width, width))
                product = piece[part * TILE : (part + 1) * TILE]
                left_new[at] = decay_rate * left_ref[at] + weight * product
            at = (slot, pl.ds(ROWS * index, ROWS))
            right_new[at] = decay_rate * right_ref[at] + weight * piece[ROWS:]
        for copy in writes[slot]:
            copy.start()
        which += named.astype(jnp.int32)
    for slot in range(slots):
        for copy in writes[slot]:
            copy.wait()


def factors(plan, place, own, products, left, right):
    slots, width, order = left.shape[1:]
    hbm = pl.BlockSpec(memory_space=pltpu.HBM)
    return pl.pallas_call(
        factor_kernel,
        in_specs=[
            pl.BlockSpec(memory_space=pltpu.SMEM),
            pl.BlockSpec(memory_space=pltpu.SMEM),
            pl.BlockSpec(memory_space=pltpu.VMEM),
            pl.BlockSpec(memory_space=pltpu.VMEM),
            hbm,
            hbm,
        ],
        out_specs=[hbm, hbm],
        out_shape=[
            jax.ShapeDtypeStruct(left.shape, F32),
            jax.ShapeDtypeStruct(right.shape, F32),
        ],
        scratch_shapes=[
            pltpu.VMEM((slots, width, order), F32),
            pltpu.VMEM((slots, order, width), F32),
            pltpu.VMEM((slots, width, order), F32),
            pltpu.VMEM((slots, order, width), F32),
            pltpu.VMEM((slots,) + own.shape, BF16),
            pltpu.SemaphoreType.DMA((4, slots)),
        ],
        compiler_params=params(16),
        cost_estimate=cost(2 * slots * order * order, 5 * slots * order * order),
        name="factors",
    )(plan, place, own, products, *in_hbm(left, right))


def ring_gather(share, axis, before_last=None):
    size = lax.axis_size(axis)
    half = share.shape[0] // 2

    def shift(value, by):
        return lax.ppermute(value, axis, [(i, (i + by) % size) for i in range(size)])

    down = [share, shift(share, -1)]
    up = [share, *anchor(shift(share, 1))]
    for _ in range(size // 2 - 2):
        down.append(shift(down[-1], -1))
        up.append(shift(up[-1], 1))
    if before_last is not None:
        up[-1], down[-1], before_last = lax.optimization_barrier((up[-1], down[-1], before_last))
    far_down = shift(down[-1][half:], -1)
    far_up = shift(up[-1][:half], 1)
    return up + down[1:] + [far_up, far_down], before_last


def anchor_kernel(*refs):
    del refs


def anchor(*arrays):
    hbm = pl.BlockSpec(memory_space=pl.ANY)
    return pl.pallas_call(
        anchor_kernel,
        in_specs=[hbm] * len(arrays),
        out_specs=[hbm] * len(arrays),
        out_shape=[jax.ShapeDtypeStruct(array.shape, array.dtype) for array in arrays],
        input_output_aliases={index: index for index in range(len(arrays))},
        compiler_params=params(4),
        cost_estimate=cost(1 << 38, 1 << 10),
        name="anchor",
    )(*arrays)


def exchange(value):
    return lax.all_to_all(value, "fsdp", split_axis=0, concat_axis=0, tiled=True)


def local(gradient, block_owner, block_slot, left_state, right_state, left_root, right_root):
    owners = lax.axis_size("fsdp")
    count, rows, order = gradient.shape
    slots = left_state.shape[1]
    rep = lax.axis_index("rep").astype(jnp.int32).reshape(1)
    place = jnp.concatenate([rep, lax.axis_index("fsdp").astype(jnp.int32).reshape(1)])
    plan = make_plan(block_owner, block_slot)

    spare = pack(place, block_owner, block_slot, left_root[0], right_root[0], owners)
    kept = keep(place, plan, left_root[0], right_root[0], owners)
    roots = exchange(route(plan, exchange(spare)))
    left, both = pick(place, plan, kept, roots)
    packed, left = lax.optimization_barrier((gather(plan, gradient), left))
    left_shares, _ = ring_gather(left, "rep")
    outgoing, own = block_shares(rep, exchange(packed), both, left_shares[1:])

    arrived = exchange(outgoing)
    products = exchange(deal(plan, arrived, slots - 1))
    outputs = factors(plan, place, own, products, left_state, right_state)
    shares, outputs = ring_gather(named(arrived), "rep", outputs)
    left_factor, right_factor = outputs
    update = finish(rep, plan, shares, count, rows, order)
    return (update, left_factor, right_factor)


def solution(mesh):
    in_specs = (
        P(None, "fsdp", None),
        P(),
        P(),
        P("fsdp", None, "rep", None),
        P("fsdp", None, None, "rep"),
        P("fsdp", None, "rep", None),
        P("fsdp", None, None, "rep"),
    )
    out_specs = (P(None, "fsdp", None), P("fsdp", None, "rep", None), P("fsdp", None, None, "rep"))
    return jax.shard_map(local, mesh=mesh, in_specs=in_specs, out_specs=out_specs, check_vma=False)
```

time: 180 us -> 154 us (0.86)
  blocking collectives: 43.8 us -> 22 us
  local copies, waits for them, and re-layouts: 21.5 us -> 0.05 us
  Pallas kernels: 13.5 us -> 26.7 us
  starting transfers between devices: 45.7 us -> 50.3 us
  waiting for transfers between devices: 54 us -> 51.8 us
    all_to_all x2 -> x1, blocking collectives: 43.8 us -> 22 us  [exchange(): lax.all_to_all(value, 'fsdp', split_axis=0, concat_axis=0, tiled=True)]
    unnamed x54 -> x6, local copies, waits for them, and re-layouts: 18.1 us -> 0.01 us
    pallas_call x4 -> x11, Pallas kernels: 5.47 us -> 18.7 us  [the longest x1 4.26 us: factors(): pl.pallas_call(factor_kernel, in_specs=[pl.BlockSpec(memory_space=pltpu.S...]
    ppermute x16, waiting for transfers between devices: 39.8 us -> 29 us  [shift(): lax.ppermute(value, axis, [(i, (i + by) % size) for i in range(size)])]
    all_to_all x3 -> x4, waiting for transfers between devices: 14.1 us -> 22.7 us  [exchange(): lax.all_to_all(value, 'fsdp', split_axis=0, concat_axis=0, tiled=True)]
    all_to_all x3 -> x4, starting transfers between devices: 17.7 us -> 24.1 us  [exchange(): lax.all_to_all(value, 'fsdp', split_axis=0, concat_axis=0, tiled=True)]
  transfers between devices with their start and end apart: 19 -> 20, of which waited for: 10 -> 11; matrix products, arithmetic and copies ran while one was open for 2% -> 0% of each run, Pallas kernels for 2% -> 9%
where the time goes in v3:
time: 154 us; the launch traced here: 152 us
  waiting for transfers between devices  51.8 us (34%)
  starting transfers between devices  50.3 us (33%)
  Pallas kernels  26.7 us (17%)
  blocking collectives  22 us (14%)
    ppermute x16, waiting for transfers between devices, shift(): lax.ppermute(value, axis, [(i, (i + by) % size) for i in range(size)])  29 us
    ppermute x16, starting transfers between devices, shift(): lax.ppermute(value, axis, [(i, (i + by) % size) for i in range(size)])  26.3 us
    all_to_all x4, starting transfers between devices, exchange(): lax.all_to_all(value, 'fsdp', split_axis=0, concat_axis=0, tiled=True)  24.1 us
    all_to_all x4, waiting for transfers between devices, exchange(): lax.all_to_all(value, 'fsdp', split_axis=0, concat_axis=0, tiled=True)  22.7 us
    all_to_all x1, blocking collectives, exchange(): lax.all_to_all(value, 'fsdp', split_axis=0, concat_axis=0, tiled=True)  22 us
    pallas_call x1, Pallas kernels, block_shares(): pl.pallas_call(block_kernel, in_specs=[pl.BlockSpec(memory_space=pltpu.SM...  5.22 us
    pallas_call x1, Pallas kernels, factors(): pl.pallas_call(factor_kernel, in_specs=[pl.BlockSpec(memory_space=pltpu.S...  4.26 us
    pallas_call x1, Pallas kernels, make_plan(): pl.pallas_call(plan_kernel, in_specs=[smem, smem], out_specs=smem, out_sh...  3.51 us
  transfers between devices with their start and end apart: 20, of which 11 were waited for; matrix products, arithmetic and copies ran while one was open for 0% of the time, Pallas kernels for 9%

profile of v3, /device:TPU:8, one launch (start us, length us, event | category | flops | bytes accessed | tf_op | source)
XLA Modules:
  0.0 151.9 jit_solution(14285757898195814375)
XLA Ops:
  0.6 0.1 pad_add_fusion.place_ref
  0.7 0.0 copy-start.1
  0.7 0.0 copy-start.2
  0.7 2.7 %pack.1 = bf16[32,128,128]{2,1,0:T(8,128)(2,1)} custom-call(s32[2]{0:T(128)S(1)} %pad_add_fusion.place_ref, s32[32]{0:T(128)} %owner_hbm.1, s32[32]{0:T(128)} %slot_hbm.1, bf16[3,128,1024]{2,1,0:T(8,128)(2,1)} %bitcast.4, bf16[3,1024,128]{2,1,0:T(8,128)(2,1)} %bitcast.6), custom_call_target="tpu_custom_call" | custom-call | tf_op jit(solution)/shard_map/pack/pallas_call | solution.py:185
  3.4 7.5 %all-to-all-start = ((bf16[32,128,128]{2,1,0:T(8,128)(2,1)}), bf16[32,128,128]{2,1,0:T(8,128)(2,1)S(1)}, u32[]{:S(2)}, u32[]{:S(2)}) async-start(bf16[32,128,128]{2,1,0:T(8,128)(2,1)} %pack.1), calls=%async_computation | async-start | bytes 2097152 | tf_op jit(solution)/shard_map/all_to_all | solution.py:645
  10.9 0.0 copy-done.1
  10.9 0.0 copy-done.2
  11.0 3.5 %make_plan.1.plan_ref = s32[256]{0:T(256)S(1)} custom-call(s32[32]{0:T(128)S(1)} %copy-done.1, s32[32]{0:T(128)S(1)} %copy-done.2), custom_call_target="tpu_custom_call" | custom-call | tf_op jit(solution)/shard_map/make_plan/pallas_call | solution.py:114
  14.5 0.0 copy-start
  14.5 12.0 %all-to-all-done.arrived_ref = bf16[32,128,128]{2,1,0:T(8,128)(2,1)S(1)} async-done(((bf16[32,128,128]{2,1,0:T(8,128)(2,1)}), bf16[32,128,128]{2,1,0:T(8,128)(2,1)S(1)}, u32[]{:S(2)}, u32[]{:S(2)}) %all-to-all-start) | async-done | bytes 1048608 | tf_op jit(solution)/shard_map/all_to_all | solution.py:645
  26.5 1.6 %route.1 = bf16[32,64,128]{2,1,0:T(8,128)(2,1)} custom-call(s32[256]{0:T(256)S(1)} %make_plan.1.plan_ref, bf16[32,128,128]{2,1,0:T(8,128)(2,1)S(1)} %all-to-all-done.arrived_ref), custom_call_target="tpu_custom_call" | custom-call | tf_op jit(solution)/shard_map/route/pallas_call | solution.py:251
  28.1 5.3 %all-to-all-start.1 = ((bf16[32,64,128]{2,1,0:T(8,128)(2,1)}), bf16[32,64,128]{2,1,0:T(8,128)(2,1)S(1)}, u32[]{:S(2)}, u32[]{:S(2)}) async-start(bf16[32,64,128]{2,1,0:T(8,128)(2,1)} %route.1), calls=%async_computation.1 | async-start | bytes 1048576 | tf_op jit(solution)/shard_map/all_to_all | solution.py:645
  33.4 1.7 %keep.1.kept_ref = bf16[32,64,128]{2,1,0:T(8,128)(2,1)S(1)} custom-call(s32[2]{0:T(128)S(1)} %pad_add_fusion.place_ref, s32[256]{0:T(256)S(1)} %make_plan.1.plan_ref, bf16[3,128,1024]{2,1,0:T(8,128)(2,1)} %bitcast.5, bf16[3,1024,128]{2,1,0:T(8,128)(2,1)} %bitcast.7), custom_call_target="tpu_custom_call" | custom-call | tf_op jit(solution)/shard_map/keep/pallas_call | solution.py:222
  35.1 0.0 copy-done
  35.1 2.0 %gather.1 = bf16[32,32,1024]{2,1,0:T(8,128)(2,1)} custom-call(s32[256]{0:T(256)S(1)} %make_plan.1.plan_ref, bf16[32,32,1024]{2,1,0:T(8,128)(2,1)S(1)} %copy-done), custom_call_target="tpu_custom_call" | custom-call | tf_op jit(solution)/shard_map/gather/pallas_call | solution.py:306
  37.1 6.5 %all-to-all-done.1.roots_ref = bf16[32,64,128]{2,1,0:T(8,128)(2,1)S(1)} async-done(((bf16[32,64,128]{2,1,0:T(8,128)(2,1)}), bf16[32,64,128]{2,1,0:T(8,128)(2,1)S(1)}, u32[]{:S(2)}, u32[]{:S(2)}) %all-to-all-start.1) | async-done | bytes 524320 | tf_op jit(solution)/shard_map/all_to_all | solution.py:645
  43.6 1.4 pick.1
  45.0 5.9 %collective-permute-start.3 = (bf16[32,32,128]{2,1,0:T(8,128)(2,1)S(1)}, bf16[32,32,128]{2,1,0:T(8,128)(2,1)}, u32[]{:S(2)}, u32[]{:S(2)}) collective-permute-start(bf16[32,32,128]{2,1,0:T(8,128)(2,1)S(1)} %get-tuple-element.18), channel_id=1, source_target_pairs={{0,7},{1,0},{2,1},{3,2},{4,3},{5,4},{6,5},{7,6},{8,15},{9,8},{10,9... | collective-permute-start | bytes 786440 | tf_op jit(solution)/shard_map/ppermute | solution.py:612
  50.9 0.0 collective-permute-start
  50.9 5.6 %all-to-all-start.2 = ((bf16[32,32,1024]{2,1,0:T(8,128)(2,1)}), bf16[32,32,1024]{2,1,0:T(8,128)(2,1)}, u32[]{:S(2)}, u32[]{:S(2)}) async-start(bf16[32,32,1024]{2,1,0:T(8,128)(2,1)} %gather.1), calls=%async_computation.2 | async-start | bytes 4194304 | tf_op jit(solution)/shard_map/all_to_all | solution.py:645
  56.5 0.4 collective-permute-done.3.refs_3_
  56.9 3.8 %collective-permute-start.4 = (bf16[32,32,128]{2,1,0:T(8,128)(2,1)}, bf16[32,32,128]{2,1,0:T(8,128)(2,1)}, u32[]{:S(2)}, u32[]{:S(2)}) collective-permute-start(bf16[32,32,128]{2,1,0:T(8,128)(2,1)} %collective-permute-done.3.refs_3_), channel_id=1, source_target_pairs={{0,7},{1,0},{2,1},{3,2},{4,3},{5,4},{6,5},{7,6},{8,15},{9,8},{10,9... | collective-permute-start | bytes 786440 | tf_op jit(solution)/shard_map/ppermute | solution.py:612
  60.7 0.0 collective-permute-done.refs_0_
  60.7 0.0 collective-permute-start.1
  60.7 5.5 %collective-permute-done.4.refs_4_ = bf16[32,32,128]{2,1,0:T(8,128)(2,1)} collective-permute-done((bf16[32,32,128]{2,1,0:T(8,128)(2,1)}, bf16[32,32,128]{2,1,0:T(8,128)(2,1)}, u32[]{:S(2)}, u32[]{:S(2)}) %collective-permute-start.4) | collective-permute-done | bytes 262176 | tf_op jit(solution)/shard_map/ppermute | solution.py:612
  66.3 3.7 %collective-permute-start.5 = (bf16[32,32,128]{2,1,0:T(8,128)(2,1)}, bf16[32,32,128]{2,1,0:T(8,128)(2,1)S(1)}, u32[]{:S(2)}, u32[]{:S(2)}) collective-permute-start(bf16[32,32,128]{2,1,0:T(8,128)(2,1)} %collective-permute-done.4.refs_4_), channel_id=1, source_target_pairs={{0,7},{1,0},{2,1},{3,2},{4,3},{5,4},{6,5},{7,6},{8,15},{9,8},{10,9... | collective-permute-start | bytes 786440 | tf_op jit(solution)/shard_map/ppermute | solution.py:612
  70.0 0.0 collective-permute-done.1.refs_1_
  70.0 0.0 collective-permute-start.2
  70.0 4.6 %collective-permute-done.5.refs_5_ = bf16[32,32,128]{2,1,0:T(8,128)(2,1)S(1)} collective-permute-done((bf16[32,32,128]{2,1,0:T(8,128)(2,1)}, bf16[32,32,128]{2,1,0:T(8,128)(2,1)S(1)}, u32[]{:S(2)}, u32[]{:S(2)}) %collective-permute-start.5) | collective-permute-done | bytes 262176 | tf_op jit(solution)/shard_map/ppermute | solution.py:612
  74.6 3.7 %collective-permute-start.7 = (bf16[16,32,128]{2,1,0:T(8,128)(2,1)S(1)}, bf16[16,32,128]{2,1,0:T(8,128)(2,1)S(1)}, u32[]{:S(2)}, u32[]{:S(2)}) collective-permute-start(bf16[16,32,128]{2,1,0:T(8,128)(2,1)S(1)} %slice.17), channel_id=1, source_target_pairs={{0,7},{1,0},{2,1},{3,2},{4,3},{5,4},{6,5},{7,6},{8,15},{9,8},{10,9... | collective-permute-start | bytes 393224 | tf_op jit(solution)/shard_map/ppermute | solution.py:612
  78.3 0.0 collective-permute-done.2.refs_2_
  78.3 0.1 collective-permute-start.6
  78.4 2.4 %collective-permute-done.7.refs_7_ = bf16[16,32,128]{2,1,0:T(8,128)(2,1)S(1)} collective-permute-done((bf16[16,32,128]{2,1,0:T(8,128)(2,1)S(1)}, bf16[16,32,128]{2,1,0:T(8,128)(2,1)S(1)}, u32[]{:S(2)}, u32[]{:S(2)}) %collective-permute-start.7) | collective-permute-done | bytes 131104 | tf_op jit(solution)/shard_map/ppermute | solution.py:612
  80.8 3.8 %collective-permute-done.6.refs_6_ = bf16[16,32,128]{2,1,0:T(8,128)(2,1)S(1)} collective-permute-done((bf16[16,32,128]{2,1,0:T(8,128)(2,1)S(1)}, bf16[16,32,128]{2,1,0:T(8,128)(2,1)S(1)}, u32[]{:S(2)}, u32[]{:S(2)}) %collective-permute-start.6) | collective-permute-done | bytes 131104 | tf_op jit(solution)/shard_map/ppermute | solution.py:612
  84.5 0.0 all-to-all-done.2.block_hbm
  84.5 5.2 %block_shares.1 = (bf16[32,112,128]{2,1,0:T(8,128)(2,1)S(1)}, bf16[32,64,128]{2,1,0:T(8,128)(2,1)S(1)}) custom-call(s32[1]{0:T(128)} %bitcast.rep_ref, bf16[32,32,1024]{2,1,0:T(8,128)(2,1)} %all-to-all-done.2.block_hbm, bf16[32,64,128]{2,1,0:T(8,128)(2,1)} %get-tuple-element.17.both_hbm, bf16[32,32,128]{2,1,0:T(8,128)(2,1)S(1)} %anchor.2.refs_0_, ...), custom_call_target="tpu_custom_call" | custom-call | flops 1073741824 | bytes 6291456 | tf_op jit(solution)/shard_map/block_shares/pallas_call | solution.py:402
  89.8 22.0 %all_to_all.25.arrived_ref = bf16[32,112,128]{2,1,0:T(8,128)(2,1)S(1)} all-to-all(bf16[32,112,128]{2,1,0:T(8,128)(2,1)S(1)} %get-tuple-element.19), channel_id=1, replica_groups=mesh['fsdp'=32,'rep'=8] {'fsdp'}, dimensions={0} | all-to-all | bytes 1835008 | tf_op jit(solution)/shard_map/all_to_all | solution.py:645
  111.8 0.3 collective-permute-start.11
  112.1 2.0 %collective-permute-start.8 = (bf16[33,32,128]{2,1,0:T(8,128)(2,1)S(1)}, bf16[33,32,128]{2,1,0:T(8,128)(2,1)S(1)}, u32[]{:S(2)}, u32[]{:S(2)}) collective-permute-start(bf16[33,32,128]{2,1,0:T(8,128)(2,1)S(1)} %named.1.refs_0_), channel_id=1, source_target_pairs={{0,1},{1,2},{2,3},{3,4},{4,5},{5,6},{6,7},{7,0},{8,9},{9,10},{10,1... | collective-permute-start | bytes 811016 | tf_op jit(solution)/shard_map/ppermute | solution.py:612
  114.1 1.6 %deal.1 = bf16[32,128,128]{2,1,0:T(8,128)(2,1)} custom-call(s32[256]{0:T(256)S(1)} %make_plan.1.plan_ref, bf16[32,112,128]{2,1,0:T(8,128)(2,1)S(1)} %all_to_all.25.arrived_ref), custom_call_target="tpu_custom_call" | custom-call | tf_op jit(solution)/shard_map/deal/pallas_call | solution.py:454
  115.7 5.6 %all-to-all-start.4 = ((bf16[32,128,128]{2,1,0:T(8,128)(2,1)}), bf16[32,128,128]{2,1,0:T(8,128)(2,1)}, u32[]{:S(2)}, u32[]{:S(2)}) async-start(bf16[32,128,128]{2,1,0:T(8,128)(2,1)} %deal.1), calls=%async_computation.4 | async-start | bytes 2097152 | tf_op jit(solution)/shard_map/all_to_all | solution.py:645
  121.3 0.0 collective-permute-done.11.refs_4_
  121.3 1.4 collective-permute-start.12
  122.7 0.0 collective-permute-done.8.refs_0_
  122.7 0.7 collective-permute-start.9
  123.4 6.8 %collective-permute-done.12.refs_5_ = bf16[33,32,128]{2,1,0:T(8,128)(2,1)} collective-permute-done((bf16[33,32,128]{2,1,0:T(8,128)(2,1)}, bf16[33,32,128]{2,1,0:T(8,128)(2,1)}, u32[]{:S(2)}, u32[]{:S(2)}) %collective-permute-start.12) | collective-permute-done | bytes 270368 | tf_op jit(solution)/shard_map/ppermute | solution.py:612
  130.2 2.5 %collective-permute-start.13 = (bf16[33,32,128]{2,1,0:T(8,128)(2,1)}, bf16[33,32,128]{2,1,0:T(8,128)(2,1)S(1)}, u32[]{:S(2)}, u32[]{:S(2)}) collective-permute-start(bf16[33,32,128]{2,1,0:T(8,128)(2,1)} %collective-permute-done.12.refs_5_), channel_id=1, source_target_pairs={{0,7},{1,0},{2,1},{3,2},{4,3},{5,4},{6,5},{7,6},{8,15},{9,8},{10,9... | collective-permute-start | bytes 811016 | tf_op jit(solution)/shard_map/ppermute | solution.py:612
  132.7 0.0 collective-permute-done.9.refs_2_
  132.7 0.0 collective-permute-start.10
  132.7 4.2 %all-to-all-done.4.products_ref = bf16[32,128,128]{2,1,0:T(8,128)(2,1)} async-done(((bf16[32,128,128]{2,1,0:T(8,128)(2,1)}), bf16[32,128,128]{2,1,0:T(8,128)(2,1)}, u32[]{:S(2)}, u32[]{:S(2)}) %all-to-all-start.4) | async-done | bytes 1048608 | tf_op jit(solution)/shard_map/all_to_all | solution.py:645
  137.0 4.3 %factors.1 = (f32[1,3,128,1024]{3,2,1,0:T(8,128)}, f32[1,3,1024,128]{3,2,1,0:T(8,128)}) custom-call(s32[256]{0:T(256)S(1)} %make_plan.1.plan_ref, s32[2]{0:T(128)S(1)} %pad_add_fusion.place_ref, bf16[32,64,128]{2,1,0:T(8,128)(2,1)S(1)} %get-tuple-element.20.own_ref, bf16[32,128,128]{2,1,0:T(8,128)(2,1)} %all-to-all-done.4.products_ref, ...), custom_call_target="tpu_custom_call" | custom-call | flops 6291456 | bytes 15728640 | tf_op jit(solution)/shard_map/factors/pallas_call | solution.py:578
  141.3 0.0 collective-permute-done.13.refs_6_
  141.3 0.1 collective-permute-done.10.refs_3_
  141.4 1.3 collective-permute-start.15
  142.7 0.9 collective-permute-start.14
  143.6 5.4 %collective-permute-done.14.refs_7_ = bf16[16,32,128]{2,1,0:T(8,128)(2,1)S(1)} collective-permute-done((bf16[16,32,128]{2,1,0:T(8,128)(2,1)S(1)}, bf16[16,32,128]{2,1,0:T(8,128)(2,1)S(1)}, u32[]{:S(2)}, u32[]{:S(2)}) %collective-permute-start.14) | collective-permute-done | bytes 131104 | tf_op jit(solution)/shard_map/ppermute | solution.py:612
  149.0 0.0 collective-permute-done.15.refs_8_
  149.0 2.7 %finish.1 = bf16[32,32,1024]{2,1,0:T(8,128)(2,1)} custom-call(s32[1]{0:T(128)} %bitcast.rep_ref, s32[256]{0:T(256)S(1)} %make_plan.1.plan_ref, bf16[33,32,128]{2,1,0:T(8,128)(2,1)S(1)} %named.1.refs_0_, bf16[33,32,128]{2,1,0:T(8,128)(2,1)S(1)} %anchor.3.refs_1_, bf16[33,32,128]{2,1,0:T(8,128)(2,1)S(1)} %collective-permute-done.9.refs_2_, ...), custom_call_target="tpu_custom_call" | custom-call | tf_op jit(solution)/shard_map/finish/pallas_call | solution.py:502
  (7 shorter events, 0.1 us)
Async XLA Ops:
  0.7 10.2 %copy-start.1 = (s32[32]{0:T(128)S(1)}, s32[32]{0:T(128)}, u32[]{:S(2)}) copy-start(s32[32]{0:T(128)} %owner_hbm.1) | copy-start | bytes 388
  0.7 10.2 %copy-start.2 = (s32[32]{0:T(128)S(1)}, s32[32]{0:T(128)}, u32[]{:S(2)}) copy-start(s32[32]{0:T(128)} %slot_hbm.1) | copy-start | bytes 388
  3.4 23.1 %all-to-all-start = ((bf16[32,128,128]{2,1,0:T(8,128)(2,1)}), bf16[32,128,128]{2,1,0:T(8,128)(2,1)S(1)}, u32[]{:S(2)}, u32[]{:S(2)}) async-start(bf16[32,128,128]{2,1,0:T(8,128)(2,1)} %pack.1), calls=%async_computation | async-start | bytes 2097152 | tf_op jit(solution)/shard_map/all_to_all | solution.py:645
  14.5 20.6 %copy-start = (bf16[32,32,1024]{2,1,0:T(8,128)(2,1)S(1)}, bf16[32,32,1024]{2,1,0:T(8,128)(2,1)}, u32[]{:S(2)}) copy-start(bf16[32,32,1024]{2,1,0:T(8,128)(2,1)} %gradient_ref.1) | copy-start | bytes 6291460
  28.1 15.5 %all-to-all-start.1 = ((bf16[32,64,128]{2,1,0:T(8,128)(2,1)}), bf16[32,64,128]{2,1,0:T(8,128)(2,1)S(1)}, u32[]{:S(2)}, u32[]{:S(2)}) async-start(bf16[32,64,128]{2,1,0:T(8,128)(2,1)} %route.1), calls=%async_computation.1 | async-start | bytes 1048576 | tf_op jit(solution)/shard_map/all_to_all | solution.py:645
  45.0 12.0 %collective-permute-start.3 = (bf16[32,32,128]{2,1,0:T(8,128)(2,1)S(1)}, bf16[32,32,128]{2,1,0:T(8,128)(2,1)}, u32[]{:S(2)}, u32[]{:S(2)}) collective-permute-start(bf16[32,32,128]{2,1,0:T(8,128)(2,1)S(1)} %get-tuple-element.18), channel_id=1, source_target_pairs={{0,7},{1,0},{2,1},{3,2},{4,3},{5,4},{6,5},{7,6},{8,15},{9,8},{10,9... | collective-permute-start | bytes 786440 | tf_op jit(solution)/shard_map/ppermute | solution.py:612
  50.9 9.8 %collective-permute-start = (bf16[32,32,128]{2,1,0:T(8,128)(2,1)S(1)}, bf16[32,32,128]{2,1,0:T(8,128)(2,1)S(1)}, u32[]{:S(2)}, u32[]{:S(2)}) collective-permute-start(bf16[32,32,128]{2,1,0:T(8,128)(2,1)S(1)} %get-tuple-element.18), channel_id=1, source_target_pairs={{0,1},{1,2},{2,3},{3,4},{4,5},{5,6},{6,7},{7,0},{8,9},{9,10},{10,1... | collective-permute-start | bytes 786440 | tf_op jit(solution)/shard_map/ppermute | solution.py:612
  50.9 33.6 %all-to-all-start.2 = ((bf16[32,32,1024]{2,1,0:T(8,128)(2,1)}), bf16[32,32,1024]{2,1,0:T(8,128)(2,1)}, u32[]{:S(2)}, u32[]{:S(2)}) async-start(bf16[32,32,1024]{2,1,0:T(8,128)(2,1)} %gather.1), calls=%async_computation.2 | async-start | bytes 4194304 | tf_op jit(solution)/shard_map/all_to_all | solution.py:645
  56.9 9.3 %collective-permute-start.4 = (bf16[32,32,128]{2,1,0:T(8,128)(2,1)}, bf16[32,32,128]{2,1,0:T(8,128)(2,1)}, u32[]{:S(2)}, u32[]{:S(2)}) collective-permute-start(bf16[32,32,128]{2,1,0:T(8,128)(2,1)} %collective-permute-done.3.refs_3_), channel_id=1, source_target_pairs={{0,7},{1,0},{2,1},{3,2},{4,3},{5,4},{6,5},{7,6},{8,15},{9,8},{10,9... | collective-permute-start | bytes 786440 | tf_op jit(solution)/shard_map/ppermute | solution.py:612
  60.7 9.2 %collective-permute-start.1 = (bf16[32,32,128]{2,1,0:T(8,128)(2,1)S(1)}, bf16[32,32,128]{2,1,0:T(8,128)(2,1)S(1)}, u32[]{:S(2)}, u32[]{:S(2)}) collective-permute-start(bf16[32,32,128]{2,1,0:T(8,128)(2,1)S(1)} %anchor.2.refs_0_), channel_id=1, source_target_pairs={{0,1},{1,2},{2,3},{3,4},{4,5},{5,6},{6,7},{7,0},{8,9},{9,10},{10,1... | collective-permute-start | bytes 786440 | tf_op jit(solution)/shard_map/ppermute | solution.py:612
  66.3 8.3 %collective-permute-start.5 = (bf16[32,32,128]{2,1,0:T(8,128)(2,1)}, bf16[32,32,128]{2,1,0:T(8,128)(2,1)S(1)}, u32[]{:S(2)}, u32[]{:S(2)}) collective-permute-start(bf16[32,32,128]{2,1,0:T(8,128)(2,1)} %collective-permute-done.4.refs_4_), channel_id=1, source_target_pairs={{0,7},{1,0},{2,1},{3,2},{4,3},{5,4},{6,5},{7,6},{8,15},{9,8},{10,9... | collective-permute-start | bytes 786440 | tf_op jit(solution)/shard_map/ppermute | solution.py:612
  70.0 8.3 %collective-permute-start.2 = (bf16[32,32,128]{2,1,0:T(8,128)(2,1)S(1)}, bf16[32,32,128]{2,1,0:T(8,128)(2,1)S(1)}, u32[]{:S(2)}, u32[]{:S(2)}) collective-permute-start(bf16[32,32,128]{2,1,0:T(8,128)(2,1)S(1)} %collective-permute-done.1.refs_1_), channel_id=1, source_target_pairs={{0,1},{1,2},{2,3},{3,4},{4,5},{5,6},{6,7},{7,0},{8,9},{9,10},{10,1... | collective-permute-start | bytes 786440 | tf_op jit(solution)/shard_map/ppermute | solution.py:612
  74.6 6.2 %collective-permute-start.7 = (bf16[16,32,128]{2,1,0:T(8,128)(2,1)S(1)}, bf16[16,32,128]{2,1,0:T(8,128)(2,1)S(1)}, u32[]{:S(2)}, u32[]{:S(2)}) collective-permute-start(bf16[16,32,128]{2,1,0:T(8,128)(2,1)S(1)} %slice.17), channel_id=1, source_target_pairs={{0,7},{1,0},{2,1},{3,2},{4,3},{5,4},{6,5},{7,6},{8,15},{9,8},{10,9... | collective-permute-start | bytes 393224 | tf_op jit(solution)/shard_map/ppermute | solution.py:612
  78.3 6.3 %collective-permute-start.6 = (bf16[16,32,128]{2,1,0:T(8,128)(2,1)S(1)}, bf16[16,32,128]{2,1,0:T(8,128)(2,1)S(1)}, u32[]{:S(2)}, u32[]{:S(2)}) collective-permute-start(bf16[16,32,128]{2,1,0:T(8,128)(2,1)S(1)} %slice.16), channel_id=1, source_target_pairs={{0,1},{1,2},{2,3},{3,4},{4,5},{5,6},{6,7},{7,0},{8,9},{9,10},{10,1... | collective-permute-start | bytes 393224 | tf_op jit(solution)/shard_map/ppermute | solution.py:612
  111.8 9.5 %collective-permute-start.11 = (bf16[33,32,128]{2,1,0:T(8,128)(2,1)S(1)}, bf16[33,32,128]{2,1,0:T(8,128)(2,1)}, u32[]{:S(2)}, u32[]{:S(2)}) collective-permute-start(bf16[33,32,128]{2,1,0:T(8,128)(2,1)S(1)} %named.1.refs_0_), channel_id=1, source_target_pairs={{0,7},{1,0},{2,1},{3,2},{4,3},{5,4},{6,5},{7,6},{8,15},{9,8},{10,9... | collective-permute-start | bytes 811016 | tf_op jit(solution)/shard_map/ppermute | solution.py:612
  112.1 10.6 %collective-permute-start.8 = (bf16[33,32,128]{2,1,0:T(8,128)(2,1)S(1)}, bf16[33,32,128]{2,1,0:T(8,128)(2,1)S(1)}, u32[]{:S(2)}, u32[]{:S(2)}) collective-permute-start(bf16[33,32,128]{2,1,0:T(8,128)(2,1)S(1)} %named.1.refs_0_), channel_id=1, source_target_pairs={{0,1},{1,2},{2,3},{3,4},{4,5},{5,6},{6,7},{7,0},{8,9},{9,10},{10,1... | collective-permute-start | bytes 811016 | tf_op jit(solution)/shard_map/ppermute | solution.py:612
  115.7 21.3 %all-to-all-start.4 = ((bf16[32,128,128]{2,1,0:T(8,128)(2,1)}), bf16[32,128,128]{2,1,0:T(8,128)(2,1)}, u32[]{:S(2)}, u32[]{:S(2)}) async-start(bf16[32,128,128]{2,1,0:T(8,128)(2,1)} %deal.1), calls=%async_computation.4 | async-start | bytes 2097152 | tf_op jit(solution)/shard_map/all_to_all | solution.py:645
  121.3 8.9 %collective-permute-start.12 = (bf16[33,32,128]{2,1,0:T(8,128)(2,1)}, bf16[33,32,128]{2,1,0:T(8,128)(2,1)}, u32[]{:S(2)}, u32[]{:S(2)}) collective-permute-start(bf16[33,32,128]{2,1,0:T(8,128)(2,1)} %collective-permute-done.11.refs_4_), channel_id=1, source_target_pairs={{0,7},{1,0},{2,1},{3,2},{4,3},{5,4},{6,5},{7,6},{8,15},{9,8},{10,9... | collective-permute-start | bytes 811016 | tf_op jit(solution)/shard_map/ppermute | solution.py:612
  122.7 10.1 %collective-permute-start.9 = (bf16[33,32,128]{2,1,0:T(8,128)(2,1)S(1)}, bf16[33,32,128]{2,1,0:T(8,128)(2,1)S(1)}, u32[]{:S(2)}, u32[]{:S(2)}) collective-permute-start(bf16[33,32,128]{2,1,0:T(8,128)(2,1)S(1)} %anchor.3.refs_1_), channel_id=1, source_target_pairs={{0,1},{1,2},{2,3},{3,4},{4,5},{5,6},{6,7},{7,0},{8,9},{9,10},{10,1... | collective-permute-start | bytes 811016 | tf_op jit(solution)/shard_map/ppermute | solution.py:612
  130.2 11.0 %collective-permute-start.13 = (bf16[33,32,128]{2,1,0:T(8,128)(2,1)}, bf16[33,32,128]{2,1,0:T(8,128)(2,1)S(1)}, u32[]{:S(2)}, u32[]{:S(2)}) collective-permute-start(bf16[33,32,128]{2,1,0:T(8,128)(2,1)} %collective-permute-done.12.refs_5_), channel_id=1, source_target_pairs={{0,7},{1,0},{2,1},{3,2},{4,3},{5,4},{6,5},{7,6},{8,15},{9,8},{10,9... | collective-permute-start | bytes 811016 | tf_op jit(solution)/shard_map/ppermute | solution.py:612
  132.7 8.6 %collective-permute-start.10 = (bf16[33,32,128]{2,1,0:T(8,128)(2,1)S(1)}, bf16[33,32,128]{2,1,0:T(8,128)(2,1)S(1)}, u32[]{:S(2)}, u32[]{:S(2)}) collective-permute-start(bf16[33,32,128]{2,1,0:T(8,128)(2,1)S(1)} %collective-permute-done.9.refs_2_), channel_id=1, source_target_pairs={{0,1},{1,2},{2,3},{3,4},{4,5},{5,6},{6,7},{7,0},{8,9},{9,10},{10,1... | collective-permute-start | bytes 811016 | tf_op jit(solution)/shard_map/ppermute | solution.py:612
  141.4 7.6 %collective-permute-start.15 = (bf16[17,32,128]{2,1,0:T(8,128)(2,1)S(1)}, bf16[17,32,128]{2,1,0:T(8,128)(2,1)S(1)}, u32[]{:S(2)}, u32[]{:S(2)}) collective-permute-start(bf16[17,32,128]{2,1,0:T(8,128)(2,1)S(1)} %slice.15), channel_id=1, source_target_pairs={{0,7},{1,0},{2,1},{3,2},{4,3},{5,4},{6,5},{7,6},{8,15},{9,8},{10,9... | collective-permute-start | bytes 417800 | tf_op jit(solution)/shard_map/ppermute | solution.py:612
  142.7 6.3 %collective-permute-start.14 = (bf16[16,32,128]{2,1,0:T(8,128)(2,1)S(1)}, bf16[16,32,128]{2,1,0:T(8,128)(2,1)S(1)}, u32[]{:S(2)}, u32[]{:S(2)}) collective-permute-start(bf16[16,32,128]{2,1,0:T(8,128)(2,1)S(1)} %slice.14), channel_id=1, source_target_pairs={{0,1},{1,2},{2,3},{3,4},{4,5},{5,6},{6,7},{7,0},{8,9},{9,10},{10,1... | collective-permute-start | bytes 393224 | tf_op jit(solution)/shard_map/ppermute | solution.py:612

commit v4 on v3

--- a/solution.py
+++ b/solution.py
@@ -13,7 +13,7 @@
 ROWS = 32
 TILE = 16
 LANES = 128
-DISTANCES = (0, 1, 2, 3, -1, -2, -3)
+DISTANCES = (0, 1, 2, 3, -1, -2, -3, 4)
 
 
 def params(mebibytes):
@@ -321,7 +321,6 @@
     width = LANES
     replicas = order // width
     rep = rep_ref[0]
-    half = shares[6].shape[0]
     roots = pltpu.make_async_copy(both_hbm, both_ref, sems.at[0])
     roots.start()
     parts = 4
@@ -340,14 +339,10 @@
         left_ref[lines, column : column + width] = share[:TILE]
         left_ref[lines, column + width : column + 2 * width] = share[TILE:]
 
-    for share, distance in zip(shares[:6], DISTANCES[1:]):
+    for share, distance in zip(shares, DISTANCES[1:]):
         start = lax.rem(rep - distance + replicas, replicas) * width
         for index in range(pieces):
             place(index, share[index], start)
-    start = lax.rem(rep + replicas // 2, replicas) * width
-    for index in range(pieces):
-        share = shares[6][index] if index < half else shares[7][index - half]
-        place(index, share, start)
     roots.wait()
     for index in range(pieces):
         place(index, both_ref[index, :ROWS], rep * width)
@@ -467,10 +462,9 @@
     shares, (out_hbm, out_ref, scale_ref, sems) = refs[:-4], refs[-4:]
     count, rows, order = out_ref.shape
     width = LANES
-    half = shares[7].shape[0]
     replicas = order // width
-    sums = shares[8][count - half].astype(F32)
-    for share in shares[:7]:
+    sums = shares[0][count].astype(F32)
+    for share in shares[1:]:
         sums += share[count].astype(F32)
     lane = lax.broadcasted_iota(jnp.int32, (rows, width), 1)
     pre = jnp.sum(jnp.where(lane < 3, sums, 0.0), axis=1, keepdims=True)
@@ -485,11 +479,8 @@
 
     copies = []
     for index in range(count):
-        for share, distance in zip(shares[:7], DISTANCES):
+        for share, distance in zip(shares, DISTANCES):
             place(index, share[index], lax.rem(rep_ref[0] - distance + replicas, replicas))
-        far = lax.rem(rep_ref[0] + replicas // 2, replicas)
-        share = shares[7][index] if index < half else shares[8][index - half]
-        place(index, share, far)
         block = plan_ref[HOME_BLOCK + index]
         copies.append(pltpu.make_async_copy(out_ref.at[index], out_hbm.at[block], sems.at[index]))
         copies[-1].start()
@@ -604,23 +595,26 @@
     )(plan, place, own, products, *in_hbm(left, right))
 
 
-def ring_gather(share, axis, before_last=None):
-    size = lax.axis_size(axis)
-    half = share.shape[0] // 2
+def ring_gather(share):
+    size = lax.axis_size("rep")
+    owners = lax.axis_size("fsdp")
 
     def shift(value, by):
-        return lax.ppermute(value, axis, [(i, (i + by) % size) for i in range(size)])
+        return lax.ppermute(value, "rep", [(i, (i + by) % size) for i in range(size)])
 
     down = [share, shift(share, -1)]
     up = [share, *anchor(shift(share, 1))]
     for _ in range(size // 2 - 2):
         down.append(shift(down[-1], -1))
         up.append(shift(up[-1], 1))
-    if before_last is not None:
-        up[-1], down[-1], before_last = lax.optimization_barrier((up[-1], down[-1], before_last))
-    far_down = shift(down[-1][half:], -1)
-    far_up = shift(up[-1][:half], 1)
-    return up + down[1:] + [far_up, far_down], before_last
+    even = lax.axis_index("fsdp") % 2 == 0
+    passed = lax.select(even, up[1], down[1])
+    pairs = [
+        (owner * size + i, owner * size + (i + (-3 if owner % 2 else 3)) % size)
+        for owner in range(owners)
+        for i in range(size)
+    ]
+    return up + down[1:] + [lax.ppermute(passed, ("fsdp", "rep"), pairs)]
 
 
 def anchor_kernel(*refs):
@@ -658,14 +652,16 @@
     roots = exchange(route(plan, exchange(spare)))
     left, both = pick(place, plan, kept, roots)
     packed, left = lax.optimization_barrier((gather(plan, gradient), left))
-    left_shares, _ = ring_gather(left, "rep")
+    left_shares = ring_gather(left)
     outgoing, own = block_shares(rep, exchange(packed), both, left_shares[1:])
 
     arrived = exchange(outgoing)
     products = exchange(deal(plan, arrived, slots - 1))
-    outputs = factors(plan, place, own, products, left_state, right_state)
-    shares, outputs = ring_gather(named(arrived), "rep", outputs)
-    left_factor, right_factor = outputs
+    left_factor, right_factor = factors(plan, place, own, products, left_state, right_state)
+    shares = ring_gather(named(arrived))
+    shares, left_factor, right_factor = lax.optimization_barrier(
+        (shares, left_factor, right_factor)
+    )
     update = finish(rep, plan, shares, count, rows, order)
     return (update, left_factor, right_factor)
 

time: 154 us -> 150 us (0.974)
    all_to_all x4, waiting for transfers between devices: 22.7 us -> 18.5 us  [exchange(): lax.all_to_all(value, 'fsdp', split_axis=0, concat_axis=0, tiled=True)]
    ppermute x16 -> x14, waiting for transfers between devices: 29 us -> 32.7 us  [the longest x12 32.3 us: shift(): lax.ppermute(value, 'rep', [(i, (i + by) % size) for i in range(size)])]
    ppermute x16 -> x14, starting transfers between devices: 26.3 us -> 24.8 us  [the longest x12 20.5 us: shift(): lax.ppermute(value, 'rep', [(i, (i + by) % size) for i in range(size)])]
  transfers between devices with their start and end apart: 20 -> 18, of which waited for: 11 -> 10; matrix products, arithmetic and copies ran while one was open for 0% -> 0% of each run, Pallas kernels for 9% -> 9%
where the time goes in v4:
time: 150 us; the launch traced here: 149 us
  waiting for transfers between devices  51.2 us (34%)
  starting transfers between devices  48.8 us (33%)
  Pallas kernels  26.7 us (18%)
  blocking collectives  20.9 us (14%)
    ppermute x12, waiting for transfers between devices, shift(): lax.ppermute(value, 'rep', [(i, (i + by) % size) for i in range(size)])  32.3 us
    all_to_all x4, starting transfers between devices, exchange(): lax.all_to_all(value, 'fsdp', split_axis=0, concat_axis=0, tiled=True)  24.1 us
    all_to_all x1, blocking collectives, exchange(): lax.all_to_all(value, 'fsdp', split_axis=0, concat_axis=0, tiled=True)  20.9 us
    ppermute x12, starting transfers between devices, shift(): lax.ppermute(value, 'rep', [(i, (i + by) % size) for i in range(size)])  20.5 us
    all_to_all x4, waiting for transfers between devices, exchange(): lax.all_to_all(value, 'fsdp', split_axis=0, concat_axis=0, tiled=True)  18.5 us
    pallas_call x1, Pallas kernels, block_shares(): pl.pallas_call(block_kernel, in_specs=[pl.BlockSpec(memory_space=pltpu.SM...  5.23 us
    ppermute x2, starting transfers between devices, ring_gather(): return up + down[1:] + [lax.ppermute(passed, ('fsdp', 'rep'), pairs)]  4.3 us
    pallas_call x1, Pallas kernels, factors(): pl.pallas_call(factor_kernel, in_specs=[pl.BlockSpec(memory_space=pltpu.S...  4.26 us
  transfers between devices with their start and end apart: 18, of which 10 were waited for; matrix products, arithmetic and copies ran while one was open for 0% of the time, Pallas kernels for 9%

profile of v4, /device:TPU:8, one launch (start us, length us, event | category | flops | bytes accessed | tf_op | source)
XLA Modules:
  0.0 148.8 jit_solution(17908201152981180784)
XLA Ops:
  0.6 0.1 pad_add_fusion.place_ref
  0.7 0.0 copy-start.1
  0.7 0.0 copy-start.2
  0.7 2.7 %pack.1 = bf16[32,128,128]{2,1,0:T(8,128)(2,1)} custom-call(s32[2]{0:T(128)S(1)} %pad_add_fusion.place_ref, s32[32]{0:T(128)} %owner_hbm.1, s32[32]{0:T(128)} %slot_hbm.1, bf16[3,128,1024]{2,1,0:T(8,128)(2,1)} %bitcast.4, bf16[3,1024,128]{2,1,0:T(8,128)(2,1)} %bitcast.6), custom_call_target="tpu_custom_call" | custom-call | tf_op jit(solution)/shard_map/pack/pallas_call | solution.py:185
  3.4 7.5 %all-to-all-start = ((bf16[32,128,128]{2,1,0:T(8,128)(2,1)}), bf16[32,128,128]{2,1,0:T(8,128)(2,1)S(1)}, u32[]{:S(2)}, u32[]{:S(2)}) async-start(bf16[32,128,128]{2,1,0:T(8,128)(2,1)} %pack.1), calls=%async_computation | async-start | bytes 2097152 | tf_op jit(solution)/shard_map/all_to_all | solution.py:639
  10.9 0.0 copy-done.1
  10.9 0.0 copy-done.2
  11.0 3.5 %make_plan.1.plan_ref = s32[256]{0:T(256)S(1)} custom-call(s32[32]{0:T(128)S(1)} %copy-done.1, s32[32]{0:T(128)S(1)} %copy-done.2), custom_call_target="tpu_custom_call" | custom-call | tf_op jit(solution)/shard_map/make_plan/pallas_call | solution.py:114
  14.5 0.0 copy-start
  14.5 12.0 %all-to-all-done.arrived_ref = bf16[32,128,128]{2,1,0:T(8,128)(2,1)S(1)} async-done(((bf16[32,128,128]{2,1,0:T(8,128)(2,1)}), bf16[32,128,128]{2,1,0:T(8,128)(2,1)S(1)}, u32[]{:S(2)}, u32[]{:S(2)}) %all-to-all-start) | async-done | bytes 1048608 | tf_op jit(solution)/shard_map/all_to_all | solution.py:639
  26.5 1.6 %route.1 = bf16[32,64,128]{2,1,0:T(8,128)(2,1)} custom-call(s32[256]{0:T(256)S(1)} %make_plan.1.plan_ref, bf16[32,128,128]{2,1,0:T(8,128)(2,1)S(1)} %all-to-all-done.arrived_ref), custom_call_target="tpu_custom_call" | custom-call | tf_op jit(solution)/shard_map/route/pallas_call | solution.py:251
  28.1 5.3 %all-to-all-start.1 = ((bf16[32,64,128]{2,1,0:T(8,128)(2,1)}), bf16[32,64,128]{2,1,0:T(8,128)(2,1)S(1)}, u32[]{:S(2)}, u32[]{:S(2)}) async-start(bf16[32,64,128]{2,1,0:T(8,128)(2,1)} %route.1), calls=%async_computation.1 | async-start | bytes 1048576 | tf_op jit(solution)/shard_map/all_to_all | solution.py:639
  33.4 1.7 %keep.1.kept_ref = bf16[32,64,128]{2,1,0:T(8,128)(2,1)S(1)} custom-call(s32[2]{0:T(128)S(1)} %pad_add_fusion.place_ref, s32[256]{0:T(256)S(1)} %make_plan.1.plan_ref, bf16[3,128,1024]{2,1,0:T(8,128)(2,1)} %bitcast.5, bf16[3,1024,128]{2,1,0:T(8,128)(2,1)} %bitcast.7), custom_call_target="tpu_custom_call" | custom-call | tf_op jit(solution)/shard_map/keep/pallas_call | solution.py:222
  35.1 0.0 copy-done
  35.1 2.0 %gather.1 = bf16[32,32,1024]{2,1,0:T(8,128)(2,1)} custom-call(s32[256]{0:T(256)S(1)} %make_plan.1.plan_ref, bf16[32,32,1024]{2,1,0:T(8,128)(2,1)S(1)} %copy-done), custom_call_target="tpu_custom_call" | custom-call | tf_op jit(solution)/shard_map/gather/pallas_call | solution.py:306
  37.1 6.5 %all-to-all-done.1.roots_ref = bf16[32,64,128]{2,1,0:T(8,128)(2,1)S(1)} async-done(((bf16[32,64,128]{2,1,0:T(8,128)(2,1)}), bf16[32,64,128]{2,1,0:T(8,128)(2,1)S(1)}, u32[]{:S(2)}, u32[]{:S(2)}) %all-to-all-start.1) | async-done | bytes 524320 | tf_op jit(solution)/shard_map/all_to_all | solution.py:639
  43.6 1.4 pick.1
  45.0 5.9 %collective-permute-start.3 = (bf16[32,32,128]{2,1,0:T(8,128)(2,1)S(1)}, bf16[32,32,128]{2,1,0:T(8,128)(2,1)}, u32[]{:S(2)}, u32[]{:S(2)}) collective-permute-start(bf16[32,32,128]{2,1,0:T(8,128)(2,1)S(1)} %get-tuple-element.24), channel_id=1, source_target_pairs={{0,7},{1,0},{2,1},{3,2},{4,3},{5,4},{6,5},{7,6},{8,15},{9,8},{10,9... | collective-permute-start | bytes 786440 | tf_op jit(solution)/shard_map/ppermute | solution.py:603
  50.9 0.0 collective-permute-start
  50.9 5.6 %all-to-all-start.2 = ((bf16[32,32,1024]{2,1,0:T(8,128)(2,1)}), bf16[32,32,1024]{2,1,0:T(8,128)(2,1)}, u32[]{:S(2)}, u32[]{:S(2)}) async-start(bf16[32,32,1024]{2,1,0:T(8,128)(2,1)} %gather.1), calls=%async_computation.2 | async-start | bytes 4194304 | tf_op jit(solution)/shard_map/all_to_all | solution.py:639
  56.5 0.4 collective-permute-done.3.refs_3_
  56.9 3.8 %collective-permute-start.4 = (bf16[32,32,128]{2,1,0:T(8,128)(2,1)}, bf16[32,32,128]{2,1,0:T(8,128)(2,1)}, u32[]{:S(2)}, u32[]{:S(2)}) collective-permute-start(bf16[32,32,128]{2,1,0:T(8,128)(2,1)} %collective-permute-done.3.refs_3_), channel_id=1, source_target_pairs={{0,7},{1,0},{2,1},{3,2},{4,3},{5,4},{6,5},{7,6},{8,15},{9,8},{10,9... | collective-permute-start | bytes 786440 | tf_op jit(solution)/shard_map/ppermute | solution.py:603
  60.7 0.0 collective-permute-done.refs_0_
  60.7 0.0 collective-permute-start.1
  60.8 2.3 %collective-permute-start.6 = (bf16[32,32,128]{2,1,0:T(8,128)(2,1)S(1)}, bf16[32,32,128]{2,1,0:T(8,128)(2,1)S(1)}, u32[]{:S(2)}, u32[]{:S(2)}) collective-permute-start(bf16[32,32,128]{2,1,0:T(8,128)(2,1)S(1)} %broadcast_select_fusion.1), channel_id=1, source_target_pairs={{0,3},{1,4},{2,5},{3,6},{4,7},{5,0},{6,1},{7,2},{8,13},{9,14},{10,... | collective-permute-start | bytes 786440 | tf_op jit(solution)/shard_map/ppermute | solution.py:617
  63.0 9.2 %collective-permute-done.4.refs_4_ = bf16[32,32,128]{2,1,0:T(8,128)(2,1)} collective-permute-done((bf16[32,32,128]{2,1,0:T(8,128)(2,1)}, bf16[32,32,128]{2,1,0:T(8,128)(2,1)}, u32[]{:S(2)}, u32[]{:S(2)}) %collective-permute-start.4) | collective-permute-done | bytes 262176 | tf_op jit(solution)/shard_map/ppermute | solution.py:603
  72.2 3.9 %collective-permute-start.5 = (bf16[32,32,128]{2,1,0:T(8,128)(2,1)}, bf16[32,32,128]{2,1,0:T(8,128)(2,1)S(1)}, u32[]{:S(2)}, u32[]{:S(2)}) collective-permute-start(bf16[32,32,128]{2,1,0:T(8,128)(2,1)} %collective-permute-done.4.refs_4_), channel_id=1, source_target_pairs={{0,7},{1,0},{2,1},{3,2},{4,3},{5,4},{6,5},{7,6},{8,15},{9,8},{10,9... | collective-permute-start | bytes 786440 | tf_op jit(solution)/shard_map/ppermute | solution.py:603
  76.2 0.0 collective-permute-done.1.refs_1_
  76.2 0.0 collective-permute-start.2
  76.2 0.4 collective-permute-done.6.refs_6_
  76.6 3.8 %collective-permute-done.5.refs_5_ = bf16[32,32,128]{2,1,0:T(8,128)(2,1)S(1)} collective-permute-done((bf16[32,32,128]{2,1,0:T(8,128)(2,1)}, bf16[32,32,128]{2,1,0:T(8,128)(2,1)S(1)}, u32[]{:S(2)}, u32[]{:S(2)}) %collective-permute-start.5) | collective-permute-done | bytes 262176 | tf_op jit(solution)/shard_map/ppermute | solution.py:603
  80.4 3.4 %collective-permute-done.2.refs_2_ = bf16[32,32,128]{2,1,0:T(8,128)(2,1)S(1)} collective-permute-done((bf16[32,32,128]{2,1,0:T(8,128)(2,1)S(1)}, bf16[32,32,128]{2,1,0:T(8,128)(2,1)S(1)}, u32[]{:S(2)}, u32[]{:S(2)}) %collective-permute-start.2) | collective-permute-done | bytes 262176 | tf_op jit(solution)/shard_map/ppermute | solution.py:603
  83.7 0.0 all-to-all-done.2.block_hbm
  83.7 5.2 %block_shares.1 = (bf16[32,112,128]{2,1,0:T(8,128)(2,1)S(1)}, bf16[32,64,128]{2,1,0:T(8,128)(2,1)S(1)}) custom-call(s32[1]{0:T(128)} %bitcast.rep_ref, bf16[32,32,1024]{2,1,0:T(8,128)(2,1)} %all-to-all-done.2.block_hbm, bf16[32,64,128]{2,1,0:T(8,128)(2,1)} %get-tuple-element.23.both_hbm, bf16[32,32,128]{2,1,0:T(8,128)(2,1)S(1)} %anchor.2.refs_0_, ...), custom_call_target="tpu_custom_call" | custom-call | flops 1073741824 | bytes 6291456 | tf_op jit(solution)/shard_map/block_shares/pallas_call | solution.py:397
  89.0 20.9 %all_to_all.25.arrived_ref = bf16[32,112,128]{2,1,0:T(8,128)(2,1)S(1)} all-to-all(bf16[32,112,128]{2,1,0:T(8,128)(2,1)S(1)} %get-tuple-element.25), channel_id=1, replica_groups=mesh['fsdp'=32,'rep'=8] {'fsdp'}, dimensions={0} | all-to-all | bytes 1835008 | tf_op jit(solution)/shard_map/all_to_all | solution.py:639
  110.0 1.4 collective-permute-start.10
  111.4 0.7 collective-permute-start.7
  112.1 1.6 %deal.1 = bf16[32,128,128]{2,1,0:T(8,128)(2,1)} custom-call(s32[256]{0:T(256)S(1)} %make_plan.1.plan_ref, bf16[32,112,128]{2,1,0:T(8,128)(2,1)S(1)} %all_to_all.25.arrived_ref), custom_call_target="tpu_custom_call" | custom-call | tf_op jit(solution)/shard_map/deal/pallas_call | solution.py:449
  113.7 5.6 %all-to-all-start.4 = ((bf16[32,128,128]{2,1,0:T(8,128)(2,1)}), bf16[32,128,128]{2,1,0:T(8,128)(2,1)}, u32[]{:S(2)}, u32[]{:S(2)}) async-start(bf16[32,128,128]{2,1,0:T(8,128)(2,1)} %deal.1), calls=%async_computation.4 | async-start | bytes 2097152 | tf_op jit(solution)/shard_map/all_to_all | solution.py:639
  119.3 0.0 collective-permute-done.10.refs_4_
  119.3 2.7 %collective-permute-start.11 = (bf16[33,32,128]{2,1,0:T(8,128)(2,1)}, bf16[33,32,128]{2,1,0:T(8,128)(2,1)}, u32[]{:S(2)}, u32[]{:S(2)}) collective-permute-start(bf16[33,32,128]{2,1,0:T(8,128)(2,1)} %collective-permute-done.10.refs_4_), channel_id=1, source_target_pairs={{0,7},{1,0},{2,1},{3,2},{4,3},{5,4},{6,5},{7,6},{8,15},{9,8},{10,9... | collective-permute-start | bytes 811016 | tf_op jit(solution)/shard_map/ppermute | solution.py:603
  121.9 0.0 collective-permute-done.7.refs_0_
  121.9 0.0 collective-permute-start.8
  122.0 2.0 %collective-permute-start.13 = (bf16[33,32,128]{2,1,0:T(8,128)(2,1)S(1)}, bf16[33,32,128]{2,1,0:T(8,128)(2,1)S(1)}, u32[]{:S(2)}, u32[]{:S(2)}) collective-permute-start(bf16[33,32,128]{2,1,0:T(8,128)(2,1)S(1)} %broadcast_select_fusion), channel_id=1, source_target_pairs={{0,3},{1,4},{2,5},{3,6},{4,7},{5,0},{6,1},{7,2},{8,13},{9,14},{10,... | collective-permute-start | bytes 811016 | tf_op jit(solution)/shard_map/ppermute | solution.py:617
  124.0 10.2 %collective-permute-done.11.refs_5_ = bf16[33,32,128]{2,1,0:T(8,128)(2,1)} collective-permute-done((bf16[33,32,128]{2,1,0:T(8,128)(2,1)}, bf16[33,32,128]{2,1,0:T(8,128)(2,1)}, u32[]{:S(2)}, u32[]{:S(2)}) %collective-permute-start.11) | collective-permute-done | bytes 270368 | tf_op jit(solution)/shard_map/ppermute | solution.py:603
  134.3 0.0 collective-permute-start.12
  134.3 0.0 collective-permute-done.8.refs_2_
  134.3 2.0 %collective-permute-start.9 = (bf16[33,32,128]{2,1,0:T(8,128)(2,1)S(1)}, bf16[33,32,128]{2,1,0:T(8,128)(2,1)S(1)}, u32[]{:S(2)}, u32[]{:S(2)}) collective-permute-start(bf16[33,32,128]{2,1,0:T(8,128)(2,1)S(1)} %collective-permute-done.8.refs_2_), channel_id=1, source_target_pairs={{0,1},{1,2},{2,3},{3,4},{4,5},{5,6},{6,7},{7,0},{8,9},{9,10},{10,1... | collective-permute-start | bytes 811016 | tf_op jit(solution)/shard_map/ppermute | solution.py:603
  136.3 0.0 all-to-all-done.4.products_ref
  136.3 4.3 %factors.1 = (f32[1,3,128,1024]{3,2,1,0:T(8,128)}, f32[1,3,1024,128]{3,2,1,0:T(8,128)}) custom-call(s32[256]{0:T(256)S(1)} %make_plan.1.plan_ref, s32[2]{0:T(128)S(1)} %pad_add_fusion.place_ref, bf16[32,64,128]{2,1,0:T(8,128)(2,1)S(1)} %get-tuple-element.26.own_ref, bf16[32,128,128]{2,1,0:T(8,128)(2,1)} %all-to-all-done.4.products_ref, ...), custom_call_target="tpu_custom_call" | custom-call | flops 6291456 | bytes 15728640 | tf_op jit(solution)/shard_map/factors/pallas_call | solution.py:569
  140.6 0.0 collective-permute-done.13.refs_7_
  140.6 2.0 %collective-permute-done.12.refs_6_ = bf16[33,32,128]{2,1,0:T(8,128)(2,1)S(1)} collective-permute-done((bf16[33,32,128]{2,1,0:T(8,128)(2,1)}, bf16[33,32,128]{2,1,0:T(8,128)(2,1)S(1)}, u32[]{:S(2)}, u32[]{:S(2)}) %collective-permute-start.12) | collective-permute-done | bytes 270368 | tf_op jit(solution)/shard_map/ppermute | solution.py:603
  142.6 3.3 %collective-permute-done.9.refs_3_ = bf16[33,32,128]{2,1,0:T(8,128)(2,1)S(1)} collective-permute-done((bf16[33,32,128]{2,1,0:T(8,128)(2,1)S(1)}, bf16[33,32,128]{2,1,0:T(8,128)(2,1)S(1)}, u32[]{:S(2)}, u32[]{:S(2)}) %collective-permute-start.9) | collective-permute-done | bytes 270368 | tf_op jit(solution)/shard_map/ppermute | solution.py:603
  145.9 2.7 %finish.1 = bf16[32,32,1024]{2,1,0:T(8,128)(2,1)} custom-call(s32[1]{0:T(128)} %bitcast.rep_ref, s32[256]{0:T(256)S(1)} %make_plan.1.plan_ref, bf16[33,32,128]{2,1,0:T(8,128)(2,1)S(1)} %named.1.refs_0_, bf16[33,32,128]{2,1,0:T(8,128)(2,1)S(1)} %anchor.3.refs_1_, bf16[33,32,128]{2,1,0:T(8,128)(2,1)S(1)} %collective-permute-done.8.refs_2_, ...), custom_call_target="tpu_custom_call" | custom-call | tf_op jit(solution)/shard_map/finish/pallas_call | solution.py:493
  (5 shorter events, 0.1 us)
Async XLA Ops:
  0.7 10.2 %copy-start.1 = (s32[32]{0:T(128)S(1)}, s32[32]{0:T(128)}, u32[]{:S(2)}) copy-start(s32[32]{0:T(128)} %owner_hbm.1) | copy-start | bytes 388
  0.7 10.2 %copy-start.2 = (s32[32]{0:T(128)S(1)}, s32[32]{0:T(128)}, u32[]{:S(2)}) copy-start(s32[32]{0:T(128)} %slot_hbm.1) | copy-start | bytes 388
  3.4 23.1 %all-to-all-start = ((bf16[32,128,128]{2,1,0:T(8,128)(2,1)}), bf16[32,128,128]{2,1,0:T(8,128)(2,1)S(1)}, u32[]{:S(2)}, u32[]{:S(2)}) async-start(bf16[32,128,128]{2,1,0:T(8,128)(2,1)} %pack.1), calls=%async_computation | async-start | bytes 2097152 | tf_op jit(solution)/shard_map/all_to_all | solution.py:639
  14.5 20.6 %copy-start = (bf16[32,32,1024]{2,1,0:T(8,128)(2,1)S(1)}, bf16[32,32,1024]{2,1,0:T(8,128)(2,1)}, u32[]{:S(2)}) copy-start(bf16[32,32,1024]{2,1,0:T(8,128)(2,1)} %gradient_ref.1) | copy-start | bytes 6291460
  28.1 15.5 %all-to-all-start.1 = ((bf16[32,64,128]{2,1,0:T(8,128)(2,1)}), bf16[32,64,128]{2,1,0:T(8,128)(2,1)S(1)}, u32[]{:S(2)}, u32[]{:S(2)}) async-start(bf16[32,64,128]{2,1,0:T(8,128)(2,1)} %route.1), calls=%async_computation.1 | async-start | bytes 1048576 | tf_op jit(solution)/shard_map/all_to_all | solution.py:639
  45.0 12.0 %collective-permute-start.3 = (bf16[32,32,128]{2,1,0:T(8,128)(2,1)S(1)}, bf16[32,32,128]{2,1,0:T(8,128)(2,1)}, u32[]{:S(2)}, u32[]{:S(2)}) collective-permute-start(bf16[32,32,128]{2,1,0:T(8,128)(2,1)S(1)} %get-tuple-element.24), channel_id=1, source_target_pairs={{0,7},{1,0},{2,1},{3,2},{4,3},{5,4},{6,5},{7,6},{8,15},{9,8},{10,9... | collective-permute-start | bytes 786440 | tf_op jit(solution)/shard_map/ppermute | solution.py:603
  50.9 9.8 %collective-permute-start = (bf16[32,32,128]{2,1,0:T(8,128)(2,1)S(1)}, bf16[32,32,128]{2,1,0:T(8,128)(2,1)S(1)}, u32[]{:S(2)}, u32[]{:S(2)}) collective-permute-start(bf16[32,32,128]{2,1,0:T(8,128)(2,1)S(1)} %get-tuple-element.24), channel_id=1, source_target_pairs={{0,1},{1,2},{2,3},{3,4},{4,5},{5,6},{6,7},{7,0},{8,9},{9,10},{10,1... | collective-permute-start | bytes 786440 | tf_op jit(solution)/shard_map/ppermute | solution.py:603
  50.9 32.9 %all-to-all-start.2 = ((bf16[32,32,1024]{2,1,0:T(8,128)(2,1)}), bf16[32,32,1024]{2,1,0:T(8,128)(2,1)}, u32[]{:S(2)}, u32[]{:S(2)}) async-start(bf16[32,32,1024]{2,1,0:T(8,128)(2,1)} %gather.1), calls=%async_computation.2 | async-start | bytes 4194304 | tf_op jit(solution)/shard_map/all_to_all | solution.py:639
  56.9 15.3 %collective-permute-start.4 = (bf16[32,32,128]{2,1,0:T(8,128)(2,1)}, bf16[32,32,128]{2,1,0:T(8,128)(2,1)}, u32[]{:S(2)}, u32[]{:S(2)}) collective-permute-start(bf16[32,32,128]{2,1,0:T(8,128)(2,1)} %collective-permute-done.3.refs_3_), channel_id=1, source_target_pairs={{0,7},{1,0},{2,1},{3,2},{4,3},{5,4},{6,5},{7,6},{8,15},{9,8},{10,9... | collective-permute-start | bytes 786440 | tf_op jit(solution)/shard_map/ppermute | solution.py:603
  60.7 15.4 %collective-permute-start.1 = (bf16[32,32,128]{2,1,0:T(8,128)(2,1)S(1)}, bf16[32,32,128]{2,1,0:T(8,128)(2,1)S(1)}, u32[]{:S(2)}, u32[]{:S(2)}) collective-permute-start(bf16[32,32,128]{2,1,0:T(8,128)(2,1)S(1)} %anchor.2.refs_0_), channel_id=1, source_target_pairs={{0,1},{1,2},{2,3},{3,4},{4,5},{5,6},{6,7},{7,0},{8,9},{9,10},{10,1... | collective-permute-start | bytes 786440 | tf_op jit(solution)/shard_map/ppermute | solution.py:603
  60.8 15.8 %collective-permute-start.6 = (bf16[32,32,128]{2,1,0:T(8,128)(2,1)S(1)}, bf16[32,32,128]{2,1,0:T(8,128)(2,1)S(1)}, u32[]{:S(2)}, u32[]{:S(2)}) collective-permute-start(bf16[32,32,128]{2,1,0:T(8,128)(2,1)S(1)} %broadcast_select_fusion.1), channel_id=1, source_target_pairs={{0,3},{1,4},{2,5},{3,6},{4,7},{5,0},{6,1},{7,2},{8,13},{9,14},{10,... | collective-permute-start | bytes 786440 | tf_op jit(solution)/shard_map/ppermute | solution.py:617
  72.2 8.1 %collective-permute-start.5 = (bf16[32,32,128]{2,1,0:T(8,128)(2,1)}, bf16[32,32,128]{2,1,0:T(8,128)(2,1)S(1)}, u32[]{:S(2)}, u32[]{:S(2)}) collective-permute-start(bf16[32,32,128]{2,1,0:T(8,128)(2,1)} %collective-permute-done.4.refs_4_), channel_id=1, source_target_pairs={{0,7},{1,0},{2,1},{3,2},{4,3},{5,4},{6,5},{7,6},{8,15},{9,8},{10,9... | collective-permute-start | bytes 786440 | tf_op jit(solution)/shard_map/ppermute | solution.py:603
  76.2 7.6 %collective-permute-start.2 = (bf16[32,32,128]{2,1,0:T(8,128)(2,1)S(1)}, bf16[32,32,128]{2,1,0:T(8,128)(2,1)S(1)}, u32[]{:S(2)}, u32[]{:S(2)}) collective-permute-start(bf16[32,32,128]{2,1,0:T(8,128)(2,1)S(1)} %collective-permute-done.1.refs_1_), channel_id=1, source_target_pairs={{0,1},{1,2},{2,3},{3,4},{4,5},{5,6},{6,7},{7,0},{8,9},{9,10},{10,1... | collective-permute-start | bytes 786440 | tf_op jit(solution)/shard_map/ppermute | solution.py:603
  110.0 9.3 %collective-permute-start.10 = (bf16[33,32,128]{2,1,0:T(8,128)(2,1)S(1)}, bf16[33,32,128]{2,1,0:T(8,128)(2,1)}, u32[]{:S(2)}, u32[]{:S(2)}) collective-permute-start(bf16[33,32,128]{2,1,0:T(8,128)(2,1)S(1)} %named.1.refs_0_), channel_id=1, source_target_pairs={{0,7},{1,0},{2,1},{3,2},{4,3},{5,4},{6,5},{7,6},{8,15},{9,8},{10,9... | collective-permute-start | bytes 811016 | tf_op jit(solution)/shard_map/ppermute | solution.py:603
  111.4 10.5 %collective-permute-start.7 = (bf16[33,32,128]{2,1,0:T(8,128)(2,1)S(1)}, bf16[33,32,128]{2,1,0:T(8,128)(2,1)S(1)}, u32[]{:S(2)}, u32[]{:S(2)}) collective-permute-start(bf16[33,32,128]{2,1,0:T(8,128)(2,1)S(1)} %named.1.refs_0_), channel_id=1, source_target_pairs={{0,1},{1,2},{2,3},{3,4},{4,5},{5,6},{6,7},{7,0},{8,9},{9,10},{10,1... | collective-permute-start | bytes 811016 | tf_op jit(solution)/shard_map/ppermute | solution.py:603
  113.7 22.6 %all-to-all-start.4 = ((bf16[32,128,128]{2,1,0:T(8,128)(2,1)}), bf16[32,128,128]{2,1,0:T(8,128)(2,1)}, u32[]{:S(2)}, u32[]{:S(2)}) async-start(bf16[32,128,128]{2,1,0:T(8,128)(2,1)} %deal.1), calls=%async_computation.4 | async-start | bytes 2097152 | tf_op jit(solution)/shard_map/all_to_all | solution.py:639
  119.3 15.0 %collective-permute-start.11 = (bf16[33,32,128]{2,1,0:T(8,128)(2,1)}, bf16[33,32,128]{2,1,0:T(8,128)(2,1)}, u32[]{:S(2)}, u32[]{:S(2)}) collective-permute-start(bf16[33,32,128]{2,1,0:T(8,128)(2,1)} %collective-permute-done.10.refs_4_), channel_id=1, source_target_pairs={{0,7},{1,0},{2,1},{3,2},{4,3},{5,4},{6,5},{7,6},{8,15},{9,8},{10,9... | collective-permute-start | bytes 811016 | tf_op jit(solution)/shard_map/ppermute | solution.py:603
  121.9 12.3 %collective-permute-start.8 = (bf16[33,32,128]{2,1,0:T(8,128)(2,1)S(1)}, bf16[33,32,128]{2,1,0:T(8,128)(2,1)S(1)}, u32[]{:S(2)}, u32[]{:S(2)}) collective-permute-start(bf16[33,32,128]{2,1,0:T(8,128)(2,1)S(1)} %anchor.3.refs_1_), channel_id=1, source_target_pairs={{0,1},{1,2},{2,3},{3,4},{4,5},{5,6},{6,7},{7,0},{8,9},{9,10},{10,1... | collective-permute-start | bytes 811016 | tf_op jit(solution)/shard_map/ppermute | solution.py:603
  122.0 18.6 %collective-permute-start.13 = (bf16[33,32,128]{2,1,0:T(8,128)(2,1)S(1)}, bf16[33,32,128]{2,1,0:T(8,128)(2,1)S(1)}, u32[]{:S(2)}, u32[]{:S(2)}) collective-permute-start(bf16[33,32,128]{2,1,0:T(8,128)(2,1)S(1)} %broadcast_select_fusion), channel_id=1, source_target_pairs={{0,3},{1,4},{2,5},{3,6},{4,7},{5,0},{6,1},{7,2},{8,13},{9,14},{10,... | collective-permute-start | bytes 811016 | tf_op jit(solution)/shard_map/ppermute | solution.py:617
  134.3 8.3 %collective-permute-start.12 = (bf16[33,32,128]{2,1,0:T(8,128)(2,1)}, bf16[33,32,128]{2,1,0:T(8,128)(2,1)S(1)}, u32[]{:S(2)}, u32[]{:S(2)}) collective-permute-start(bf16[33,32,128]{2,1,0:T(8,128)(2,1)} %collective-permute-done.11.refs_5_), channel_id=1, source_target_pairs={{0,7},{1,0},{2,1},{3,2},{4,3},{5,4},{6,5},{7,6},{8,15},{9,8},{10,9... | collective-permute-start | bytes 811016 | tf_op jit(solution)/shard_map/ppermute | solution.py:603
  134.3 11.6 %collective-permute-start.9 = (bf16[33,32,128]{2,1,0:T(8,128)(2,1)S(1)}, bf16[33,32,128]{2,1,0:T(8,128)(2,1)S(1)}, u32[]{:S(2)}, u32[]{:S(2)}) collective-permute-start(bf16[33,32,128]{2,1,0:T(8,128)(2,1)S(1)} %collective-permute-done.8.refs_2_), channel_id=1, source_target_pairs={{0,1},{1,2},{2,3},{3,4},{4,5},{5,6},{6,7},{7,0},{8,9},{9,10},{10,1... | collective-permute-start | bytes 811016 | tf_op jit(solution)/shard_map/ppermute | solution.py:603

commit v5 on v4

--- a/solution.py
+++ b/solution.py
@@ -82,7 +82,7 @@
             @pl.when(named & (count > 0))
             def _():
                 list_ref[0, spare] = block
-                list_ref[1, spare] = owner * 2 + count - 1
+                list_ref[1, spare] = owner * 2 + slot - 1
 
             spare += (named & (count > 0)).astype(jnp.int32)
             count += named.astype(jnp.int32)
@@ -135,69 +135,46 @@
         ]
 
 
-def pack_kernel(
-    place_ref, owner_hbm, slot_hbm, left_hbm, right_hbm, spare_hbm, *scratch
-):
-    owner_ref, slot_ref, left_ref, right_ref, spare_ref, sems = scratch
-    spares = left_ref.shape[0]
-    roots = []
-    for spare in range(spares):
+def pack_kernel(left_hbm, right_hbm, spare_hbm, left_ref, right_ref, spare_ref, sems):
+    reads, writes = [], []
+    for spare in range(left_ref.shape[0]):
         pair = (
             pltpu.make_async_copy(left_hbm.at[spare + 1], left_ref.at[spare], sems.at[0, spare]),
             pltpu.make_async_copy(right_hbm.at[spare + 1], right_ref.at[spare], sems.at[1, spare]),
         )
-        roots.append(pair)
-    names = (
-        pltpu.make_async_copy(owner_hbm, owner_ref, sems.at[2, 0]),
-        pltpu.make_async_copy(slot_hbm, slot_ref, sems.at[2, 1]),
-    )
-    for copy in names + roots[1] + roots[0]:
-        copy.start()
-    for copy in names:
-        copy.wait()
-
-    def look(index, found):
-        own = owner_ref[index] == place_ref[1]
-        return found + (own & (slot_ref[index] < spares)).astype(jnp.int32)
-
-    found = lax.fori_loop(0, owner_ref.shape[0], look, jnp.int32(0), unroll=4)
-    second = jnp.where(found == spares, 0, 1)
-    for copy in roots[1]:
-        copy.wait()
-    writes = []
-    for spare in (1, 0):
-        if spare == 0:
-            for copy in roots[0]:
-                copy.wait()
-        cut(left_ref, right_ref, 1 if spare else second, spare_ref, 2 * ROWS * spare)
+        for copy in pair:
+            copy.start()
+        reads.append(pair)
+    for spare, pair in enumerate(reads):
+        for copy in pair:
+            copy.wait()
+        cut(left_ref, right_ref, spare, spare_ref, 2 * ROWS * spare)
         part = (slice(None), pl.ds(2 * ROWS * spare, 2 * ROWS))
-        copy = pltpu.make_async_copy(spare_ref.at[part], spare_hbm.at[part], sems.at[3, spare])
+        copy = pltpu.make_async_copy(spare_ref.at[part], spare_hbm.at[part], sems.at[2, spare])
         copy.start()
         writes.append(copy)
     for copy in writes:
         copy.wait()
 
 
-def pack(place, owner, slot, left, right, pieces):
+def pack(left, right, pieces):
     hbm = pl.BlockSpec(memory_space=pltpu.HBM)
     spares = left.shape[0] - 1
     shape = (pieces, spares * 2 * ROWS, LANES)
     return pl.pallas_call(
         pack_kernel,
-        in_specs=[pl.BlockSpec(memory_space=pltpu.SMEM)] + [hbm] * 4,
+        in_specs=[hbm, hbm],
         out_specs=hbm,
         out_shape=pltpu.HBM(shape, BF16),
         scratch_shapes=[
-            pltpu.SMEM(owner.shape, jnp.int32),
-            pltpu.SMEM(slot.shape, jnp.int32),
             pltpu.VMEM((spares,) + left.shape[1:], BF16),
             pltpu.VMEM((spares,) + right.shape[1:], BF16),
             pltpu.VMEM(shape, BF16),
-            pltpu.SemaphoreType.DMA((4, 2)),
+            pltpu.SemaphoreType.DMA((3, spares)),
         ],
         compiler_params=params(8),
         name="pack",
-    )(place, *in_hbm(owner, slot, left, right))
+    )(*in_hbm(left, right))
 
 
 def keep_kernel(place_ref, plan_ref, left_hbm, right_hbm, kept_ref, left_ref, right_ref, sems):
@@ -262,22 +239,16 @@
     )(plan, arrived)
 
 
-def pick_kernel(place_ref, plan_ref, kept_ref, roots_ref, left_ref, both_hbm, sem):
+def pick_kernel(place_ref, plan_ref, kept_ref, roots_ref, left_ref):
     own = plan_ref[HOME_ORIGIN + place_ref[1]] < 0
-
-    def take(source_ref):
-        copy = pltpu.make_async_copy(source_ref, both_hbm, sem)
-        copy.start()
-        left_ref[...] = source_ref[:, :ROWS]
-        copy.wait()
 
     @pl.when(own)
     def _():
-        take(kept_ref)
+        left_ref[...] = kept_ref[:, :ROWS]
 
     @pl.when(jnp.logical_not(own))
     def _():
-        take(roots_ref)
+        left_ref[...] = roots_ref[:, :ROWS]
 
 
 def pick(place, plan, kept, roots):
@@ -286,15 +257,42 @@
     return pl.pallas_call(
         pick_kernel,
         in_specs=[smem, smem, vmem, vmem],
-        out_specs=[vmem, pl.BlockSpec(memory_space=pltpu.HBM)],
-        out_shape=[
-            jax.ShapeDtypeStruct((kept.shape[0], ROWS, LANES), BF16),
-            pltpu.HBM(kept.shape, BF16),
-        ],
-        scratch_shapes=[pltpu.SemaphoreType.DMA],
+        out_specs=vmem,
+        out_shape=jax.ShapeDtypeStruct((kept.shape[0], ROWS, LANES), BF16),
         compiler_params=params(8),
         name="pick",
     )(place, plan, kept, roots)
+
+
+def hold_kernel(place_ref, plan_ref, before_ref, kept_ref, roots_ref, both_hbm, sem):
+    del before_ref
+    own = plan_ref[HOME_ORIGIN + place_ref[1]] < 0
+
+    @pl.when(own)
+    def _():
+        copy = pltpu.make_async_copy(kept_ref, both_hbm, sem)
+        copy.start()
+        copy.wait()
+
+    @pl.when(jnp.logical_not(own))
+    def _():
+        copy = pltpu.make_async_copy(roots_ref, both_hbm, sem)
+        copy.start()
+        copy.wait()
+
+
+def hold(place, plan, before, kept, roots):
+    smem = pl.BlockSpec(memory_space=pltpu.SMEM)
+    anywhere = pl.BlockSpec(memory_space=pl.ANY)
+    return pl.pallas_call(
+        hold_kernel,
+        in_specs=[smem, smem, anywhere, anywhere, anywhere],
+        out_specs=pl.BlockSpec(memory_space=pltpu.HBM),
+        out_shape=pltpu.HBM(kept.shape, BF16),
+        scratch_shapes=[pltpu.SemaphoreType.DMA],
+        compiler_params=params(4),
+        name="hold",
+    )(place, plan, before, kept, roots)
 
 
 def gather_kernel(plan_ref, gradient_ref, out_ref):
@@ -539,16 +537,16 @@
     held_ref[0] = own_ref[...]
     for spare in range(slots - 1):
         held_ref[spare + 1] = products_ref[:, 2 * ROWS * spare : 2 * ROWS * (spare + 1)]
-    which = jnp.int32(0)
+    before = jnp.int32(0)
     for slot in range(slots):
         named = plan_ref[SOURCE + place_ref[1] * slots + slot] >= 0
         weight = jnp.where(named, 1.0 - decay_rate, 0.0).astype(F32)
         for copy in reads[slot]:
             copy.wait()
-        at_most = jnp.minimum(which, slots - 1)
+        held = jnp.where(before > 0, slot, 0)
         for index in range(pieces):
             row, column = row_piece(index)
-            piece = held_ref[at_most, index].astype(F32)
+            piece = held_ref[held, index].astype(F32)
             for part in range(2):
                 at = (slot, pl.ds(row, TILE), pl.ds(column + part * width, width))
                 product = piece[part * TILE : (part + 1) * TILE]
@@ -557,7 +555,7 @@
             right_new[at] = decay_rate * right_ref[at] + weight * piece[ROWS:]
         for copy in writes[slot]:
             copy.start()
-        which += named.astype(jnp.int32)
+        before += named.astype(jnp.int32)
     for slot in range(slots):
         for copy in writes[slot]:
             copy.wait()
@@ -602,8 +600,10 @@
     def shift(value, by):
         return lax.ppermute(value, "rep", [(i, (i + by) % size) for i in range(size)])
 
-    down = [share, shift(share, -1)]
-    up = [share, *anchor(shift(share, 1))]
+    up, down = [share], [share]
+    first = anchor(shift(share, 1), shift(share, -1))
+    up.append(first[0])
+    down.append(first[1])
     for _ in range(size // 2 - 2):
         down.append(shift(down[-1], -1))
         up.append(shift(up[-1], 1))
@@ -647,12 +647,13 @@
     place = jnp.concatenate([rep, lax.axis_index("fsdp").astype(jnp.int32).reshape(1)])
     plan = make_plan(block_owner, block_slot)
 
-    spare = pack(place, block_owner, block_slot, left_root[0], right_root[0], owners)
+    spare = pack(left_root[0], right_root[0], owners)
     kept = keep(place, plan, left_root[0], right_root[0], owners)
     roots = exchange(route(plan, exchange(spare)))
-    left, both = pick(place, plan, kept, roots)
+    left = pick(place, plan, kept, roots)
     packed, left = lax.optimization_barrier((gather(plan, gradient), left))
     left_shares = ring_gather(left)
+    both = hold(place, plan, left_shares[1], kept, roots)
     outgoing, own = block_shares(rep, exchange(packed), both, left_shares[1:])
 
     arrived = exchange(outgoing)

time: 150 us -> 145 us (0.967)
  starting transfers between devices: 48.8 us -> 43.9 us
  waiting for transfers between devices: 51.2 us -> 52.9 us
  Pallas kernels: 26.7 us -> 25.2 us
    ppermute x2, starting transfers between devices: 4.3 us -> 0.68 us  [ring_gather(): return up + down[1:] + [lax.ppermute(passed, ('fsdp', 'rep'), pairs)]]
    ppermute x12, waiting for transfers between devices: 32.3 us -> 34.3 us  [shift(): lax.ppermute(value, 'rep', [(i, (i + by) % size) for i in range(size)])]
    pallas_call x1 -> x2, Pallas kernels: 2.66 us -> 3.47 us  [the longest x1 2.11 us: pack(): pl.pallas_call(pack_kernel, in_specs=[hbm, hbm], out_specs=hbm, out_shape...]
  transfers between devices with their start and end apart: 18 -> 18, of which waited for: 10 -> 11; matrix products, arithmetic and copies ran while one was open for 0% -> 0% of each run, Pallas kernels for 9% -> 10%
where the time goes in v5:
time: 145 us; the launch traced here: 144 us
  waiting for transfers between devices  52.9 us (36%)
  starting transfers between devices  43.9 us (30%)
  Pallas kernels  25.2 us (17%)
  blocking collectives  21.1 us (15%)
    ppermute x12, waiting for transfers between devices, shift(): lax.ppermute(value, 'rep', [(i, (i + by) % size) for i in range(size)])  34.3 us
    all_to_all x4, starting transfers between devices, exchange(): lax.all_to_all(value, 'fsdp', split_axis=0, concat_axis=0, tiled=True)  24.1 us
    all_to_all x1, blocking collectives, exchange(): lax.all_to_all(value, 'fsdp', split_axis=0, concat_axis=0, tiled=True)  21.1 us
    ppermute x12, starting transfers between devices, shift(): lax.ppermute(value, 'rep', [(i, (i + by) % size) for i in range(size)])  19.2 us
    all_to_all x4, waiting for transfers between devices, exchange(): lax.all_to_all(value, 'fsdp', split_axis=0, concat_axis=0, tiled=True)  18.6 us
    pallas_call x1, Pallas kernels, factors(): pl.pallas_call(factor_kernel, in_specs=[pl.BlockSpec(memory_space=pltpu.S...  4.26 us
    pallas_call x1, Pallas kernels, block_shares(): pl.pallas_call(block_kernel, in_specs=[pl.BlockSpec(memory_space=pltpu.SM...  4.24 us
    pallas_call x1, Pallas kernels, make_plan(): pl.pallas_call(plan_kernel, in_specs=[smem, smem], out_specs=smem, out_sh...  3.52 us
  transfers between devices with their start and end apart: 18, of which 11 were waited for; matrix products, arithmetic and copies ran while one was open for 0% of the time, Pallas kernels for 10%

profile of v5, /device:TPU:8, one launch (start us, length us, event | category | flops | bytes accessed | tf_op | source)
XLA Modules:
  0.0 144.4 jit_solution(732108838589384337)
XLA Ops:
  0.6 0.0 copy-start.6
  0.6 0.0 copy-start.7
  0.7 2.1 %pack.1 = bf16[32,128,128]{2,1,0:T(8,128)(2,1)} custom-call(bf16[3,128,1024]{2,1,0:T(8,128)(2,1)} %bitcast.4, bf16[3,1024,128]{2,1,0:T(8,128)(2,1)} %bitcast.6), custom_call_target="tpu_custom_call" | custom-call | tf_op jit(solution)/shard_map/pack/pallas_call | solution.py:164
  2.8 7.5 %all-to-all-start = ((bf16[32,128,128]{2,1,0:T(8,128)(2,1)}), bf16[32,128,128]{2,1,0:T(8,128)(2,1)S(1)}, u32[]{:S(2)}, u32[]{:S(2)}) async-start(bf16[32,128,128]{2,1,0:T(8,128)(2,1)} %pack.1), calls=%async_computation | async-start | bytes 2097152 | tf_op jit(solution)/shard_map/all_to_all | solution.py:639
  10.3 0.0 copy-done.6
  10.3 0.0 copy-done.7
  10.3 3.5 %make_plan.1.plan_ref = s32[256]{0:T(256)S(1)} custom-call(s32[32]{0:T(128)S(1)} %copy-done.6, s32[32]{0:T(128)S(1)} %copy-done.7), custom_call_target="tpu_custom_call" | custom-call | tf_op jit(solution)/shard_map/make_plan/pallas_call | solution.py:114
  13.9 0.0 copy-start.1
  13.9 0.0 copy-start
  13.9 12.0 %all-to-all-done.arrived_ref = bf16[32,128,128]{2,1,0:T(8,128)(2,1)S(1)} async-done(((bf16[32,128,128]{2,1,0:T(8,128)(2,1)}), bf16[32,128,128]{2,1,0:T(8,128)(2,1)S(1)}, u32[]{:S(2)}, u32[]{:S(2)}) %all-to-all-start) | async-done | bytes 1048608 | tf_op jit(solution)/shard_map/all_to_all | solution.py:639
  25.9 1.6 %route.1 = bf16[32,64,128]{2,1,0:T(8,128)(2,1)} custom-call(s32[256]{0:T(256)S(1)} %make_plan.1.plan_ref, bf16[32,128,128]{2,1,0:T(8,128)(2,1)S(1)} %all-to-all-done.arrived_ref), custom_call_target="tpu_custom_call" | custom-call | tf_op jit(solution)/shard_map/route/pallas_call | solution.py:228
  27.5 5.3 %all-to-all-start.1 = ((bf16[32,64,128]{2,1,0:T(8,128)(2,1)}), bf16[32,64,128]{2,1,0:T(8,128)(2,1)S(1)}, u32[]{:S(2)}, u32[]{:S(2)}) async-start(bf16[32,64,128]{2,1,0:T(8,128)(2,1)} %route.1), calls=%async_computation.1 | async-start | bytes 1048576 | tf_op jit(solution)/shard_map/all_to_all | solution.py:639
  32.8 0.1 pad_add_fusion.place_ref
  32.9 0.0 copy-start.3
  32.9 1.7 %keep.1.kept_ref = bf16[32,64,128]{2,1,0:T(8,128)(2,1)S(1)} custom-call(s32[2]{0:T(128)S(1)} %pad_add_fusion.place_ref, s32[256]{0:T(256)S(1)} %make_plan.1.plan_ref, bf16[3,128,1024]{2,1,0:T(8,128)(2,1)} %bitcast.5, bf16[3,1024,128]{2,1,0:T(8,128)(2,1)} %bitcast.7), custom_call_target="tpu_custom_call" | custom-call | tf_op jit(solution)/shard_map/keep/pallas_call | solution.py:199
  34.6 0.0 copy-done
  34.6 2.0 %gather.1 = bf16[32,32,1024]{2,1,0:T(8,128)(2,1)} custom-call(s32[256]{0:T(256)S(1)} %make_plan.1.plan_ref, bf16[32,32,1024]{2,1,0:T(8,128)(2,1)S(1)} %copy-done), custom_call_target="tpu_custom_call" | custom-call | tf_op jit(solution)/shard_map/gather/pallas_call | solution.py:304
  36.6 6.4 %all-to-all-done.1.roots_ref = bf16[32,64,128]{2,1,0:T(8,128)(2,1)S(1)} async-done(((bf16[32,64,128]{2,1,0:T(8,128)(2,1)}), bf16[32,64,128]{2,1,0:T(8,128)(2,1)S(1)}, u32[]{:S(2)}, u32[]{:S(2)}) %all-to-all-start.1) | async-done | bytes 524320 | tf_op jit(solution)/shard_map/all_to_all | solution.py:639
  43.0 0.0 copy-done.1
  43.0 0.0 copy-done.3
  43.0 0.6 pick.1
  43.6 5.9 %collective-permute-start.1 = (bf16[32,32,128]{2,1,0:T(8,128)(2,1)S(1)}, bf16[32,32,128]{2,1,0:T(8,128)(2,1)S(1)}, u32[]{:S(2)}, u32[]{:S(2)}) collective-permute-start(bf16[32,32,128]{2,1,0:T(8,128)(2,1)S(1)} %pick.1), channel_id=1, source_target_pairs={{0,7},{1,0},{2,1},{3,2},{4,3},{5,4},{6,5},{7,6},{8,15},{9,8},{10,9... | collective-permute-start | bytes 786440 | tf_op jit(solution)/shard_map/ppermute | solution.py:601
  49.5 0.0 collective-permute-start
  49.5 5.6 %all-to-all-start.2 = ((bf16[32,32,1024]{2,1,0:T(8,128)(2,1)}), bf16[32,32,1024]{2,1,0:T(8,128)(2,1)}, u32[]{:S(2)}, u32[]{:S(2)}) async-start(bf16[32,32,1024]{2,1,0:T(8,128)(2,1)} %gather.1), calls=%async_computation.2 | async-start | bytes 4194304 | tf_op jit(solution)/shard_map/all_to_all | solution.py:639
  55.1 0.4 collective-permute-done.1.refs_1_
  55.5 3.4 %collective-permute-done.refs_0_ = bf16[32,32,128]{2,1,0:T(8,128)(2,1)S(1)} collective-permute-done((bf16[32,32,128]{2,1,0:T(8,128)(2,1)S(1)}, bf16[32,32,128]{2,1,0:T(8,128)(2,1)S(1)}, u32[]{:S(2)}, u32[]{:S(2)}) %collective-permute-start) | collective-permute-done | bytes 262176 | tf_op jit(solution)/shard_map/ppermute | solution.py:601
  59.0 0.0 copy-start.4
  59.0 0.4 collective-permute-start.4
  59.3 1.7 %collective-permute-start.2 = (bf16[32,32,128]{2,1,0:T(8,128)(2,1)S(1)}, bf16[32,32,128]{2,1,0:T(8,128)(2,1)S(1)}, u32[]{:S(2)}, u32[]{:S(2)}) collective-permute-start(bf16[32,32,128]{2,1,0:T(8,128)(2,1)S(1)} %get-tuple-element.25.before_ref.refs_0_), channel_id=1, source_target_pairs={{0,1},{1,2},{2,3},{3,4},{4,5},{5,6},{6,7},{7,0},{8,9},{9,10},{10,1... | collective-permute-start | bytes 786440 | tf_op jit(solution)/shard_map/ppermute | solution.py:601
  61.0 0.6 collective-permute-start.6
  61.6 12.2 %collective-permute-done.4.refs_4_ = bf16[32,32,128]{2,1,0:T(8,128)(2,1)S(1)} collective-permute-done((bf16[32,32,128]{2,1,0:T(8,128)(2,1)S(1)}, bf16[32,32,128]{2,1,0:T(8,128)(2,1)S(1)}, u32[]{:S(2)}, u32[]{:S(2)}) %collective-permute-start.4) | collective-permute-done | bytes 262176 | tf_op jit(solution)/shard_map/ppermute | solution.py:601
  73.8 0.0 collective-permute-start.5
  73.8 0.0 collective-permute-done.2.refs_1_
  73.8 2.0 %collective-permute-start.3 = (bf16[32,32,128]{2,1,0:T(8,128)(2,1)S(1)}, bf16[32,32,128]{2,1,0:T(8,128)(2,1)S(1)}, u32[]{:S(2)}, u32[]{:S(2)}) collective-permute-start(bf16[32,32,128]{2,1,0:T(8,128)(2,1)S(1)} %collective-permute-done.2.refs_1_), channel_id=1, source_target_pairs={{0,1},{1,2},{2,3},{3,4},{4,5},{5,6},{6,7},{7,0},{8,9},{9,10},{10,1... | collective-permute-start | bytes 786440 | tf_op jit(solution)/shard_map/ppermute | solution.py:601
  75.8 0.0 copy-done.2
  75.9 0.0 copy-done.4
  75.9 1.4 hold.1.both_hbm
  77.2 0.0 collective-permute-done.6.refs_6_
  77.2 3.2 %collective-permute-done.5.refs_5_ = bf16[32,32,128]{2,1,0:T(8,128)(2,1)S(1)} collective-permute-done((bf16[32,32,128]{2,1,0:T(8,128)(2,1)S(1)}, bf16[32,32,128]{2,1,0:T(8,128)(2,1)S(1)}, u32[]{:S(2)}, u32[]{:S(2)}) %collective-permute-start.5) | collective-permute-done | bytes 262176 | tf_op jit(solution)/shard_map/ppermute | solution.py:601
  80.4 1.6 %collective-permute-done.3.refs_2_ = bf16[32,32,128]{2,1,0:T(8,128)(2,1)S(1)} collective-permute-done((bf16[32,32,128]{2,1,0:T(8,128)(2,1)S(1)}, bf16[32,32,128]{2,1,0:T(8,128)(2,1)S(1)}, u32[]{:S(2)}, u32[]{:S(2)}) %collective-permute-start.3) | collective-permute-done | bytes 262176 | tf_op jit(solution)/shard_map/ppermute | solution.py:601
  82.0 0.2 all-to-all-done.2.block_hbm
  82.2 4.2 %block_shares.1 = (bf16[32,112,128]{2,1,0:T(8,128)(2,1)S(1)}, bf16[32,64,128]{2,1,0:T(8,128)(2,1)S(1)}) custom-call(s32[1]{0:T(128)} %bitcast.rep_ref, bf16[32,32,1024]{2,1,0:T(8,128)(2,1)} %all-to-all-done.2.block_hbm, bf16[32,64,128]{2,1,0:T(8,128)(2,1)} %hold.1.both_hbm, bf16[32,32,128]{2,1,0:T(8,128)(2,1)S(1)} %get-tuple-element.25.before_ref.refs_0_, ...), custom_call_target="tpu_custom_call" | custom-call | flops 1073741824 | bytes 6291456 | tf_op jit(solution)/shard_map/block_shares/pallas_call | solution.py:395
  86.5 21.1 %all_to_all.25.arrived_ref = bf16[32,112,128]{2,1,0:T(8,128)(2,1)S(1)} all-to-all(bf16[32,112,128]{2,1,0:T(8,128)(2,1)S(1)} %get-tuple-element.27), channel_id=1, replica_groups=mesh['fsdp'=32,'rep'=8] {'fsdp'}, dimensions={0} | all-to-all | bytes 1835008 | tf_op jit(solution)/shard_map/all_to_all | solution.py:639
  107.6 1.4 collective-permute-start.8
  109.0 0.7 collective-permute-start.7
  109.7 1.6 %deal.1 = bf16[32,128,128]{2,1,0:T(8,128)(2,1)} custom-call(s32[256]{0:T(256)S(1)} %copy-done.2, bf16[32,112,128]{2,1,0:T(8,128)(2,1)S(1)} %all_to_all.25.arrived_ref), custom_call_target="tpu_custom_call" | custom-call | tf_op jit(solution)/shard_map/deal/pallas_call | solution.py:447
  111.3 5.6 %all-to-all-start.4 = ((bf16[32,128,128]{2,1,0:T(8,128)(2,1)}), bf16[32,128,128]{2,1,0:T(8,128)(2,1)}, u32[]{:S(2)}, u32[]{:S(2)}) async-start(bf16[32,128,128]{2,1,0:T(8,128)(2,1)} %deal.1), calls=%async_computation.4 | async-start | bytes 2097152 | tf_op jit(solution)/shard_map/all_to_all | solution.py:639
  116.9 0.0 collective-permute-done.8.refs_1_
  116.9 1.1 collective-permute-done.7.refs_0_
  118.0 0.0 copy-start.5
  118.0 0.0 collective-permute-start.9
  118.0 3.2 %collective-permute-start.11 = (bf16[33,32,128]{2,1,0:T(8,128)(2,1)S(1)}, bf16[33,32,128]{2,1,0:T(8,128)(2,1)S(1)}, u32[]{:S(2)}, u32[]{:S(2)}) collective-permute-start(bf16[33,32,128]{2,1,0:T(8,128)(2,1)S(1)} %get-tuple-element.37.refs_4_), channel_id=1, source_target_pairs={{0,7},{1,0},{2,1},{3,2},{4,3},{5,4},{6,5},{7,6},{8,15},{9,8},{10,9... | collective-permute-start | bytes 811016 | tf_op jit(solution)/shard_map/ppermute | solution.py:601
  121.3 0.1 collective-permute-start.13
  121.4 5.4 %collective-permute-done.9.refs_2_ = bf16[33,32,128]{2,1,0:T(8,128)(2,1)S(1)} collective-permute-done((bf16[33,32,128]{2,1,0:T(8,128)(2,1)S(1)}, bf16[33,32,128]{2,1,0:T(8,128)(2,1)S(1)}, u32[]{:S(2)}, u32[]{:S(2)}) %collective-permute-start.9) | collective-permute-done | bytes 270368 | tf_op jit(solution)/shard_map/ppermute | solution.py:601
  126.8 0.0 collective-permute-start.10
  126.8 7.0 %collective-permute-done.11.refs_5_ = bf16[33,32,128]{2,1,0:T(8,128)(2,1)S(1)} collective-permute-done((bf16[33,32,128]{2,1,0:T(8,128)(2,1)S(1)}, bf16[33,32,128]{2,1,0:T(8,128)(2,1)S(1)}, u32[]{:S(2)}, u32[]{:S(2)}) %collective-permute-start.11) | collective-permute-done | bytes 270368 | tf_op jit(solution)/shard_map/ppermute | solution.py:601
  133.8 3.8 %collective-permute-start.12 = (bf16[33,32,128]{2,1,0:T(8,128)(2,1)S(1)}, bf16[33,32,128]{2,1,0:T(8,128)(2,1)S(1)}, u32[]{:S(2)}, u32[]{:S(2)}) collective-permute-start(bf16[33,32,128]{2,1,0:T(8,128)(2,1)S(1)} %collective-permute-done.11.refs_5_), channel_id=1, source_target_pairs={{0,7},{1,0},{2,1},{3,2},{4,3},{5,4},{6,5},{7,6},{8,15},{9,8},{10,9... | collective-permute-start | bytes 811016 | tf_op jit(solution)/shard_map/ppermute | solution.py:601
  137.7 0.0 all-to-all-done.4.products_ref
  137.7 0.0 copy-done.5
  137.7 4.3 %factors.1 = (f32[1,3,128,1024]{3,2,1,0:T(8,128)}, f32[1,3,1024,128]{3,2,1,0:T(8,128)}) custom-call(s32[256]{0:T(256)S(1)} %copy-done.2, s32[2]{0:T(128)S(1)} %copy-done.5, bf16[32,64,128]{2,1,0:T(8,128)(2,1)S(1)} %get-tuple-element.30.own_ref, bf16[32,128,128]{2,1,0:T(8,128)(2,1)} %all-to-all-done.4.products_ref, f32[1,3,128,1024]{3,2,1,0:T(8,128)} %left_hbm.1, ...), custom_call_target="tpu_custom_call" | custom-call | flops 6291456 | bytes 15728640 | tf_op jit(solution)/shard_map/factors/pallas_call | solution.py:567
  141.9 0.0 collective-permute-done.13.refs_7_
  142.0 0.0 collective-permute-done.10.refs_3_
  142.0 0.0 collective-permute-done.12.refs_6_
  142.0 2.2 %finish.1 = bf16[32,32,1024]{2,1,0:T(8,128)(2,1)} custom-call(s32[1]{0:T(128)} %bitcast.rep_ref, s32[256]{0:T(256)S(1)} %copy-done.2, bf16[33,32,128]{2,1,0:T(8,128)(2,1)S(1)} %named.1.refs_0_, bf16[33,32,128]{2,1,0:T(8,128)(2,1)S(1)} %get-tuple-element.34.refs_1_, bf16[33,32,128]{2,1,0:T(8,128)(2,1)S(1)} %collective-permute-done.9.refs_2_, ...), custom_call_target="tpu_custom_call" | custom-call | tf_op jit(solution)/shard_map/finish/pallas_call | solution.py:491
  (6 shorter events, 0.1 us)
Async XLA Ops:
  0.6 9.7 %copy-start.6 = (s32[32]{0:T(128)S(1)}, s32[32]{0:T(128)}, u32[]{:S(2)}) copy-start(s32[32]{0:T(128)} %owner_ref.1) | copy-start | bytes 388
  0.6 9.7 %copy-start.7 = (s32[32]{0:T(128)S(1)}, s32[32]{0:T(128)}, u32[]{:S(2)}) copy-start(s32[32]{0:T(128)} %slot_ref.1) | copy-start | bytes 388
  2.8 23.1 %all-to-all-start = ((bf16[32,128,128]{2,1,0:T(8,128)(2,1)}), bf16[32,128,128]{2,1,0:T(8,128)(2,1)S(1)}, u32[]{:S(2)}, u32[]{:S(2)}) async-start(bf16[32,128,128]{2,1,0:T(8,128)(2,1)} %pack.1), calls=%async_computation | async-start | bytes 2097152 | tf_op jit(solution)/shard_map/all_to_all | solution.py:639
  13.9 29.1 %copy-start.1 = (s32[256]{0:T(256)}, s32[256]{0:T(256)S(1)}, u32[]{:S(2)}) copy-start(s32[256]{0:T(256)S(1)} %make_plan.1.plan_ref) | copy-start | bytes 3076
  13.9 20.7 %copy-start = (bf16[32,32,1024]{2,1,0:T(8,128)(2,1)S(1)}, bf16[32,32,1024]{2,1,0:T(8,128)(2,1)}, u32[]{:S(2)}) copy-start(bf16[32,32,1024]{2,1,0:T(8,128)(2,1)} %gradient_ref.1) | copy-start | bytes 6291460
  27.5 15.5 %all-to-all-start.1 = ((bf16[32,64,128]{2,1,0:T(8,128)(2,1)}), bf16[32,64,128]{2,1,0:T(8,128)(2,1)S(1)}, u32[]{:S(2)}, u32[]{:S(2)}) async-start(bf16[32,64,128]{2,1,0:T(8,128)(2,1)} %route.1), calls=%async_computation.1 | async-start | bytes 1048576 | tf_op jit(solution)/shard_map/all_to_all | solution.py:639
  32.9 10.1 %copy-start.3 = (s32[2]{0:T(128)}, s32[2]{0:T(128)S(1)}, u32[]{:S(2)}) copy-start(s32[2]{0:T(128)S(1)} %pad_add_fusion.place_ref) | copy-start | bytes 28
  43.6 12.0 %collective-permute-start.1 = (bf16[32,32,128]{2,1,0:T(8,128)(2,1)S(1)}, bf16[32,32,128]{2,1,0:T(8,128)(2,1)S(1)}, u32[]{:S(2)}, u32[]{:S(2)}) collective-permute-start(bf16[32,32,128]{2,1,0:T(8,128)(2,1)S(1)} %pick.1), channel_id=1, source_target_pairs={{0,7},{1,0},{2,1},{3,2},{4,3},{5,4},{6,5},{7,6},{8,15},{9,8},{10,9... | collective-permute-start | bytes 786440 | tf_op jit(solution)/shard_map/ppermute | solution.py:601
  49.5 9.5 %collective-permute-start = (bf16[32,32,128]{2,1,0:T(8,128)(2,1)S(1)}, bf16[32,32,128]{2,1,0:T(8,128)(2,1)S(1)}, u32[]{:S(2)}, u32[]{:S(2)}) collective-permute-start(bf16[32,32,128]{2,1,0:T(8,128)(2,1)S(1)} %pick.1), channel_id=1, source_target_pairs={{0,1},{1,2},{2,3},{3,4},{4,5},{5,6},{6,7},{7,0},{8,9},{9,10},{10,1... | collective-permute-start | bytes 786440 | tf_op jit(solution)/shard_map/ppermute | solution.py:601
  49.5 32.7 %all-to-all-start.2 = ((bf16[32,32,1024]{2,1,0:T(8,128)(2,1)}), bf16[32,32,1024]{2,1,0:T(8,128)(2,1)}, u32[]{:S(2)}, u32[]{:S(2)}) async-start(bf16[32,32,1024]{2,1,0:T(8,128)(2,1)} %gather.1), calls=%async_computation.2 | async-start | bytes 4194304 | tf_op jit(solution)/shard_map/all_to_all | solution.py:639
  59.0 16.9 %copy-start.2 = (s32[256]{0:T(256)S(1)}, s32[256]{0:T(256)}, u32[]{:S(2)}) copy-start(s32[256]{0:T(256)} %copy-done.1) | copy-start | bytes 3076
  59.0 16.9 %copy-start.4 = (s32[2]{0:T(128)S(1)}, s32[2]{0:T(128)}, u32[]{:S(2)}) copy-start(s32[2]{0:T(128)} %copy-done.3) | copy-start | bytes 28
  59.0 14.9 %collective-permute-start.4 = (bf16[32,32,128]{2,1,0:T(8,128)(2,1)S(1)}, bf16[32,32,128]{2,1,0:T(8,128)(2,1)S(1)}, u32[]{:S(2)}, u32[]{:S(2)}) collective-permute-start(bf16[32,32,128]{2,1,0:T(8,128)(2,1)S(1)} %get-tuple-element.26.refs_3_), channel_id=1, source_target_pairs={{0,7},{1,0},{2,1},{3,2},{4,3},{5,4},{6,5},{7,6},{8,15},{9,8},{10,9... | collective-permute-start | bytes 786440 | tf_op jit(solution)/shard_map/ppermute | solution.py:601
  59.3 14.5 %collective-permute-start.2 = (bf16[32,32,128]{2,1,0:T(8,128)(2,1)S(1)}, bf16[32,32,128]{2,1,0:T(8,128)(2,1)S(1)}, u32[]{:S(2)}, u32[]{:S(2)}) collective-permute-start(bf16[32,32,128]{2,1,0:T(8,128)(2,1)S(1)} %get-tuple-element.25.before_ref.refs_0_), channel_id=1, source_target_pairs={{0,1},{1,2},{2,3},{3,4},{4,5},{5,6},{6,7},{7,0},{8,9},{9,10},{10,1... | collective-permute-start | bytes 786440 | tf_op jit(solution)/shard_map/ppermute | solution.py:601
  61.0 16.2 %collective-permute-start.6 = (bf16[32,32,128]{2,1,0:T(8,128)(2,1)S(1)}, bf16[32,32,128]{2,1,0:T(8,128)(2,1)S(1)}, u32[]{:S(2)}, u32[]{:S(2)}) collective-permute-start(bf16[32,32,128]{2,1,0:T(8,128)(2,1)S(1)} %broadcast_select_fusion.1), channel_id=1, source_target_pairs={{0,3},{1,4},{2,5},{3,6},{4,7},{5,0},{6,1},{7,2},{8,13},{9,14},{10,... | collective-permute-start | bytes 786440 | tf_op jit(solution)/shard_map/ppermute | solution.py:617
  73.8 6.6 %collective-permute-start.5 = (bf16[32,32,128]{2,1,0:T(8,128)(2,1)S(1)}, bf16[32,32,128]{2,1,0:T(8,128)(2,1)S(1)}, u32[]{:S(2)}, u32[]{:S(2)}) collective-permute-start(bf16[32,32,128]{2,1,0:T(8,128)(2,1)S(1)} %collective-permute-done.4.refs_4_), channel_id=1, source_target_pairs={{0,7},{1,0},{2,1},{3,2},{4,3},{5,4},{6,5},{7,6},{8,15},{9,8},{10,9... | collective-permute-start | bytes 786440 | tf_op jit(solution)/shard_map/ppermute | solution.py:601
  73.8 8.2 %collective-permute-start.3 = (bf16[32,32,128]{2,1,0:T(8,128)(2,1)S(1)}, bf16[32,32,128]{2,1,0:T(8,128)(2,1)S(1)}, u32[]{:S(2)}, u32[]{:S(2)}) collective-permute-start(bf16[32,32,128]{2,1,0:T(8,128)(2,1)S(1)} %collective-permute-done.2.refs_1_), channel_id=1, source_target_pairs={{0,1},{1,2},{2,3},{3,4},{4,5},{5,6},{6,7},{7,0},{8,9},{9,10},{10,1... | collective-permute-start | bytes 786440 | tf_op jit(solution)/shard_map/ppermute | solution.py:601
  107.6 9.3 %collective-permute-start.8 = (bf16[33,32,128]{2,1,0:T(8,128)(2,1)S(1)}, bf16[33,32,128]{2,1,0:T(8,128)(2,1)S(1)}, u32[]{:S(2)}, u32[]{:S(2)}) collective-permute-start(bf16[33,32,128]{2,1,0:T(8,128)(2,1)S(1)} %named.1.refs_0_), channel_id=1, source_target_pairs={{0,7},{1,0},{2,1},{3,2},{4,3},{5,4},{6,5},{7,6},{8,15},{9,8},{10,9... | collective-permute-start | bytes 811016 | tf_op jit(solution)/shard_map/ppermute | solution.py:601
  109.0 9.0 %collective-permute-start.7 = (bf16[33,32,128]{2,1,0:T(8,128)(2,1)S(1)}, bf16[33,32,128]{2,1,0:T(8,128)(2,1)S(1)}, u32[]{:S(2)}, u32[]{:S(2)}) collective-permute-start(bf16[33,32,128]{2,1,0:T(8,128)(2,1)S(1)} %named.1.refs_0_), channel_id=1, source_target_pairs={{0,1},{1,2},{2,3},{3,4},{4,5},{5,6},{6,7},{7,0},{8,9},{9,10},{10,1... | collective-permute-start | bytes 811016 | tf_op jit(solution)/shard_map/ppermute | solution.py:601
  111.3 26.3 %all-to-all-start.4 = ((bf16[32,128,128]{2,1,0:T(8,128)(2,1)}), bf16[32,128,128]{2,1,0:T(8,128)(2,1)}, u32[]{:S(2)}, u32[]{:S(2)}) async-start(bf16[32,128,128]{2,1,0:T(8,128)(2,1)} %deal.1), calls=%async_computation.4 | async-start | bytes 2097152 | tf_op jit(solution)/shard_map/all_to_all | solution.py:639
  118.0 19.7 %copy-start.5 = (s32[2]{0:T(128)S(1)}, s32[2]{0:T(128)}, u32[]{:S(2)}) copy-start(s32[2]{0:T(128)} %copy-done.3) | copy-start | bytes 28
  118.0 8.8 %collective-permute-start.9 = (bf16[33,32,128]{2,1,0:T(8,128)(2,1)S(1)}, bf16[33,32,128]{2,1,0:T(8,128)(2,1)S(1)}, u32[]{:S(2)}, u32[]{:S(2)}) collective-permute-start(bf16[33,32,128]{2,1,0:T(8,128)(2,1)S(1)} %get-tuple-element.34.refs_1_), channel_id=1, source_target_pairs={{0,1},{1,2},{2,3},{3,4},{4,5},{5,6},{6,7},{7,0},{8,9},{9,10},{10,1... | collective-permute-start | bytes 811016 | tf_op jit(solution)/shard_map/ppermute | solution.py:601
  118.0 15.8 %collective-permute-start.11 = (bf16[33,32,128]{2,1,0:T(8,128)(2,1)S(1)}, bf16[33,32,128]{2,1,0:T(8,128)(2,1)S(1)}, u32[]{:S(2)}, u32[]{:S(2)}) collective-permute-start(bf16[33,32,128]{2,1,0:T(8,128)(2,1)S(1)} %get-tuple-element.37.refs_4_), channel_id=1, source_target_pairs={{0,7},{1,0},{2,1},{3,2},{4,3},{5,4},{6,5},{7,6},{8,15},{9,8},{10,9... | collective-permute-start | bytes 811016 | tf_op jit(solution)/shard_map/ppermute | solution.py:601
  121.3 20.7 %collective-permute-start.13 = (bf16[33,32,128]{2,1,0:T(8,128)(2,1)S(1)}, bf16[33,32,128]{2,1,0:T(8,128)(2,1)S(1)}, u32[]{:S(2)}, u32[]{:S(2)}) collective-permute-start(bf16[33,32,128]{2,1,0:T(8,128)(2,1)S(1)} %broadcast_select_fusion), channel_id=1, source_target_pairs={{0,3},{1,4},{2,5},{3,6},{4,7},{5,0},{6,1},{7,2},{8,13},{9,14},{10,... | collective-permute-start | bytes 811016 | tf_op jit(solution)/shard_map/ppermute | solution.py:617
  126.8 15.2 %collective-permute-start.10 = (bf16[33,32,128]{2,1,0:T(8,128)(2,1)S(1)}, bf16[33,32,128]{2,1,0:T(8,128)(2,1)S(1)}, u32[]{:S(2)}, u32[]{:S(2)}) collective-permute-start(bf16[33,32,128]{2,1,0:T(8,128)(2,1)S(1)} %collective-permute-done.9.refs_2_), channel_id=1, source_target_pairs={{0,1},{1,2},{2,3},{3,4},{4,5},{5,6},{6,7},{7,0},{8,9},{9,10},{10,1... | collective-permute-start | bytes 811016 | tf_op jit(solution)/shard_map/ppermute | solution.py:601
  133.8 8.1 %collective-permute-start.12 = (bf16[33,32,128]{2,1,0:T(8,128)(2,1)S(1)}, bf16[33,32,128]{2,1,0:T(8,128)(2,1)S(1)}, u32[]{:S(2)}, u32[]{:S(2)}) collective-permute-start(bf16[33,32,128]{2,1,0:T(8,128)(2,1)S(1)} %collective-permute-done.11.refs_5_), channel_id=1, source_target_pairs={{0,7},{1,0},{2,1},{3,2},{4,3},{5,4},{6,5},{7,6},{8,15},{9,8},{10,9... | collective-permute-start | bytes 811016 | tf_op jit(solution)/shard_map/ppermute | solution.py:601

commit v6 on v5

--- a/solution.py
+++ b/solution.py
@@ -211,20 +211,24 @@
     )(place, plan, *in_hbm(left, right))
 
 
-def route_kernel(plan_ref, arrived_ref, out_hbm, sems):
+def route_kernel(plan_ref, arrived_ref, out_hbm, out_ref, sems):
+    homes = out_ref.shape[0]
+    parts = sems.shape[0]
     copies = []
-    for home in range(out_hbm.shape[0]):
-        origin = jnp.maximum(plan_ref[HOME_ORIGIN + home], 0)
-        start = pl.multiple_of(lax.rem(origin, 2) * (2 * ROWS), 2 * ROWS)
-        source = arrived_ref.at[lax.div(origin, 2), pl.ds(start, 2 * ROWS)]
-        copies.append(pltpu.make_async_copy(source, out_hbm.at[home], sems.at[home]))
+    for part in range(parts):
+        lines = pl.ds(part * (homes // parts), homes // parts)
+        for home in range(part * (homes // parts), (part + 1) * (homes // parts)):
+            origin = jnp.maximum(plan_ref[HOME_ORIGIN + home], 0)
+            start = pl.multiple_of(lax.rem(origin, 2) * (2 * ROWS), 2 * ROWS)
+            out_ref[home] = arrived_ref[lax.div(origin, 2), pl.ds(start, 2 * ROWS), :]
+        copies.append(pltpu.make_async_copy(out_ref.at[lines], out_hbm.at[lines], sems.at[part]))
         copies[-1].start()
     for copy in copies:
         copy.wait()
 
 
 def route(plan, arrived):
-    homes = arrived.shape[0]
+    shape = (arrived.shape[0], 2 * ROWS, LANES)
     return pl.pallas_call(
         route_kernel,
         in_specs=[
@@ -232,8 +236,8 @@
             pl.BlockSpec(memory_space=pltpu.VMEM),
         ],
         out_specs=pl.BlockSpec(memory_space=pltpu.HBM),
-        out_shape=pltpu.HBM((homes, 2 * ROWS, LANES), BF16),
-        scratch_shapes=[pltpu.SemaphoreType.DMA((homes,))],
+        out_shape=pltpu.HBM(shape, BF16),
+        scratch_shapes=[pltpu.VMEM(shape, BF16), pltpu.SemaphoreType.DMA((4,))],
         compiler_params=params(8),
         name="route",
     )(plan, arrived)
@@ -414,13 +418,10 @@
 
 def named_kernel(arrived_ref, update_ref):
     count = arrived_ref.shape[0]
-    line = lax.broadcasted_iota(jnp.int32, (ROWS, LANES), 0)
-    sums = jnp.zeros((ROWS, LANES), F32)
-    for index in range(count):
-        update_ref[index] = arrived_ref[index, :ROWS, :]
-        tail = arrived_ref[index, 3 * ROWS :, :].astype(F32)
-        sums = jnp.where(line == index, jnp.concatenate([tail, tail], axis=0), sums)
-    update_ref[count] = sums.astype(BF16)
+    update_ref[:count] = arrived_ref[:, :ROWS, :]
+    tails = arrived_ref[:, 3 * ROWS :, :].astype(F32)
+    line = lax.broadcasted_iota(jnp.int32, tails.shape, 1)
+    update_ref[count] = jnp.sum(jnp.where(line == 0, tails, 0.0), axis=1).astype(BF16)
 
 
 def named(arrived):

time: 145 us -> 145 us (level)
  no operation moved by 1% of the time
where the time goes in v6:
time: 145 us; the launch traced here: 144 us
  waiting for transfers between devices  52.9 us (36%)
  starting transfers between devices  43.9 us (30%)
  Pallas kernels  25 us (17%)
  blocking collectives  21.1 us (15%)
    ppermute x12, waiting for transfers between devices, shift(): lax.ppermute(value, 'rep', [(i, (i + by) % size) for i in range(size)])  34.3 us
    all_to_all x4, starting transfers between devices, exchange(): lax.all_to_all(value, 'fsdp', split_axis=0, concat_axis=0, tiled=True)  24.1 us
    all_to_all x1, blocking collectives, exchange(): lax.all_to_all(value, 'fsdp', split_axis=0, concat_axis=0, tiled=True)  21.1 us
    ppermute x12, starting transfers between devices, shift(): lax.ppermute(value, 'rep', [(i, (i + by) % size) for i in range(size)])  19.2 us
    all_to_all x4, waiting for transfers between devices, exchange(): lax.all_to_all(value, 'fsdp', split_axis=0, concat_axis=0, tiled=True)  18.6 us
    pallas_call x1, Pallas kernels, factors(): pl.pallas_call(factor_kernel, in_specs=[pl.BlockSpec(memory_space=pltpu.S...  4.26 us
    pallas_call x1, Pallas kernels, block_shares(): pl.pallas_call(block_kernel, in_specs=[pl.BlockSpec(memory_space=pltpu.SM...  4.24 us
    pallas_call x1, Pallas kernels, make_plan(): pl.pallas_call(plan_kernel, in_specs=[smem, smem], out_specs=smem, out_sh...  3.52 us
  transfers between devices with their start and end apart: 18, of which 11 were waited for; matrix products, arithmetic and copies ran while one was open for 0% of the time, Pallas kernels for 10%

profile of v6, /device:TPU:8, one launch (start us, length us, event | category | flops | bytes accessed | tf_op | source)
XLA Modules:
  0.0 144.2 jit_solution(4096780522822078506)
XLA Ops:
  0.6 0.0 copy-start.6
  0.6 0.0 copy-start.7
  0.7 2.1 %pack.1 = bf16[32,128,128]{2,1,0:T(8,128)(2,1)} custom-call(bf16[3,128,1024]{2,1,0:T(8,128)(2,1)} %bitcast.4, bf16[3,1024,128]{2,1,0:T(8,128)(2,1)} %bitcast.6), custom_call_target="tpu_custom_call" | custom-call | tf_op jit(solution)/shard_map/pack/pallas_call | solution.py:164
  2.8 7.5 %all-to-all-start = ((bf16[32,128,128]{2,1,0:T(8,128)(2,1)}), bf16[32,128,128]{2,1,0:T(8,128)(2,1)S(1)}, u32[]{:S(2)}, u32[]{:S(2)}) async-start(bf16[32,128,128]{2,1,0:T(8,128)(2,1)} %pack.1), calls=%async_computation | async-start | bytes 2097152 | tf_op jit(solution)/shard_map/all_to_all | solution.py:640
  10.3 0.0 copy-done.6
  10.3 0.0 copy-done.7
  10.3 3.5 %make_plan.1.plan_ref = s32[256]{0:T(256)S(1)} custom-call(s32[32]{0:T(128)S(1)} %copy-done.6, s32[32]{0:T(128)S(1)} %copy-done.7), custom_call_target="tpu_custom_call" | custom-call | tf_op jit(solution)/shard_map/make_plan/pallas_call | solution.py:114
  13.9 0.0 copy-start.1
  13.9 0.0 copy-start
  13.9 12.0 %all-to-all-done.arrived_ref = bf16[32,128,128]{2,1,0:T(8,128)(2,1)S(1)} async-done(((bf16[32,128,128]{2,1,0:T(8,128)(2,1)}), bf16[32,128,128]{2,1,0:T(8,128)(2,1)S(1)}, u32[]{:S(2)}, u32[]{:S(2)}) %all-to-all-start) | async-done | bytes 1048608 | tf_op jit(solution)/shard_map/all_to_all | solution.py:640
  25.9 1.4 route.1
  27.3 5.3 %all-to-all-start.1 = ((bf16[32,64,128]{2,1,0:T(8,128)(2,1)}), bf16[32,64,128]{2,1,0:T(8,128)(2,1)S(1)}, u32[]{:S(2)}, u32[]{:S(2)}) async-start(bf16[32,64,128]{2,1,0:T(8,128)(2,1)} %route.1), calls=%async_computation.1 | async-start | bytes 1048576 | tf_op jit(solution)/shard_map/all_to_all | solution.py:640
  32.6 0.1 pad_add_fusion.place_ref
  32.7 0.0 copy-start.3
  32.7 1.7 %keep.1.kept_ref = bf16[32,64,128]{2,1,0:T(8,128)(2,1)S(1)} custom-call(s32[2]{0:T(128)S(1)} %pad_add_fusion.place_ref, s32[256]{0:T(256)S(1)} %make_plan.1.plan_ref, bf16[3,128,1024]{2,1,0:T(8,128)(2,1)} %bitcast.5, bf16[3,1024,128]{2,1,0:T(8,128)(2,1)} %bitcast.7), custom_call_target="tpu_custom_call" | custom-call | tf_op jit(solution)/shard_map/keep/pallas_call | solution.py:199
  34.4 0.0 copy-done
  34.4 2.0 %gather.1 = bf16[32,32,1024]{2,1,0:T(8,128)(2,1)} custom-call(s32[256]{0:T(256)S(1)} %make_plan.1.plan_ref, bf16[32,32,1024]{2,1,0:T(8,128)(2,1)S(1)} %copy-done), custom_call_target="tpu_custom_call" | custom-call | tf_op jit(solution)/shard_map/gather/pallas_call | solution.py:308
  36.4 6.4 %all-to-all-done.1.roots_ref = bf16[32,64,128]{2,1,0:T(8,128)(2,1)S(1)} async-done(((bf16[32,64,128]{2,1,0:T(8,128)(2,1)}), bf16[32,64,128]{2,1,0:T(8,128)(2,1)S(1)}, u32[]{:S(2)}, u32[]{:S(2)}) %all-to-all-start.1) | async-done | bytes 524320 | tf_op jit(solution)/shard_map/all_to_all | solution.py:640
  42.8 0.0 copy-done.1
  42.8 0.0 copy-done.3
  42.8 0.6 pick.1
  43.4 5.9 %collective-permute-start.1 = (bf16[32,32,128]{2,1,0:T(8,128)(2,1)S(1)}, bf16[32,32,128]{2,1,0:T(8,128)(2,1)S(1)}, u32[]{:S(2)}, u32[]{:S(2)}) collective-permute-start(bf16[32,32,128]{2,1,0:T(8,128)(2,1)S(1)} %pick.1), channel_id=1, source_target_pairs={{0,7},{1,0},{2,1},{3,2},{4,3},{5,4},{6,5},{7,6},{8,15},{9,8},{10,9... | collective-permute-start | bytes 786440 | tf_op jit(solution)/shard_map/ppermute | solution.py:602
  49.3 0.0 collective-permute-start
  49.3 5.6 %all-to-all-start.2 = ((bf16[32,32,1024]{2,1,0:T(8,128)(2,1)}), bf16[32,32,1024]{2,1,0:T(8,128)(2,1)}, u32[]{:S(2)}, u32[]{:S(2)}) async-start(bf16[32,32,1024]{2,1,0:T(8,128)(2,1)} %gather.1), calls=%async_computation.2 | async-start | bytes 4194304 | tf_op jit(solution)/shard_map/all_to_all | solution.py:640
  54.9 0.4 collective-permute-done.1.refs_1_
  55.3 3.4 %collective-permute-done.refs_0_ = bf16[32,32,128]{2,1,0:T(8,128)(2,1)S(1)} collective-permute-done((bf16[32,32,128]{2,1,0:T(8,128)(2,1)S(1)}, bf16[32,32,128]{2,1,0:T(8,128)(2,1)S(1)}, u32[]{:S(2)}, u32[]{:S(2)}) %collective-permute-start) | collective-permute-done | bytes 262176 | tf_op jit(solution)/shard_map/ppermute | solution.py:602
  58.7 0.0 copy-start.2
  58.7 0.4 collective-permute-start.4
  59.1 1.7 %collective-permute-start.2 = (bf16[32,32,128]{2,1,0:T(8,128)(2,1)S(1)}, bf16[32,32,128]{2,1,0:T(8,128)(2,1)S(1)}, u32[]{:S(2)}, u32[]{:S(2)}) collective-permute-start(bf16[32,32,128]{2,1,0:T(8,128)(2,1)S(1)} %get-tuple-element.25.before_ref.refs_0_), channel_id=1, source_target_pairs={{0,1},{1,2},{2,3},{3,4},{4,5},{5,6},{6,7},{7,0},{8,9},{9,10},{10,1... | collective-permute-start | bytes 786440 | tf_op jit(solution)/shard_map/ppermute | solution.py:602
  60.8 0.6 collective-permute-start.6
  61.4 12.2 %collective-permute-done.4.refs_4_ = bf16[32,32,128]{2,1,0:T(8,128)(2,1)S(1)} collective-permute-done((bf16[32,32,128]{2,1,0:T(8,128)(2,1)S(1)}, bf16[32,32,128]{2,1,0:T(8,128)(2,1)S(1)}, u32[]{:S(2)}, u32[]{:S(2)}) %collective-permute-start.4) | collective-permute-done | bytes 262176 | tf_op jit(solution)/shard_map/ppermute | solution.py:602
  73.6 0.0 collective-permute-start.5
  73.6 0.0 collective-permute-done.2.refs_1_
  73.6 2.0 %collective-permute-start.3 = (bf16[32,32,128]{2,1,0:T(8,128)(2,1)S(1)}, bf16[32,32,128]{2,1,0:T(8,128)(2,1)S(1)}, u32[]{:S(2)}, u32[]{:S(2)}) collective-permute-start(bf16[32,32,128]{2,1,0:T(8,128)(2,1)S(1)} %collective-permute-done.2.refs_1_), channel_id=1, source_target_pairs={{0,1},{1,2},{2,3},{3,4},{4,5},{5,6},{6,7},{7,0},{8,9},{9,10},{10,1... | collective-permute-start | bytes 786440 | tf_op jit(solution)/shard_map/ppermute | solution.py:602
  75.6 0.0 copy-done.2
  75.6 0.0 copy-done.4
  75.6 1.4 hold.1.both_hbm
  77.0 0.0 collective-permute-done.6.refs_6_
  77.0 3.2 %collective-permute-done.5.refs_5_ = bf16[32,32,128]{2,1,0:T(8,128)(2,1)S(1)} collective-permute-done((bf16[32,32,128]{2,1,0:T(8,128)(2,1)S(1)}, bf16[32,32,128]{2,1,0:T(8,128)(2,1)S(1)}, u32[]{:S(2)}, u32[]{:S(2)}) %collective-permute-start.5) | collective-permute-done | bytes 262176 | tf_op jit(solution)/shard_map/ppermute | solution.py:602
  80.2 1.6 %collective-permute-done.3.refs_2_ = bf16[32,32,128]{2,1,0:T(8,128)(2,1)S(1)} collective-permute-done((bf16[32,32,128]{2,1,0:T(8,128)(2,1)S(1)}, bf16[32,32,128]{2,1,0:T(8,128)(2,1)S(1)}, u32[]{:S(2)}, u32[]{:S(2)}) %collective-permute-start.3) | collective-permute-done | bytes 262176 | tf_op jit(solution)/shard_map/ppermute | solution.py:602
  81.8 0.2 all-to-all-done.2.block_hbm
  82.0 4.2 %block_shares.1 = (bf16[32,112,128]{2,1,0:T(8,128)(2,1)S(1)}, bf16[32,64,128]{2,1,0:T(8,128)(2,1)S(1)}) custom-call(s32[1]{0:T(128)} %bitcast.rep_ref, bf16[32,32,1024]{2,1,0:T(8,128)(2,1)} %all-to-all-done.2.block_hbm, bf16[32,64,128]{2,1,0:T(8,128)(2,1)} %hold.1.both_hbm, bf16[32,32,128]{2,1,0:T(8,128)(2,1)S(1)} %get-tuple-element.25.before_ref.refs_0_, ...), custom_call_target="tpu_custom_call" | custom-call | flops 1073741824 | bytes 6291456 | tf_op jit(solution)/shard_map/block_shares/pallas_call | solution.py:399
  86.3 21.1 %all_to_all.25.arrived_ref = bf16[32,112,128]{2,1,0:T(8,128)(2,1)S(1)} all-to-all(bf16[32,112,128]{2,1,0:T(8,128)(2,1)S(1)} %get-tuple-element.27), channel_id=1, replica_groups=mesh['fsdp'=32,'rep'=8] {'fsdp'}, dimensions={0} | all-to-all | bytes 1835008 | tf_op jit(solution)/shard_map/all_to_all | solution.py:640
  107.4 0.1 named.1.refs_0_
  107.5 1.4 collective-permute-start.8
  108.8 0.7 collective-permute-start.7
  109.6 1.6 %deal.1 = bf16[32,128,128]{2,1,0:T(8,128)(2,1)} custom-call(s32[256]{0:T(256)S(1)} %copy-done.2, bf16[32,112,128]{2,1,0:T(8,128)(2,1)S(1)} %all_to_all.25.arrived_ref), custom_call_target="tpu_custom_call" | custom-call | tf_op jit(solution)/shard_map/deal/pallas_call | solution.py:448
  111.2 5.6 %all-to-all-start.4 = ((bf16[32,128,128]{2,1,0:T(8,128)(2,1)}), bf16[32,128,128]{2,1,0:T(8,128)(2,1)}, u32[]{:S(2)}, u32[]{:S(2)}) async-start(bf16[32,128,128]{2,1,0:T(8,128)(2,1)} %deal.1), calls=%async_computation.4 | async-start | bytes 2097152 | tf_op jit(solution)/shard_map/all_to_all | solution.py:640
  116.7 0.0 collective-permute-done.8.refs_1_
  116.8 1.1 collective-permute-done.7.refs_0_
  117.8 0.0 collective-permute-start.9
  117.8 3.2 %collective-permute-start.11 = (bf16[33,32,128]{2,1,0:T(8,128)(2,1)S(1)}, bf16[33,32,128]{2,1,0:T(8,128)(2,1)S(1)}, u32[]{:S(2)}, u32[]{:S(2)}) collective-permute-start(bf16[33,32,128]{2,1,0:T(8,128)(2,1)S(1)} %get-tuple-element.37.refs_4_), channel_id=1, source_target_pairs={{0,7},{1,0},{2,1},{3,2},{4,3},{5,4},{6,5},{7,6},{8,15},{9,8},{10,9... | collective-permute-start | bytes 811016 | tf_op jit(solution)/shard_map/ppermute | solution.py:602
  121.1 0.1 collective-permute-start.13
  121.2 5.4 %collective-permute-done.9.refs_2_ = bf16[33,32,128]{2,1,0:T(8,128)(2,1)S(1)} collective-permute-done((bf16[33,32,128]{2,1,0:T(8,128)(2,1)S(1)}, bf16[33,32,128]{2,1,0:T(8,128)(2,1)S(1)}, u32[]{:S(2)}, u32[]{:S(2)}) %collective-permute-start.9) | collective-permute-done | bytes 270368 | tf_op jit(solution)/shard_map/ppermute | solution.py:602
  126.6 0.0 collective-permute-start.10
  126.6 7.0 %collective-permute-done.11.refs_5_ = bf16[33,32,128]{2,1,0:T(8,128)(2,1)S(1)} collective-permute-done((bf16[33,32,128]{2,1,0:T(8,128)(2,1)S(1)}, bf16[33,32,128]{2,1,0:T(8,128)(2,1)S(1)}, u32[]{:S(2)}, u32[]{:S(2)}) %collective-permute-start.11) | collective-permute-done | bytes 270368 | tf_op jit(solution)/shard_map/ppermute | solution.py:602
  133.6 3.8 %collective-permute-start.12 = (bf16[33,32,128]{2,1,0:T(8,128)(2,1)S(1)}, bf16[33,32,128]{2,1,0:T(8,128)(2,1)S(1)}, u32[]{:S(2)}, u32[]{:S(2)}) collective-permute-start(bf16[33,32,128]{2,1,0:T(8,128)(2,1)S(1)} %collective-permute-done.11.refs_5_), channel_id=1, source_target_pairs={{0,7},{1,0},{2,1},{3,2},{4,3},{5,4},{6,5},{7,6},{8,15},{9,8},{10,9... | collective-permute-start | bytes 811016 | tf_op jit(solution)/shard_map/ppermute | solution.py:602
  137.5 0.0 all-to-all-done.4.products_ref
  137.5 0.0 copy-done.5
  137.5 4.3 %factors.1 = (f32[1,3,128,1024]{3,2,1,0:T(8,128)}, f32[1,3,1024,128]{3,2,1,0:T(8,128)}) custom-call(s32[256]{0:T(256)S(1)} %copy-done.2, s32[2]{0:T(128)S(1)} %copy-done.5, bf16[32,64,128]{2,1,0:T(8,128)(2,1)S(1)} %get-tuple-element.30.own_ref, bf16[32,128,128]{2,1,0:T(8,128)(2,1)} %all-to-all-done.4.products_ref, f32[1,3,128,1024]{3,2,1,0:T(8,128)} %left_hbm.1, ...), custom_call_target="tpu_custom_call" | custom-call | flops 6291456 | bytes 15728640 | tf_op jit(solution)/shard_map/factors/pallas_call | solution.py:568
  141.8 0.0 collective-permute-done.13.refs_7_
  141.8 0.0 collective-permute-done.10.refs_3_
  141.8 0.0 collective-permute-done.12.refs_6_
  141.8 2.2 %finish.1 = bf16[32,32,1024]{2,1,0:T(8,128)(2,1)} custom-call(s32[1]{0:T(128)} %bitcast.rep_ref, s32[256]{0:T(256)S(1)} %copy-done.2, bf16[33,32,128]{2,1,0:T(8,128)(2,1)S(1)} %named.1.refs_0_, bf16[33,32,128]{2,1,0:T(8,128)(2,1)S(1)} %get-tuple-element.34.refs_1_, bf16[33,32,128]{2,1,0:T(8,128)(2,1)S(1)} %collective-permute-done.9.refs_2_, ...), custom_call_target="tpu_custom_call" | custom-call | tf_op jit(solution)/shard_map/finish/pallas_call | solution.py:492
  (6 shorter events, 0.1 us)
Async XLA Ops:
  0.6 9.7 %copy-start.6 = (s32[32]{0:T(128)S(1)}, s32[32]{0:T(128)}, u32[]{:S(2)}) copy-start(s32[32]{0:T(128)} %owner_ref.1) | copy-start | bytes 388
  0.6 9.7 %copy-start.7 = (s32[32]{0:T(128)S(1)}, s32[32]{0:T(128)}, u32[]{:S(2)}) copy-start(s32[32]{0:T(128)} %slot_ref.1) | copy-start | bytes 388
  2.8 23.1 %all-to-all-start = ((bf16[32,128,128]{2,1,0:T(8,128)(2,1)}), bf16[32,128,128]{2,1,0:T(8,128)(2,1)S(1)}, u32[]{:S(2)}, u32[]{:S(2)}) async-start(bf16[32,128,128]{2,1,0:T(8,128)(2,1)} %pack.1), calls=%async_computation | async-start | bytes 2097152 | tf_op jit(solution)/shard_map/all_to_all | solution.py:640
  13.9 28.9 %copy-start.1 = (s32[256]{0:T(256)}, s32[256]{0:T(256)S(1)}, u32[]{:S(2)}) copy-start(s32[256]{0:T(256)S(1)} %make_plan.1.plan_ref) | copy-start | bytes 3076
  13.9 20.5 %copy-start = (bf16[32,32,1024]{2,1,0:T(8,128)(2,1)S(1)}, bf16[32,32,1024]{2,1,0:T(8,128)(2,1)}, u32[]{:S(2)}) copy-start(bf16[32,32,1024]{2,1,0:T(8,128)(2,1)} %gradient_ref.1) | copy-start | bytes 6291460
  27.3 15.5 %all-to-all-start.1 = ((bf16[32,64,128]{2,1,0:T(8,128)(2,1)}), bf16[32,64,128]{2,1,0:T(8,128)(2,1)S(1)}, u32[]{:S(2)}, u32[]{:S(2)}) async-start(bf16[32,64,128]{2,1,0:T(8,128)(2,1)} %route.1), calls=%async_computation.1 | async-start | bytes 1048576 | tf_op jit(solution)/shard_map/all_to_all | solution.py:640
  32.7 10.1 %copy-start.3 = (s32[2]{0:T(128)}, s32[2]{0:T(128)S(1)}, u32[]{:S(2)}) copy-start(s32[2]{0:T(128)S(1)} %pad_add_fusion.place_ref) | copy-start | bytes 28
  43.4 12.0 %collective-permute-start.1 = (bf16[32,32,128]{2,1,0:T(8,128)(2,1)S(1)}, bf16[32,32,128]{2,1,0:T(8,128)(2,1)S(1)}, u32[]{:S(2)}, u32[]{:S(2)}) collective-permute-start(bf16[32,32,128]{2,1,0:T(8,128)(2,1)S(1)} %pick.1), channel_id=1, source_target_pairs={{0,7},{1,0},{2,1},{3,2},{4,3},{5,4},{6,5},{7,6},{8,15},{9,8},{10,9... | collective-permute-start | bytes 786440 | tf_op jit(solution)/shard_map/ppermute | solution.py:602
  49.3 9.5 %collective-permute-start = (bf16[32,32,128]{2,1,0:T(8,128)(2,1)S(1)}, bf16[32,32,128]{2,1,0:T(8,128)(2,1)S(1)}, u32[]{:S(2)}, u32[]{:S(2)}) collective-permute-start(bf16[32,32,128]{2,1,0:T(8,128)(2,1)S(1)} %pick.1), channel_id=1, source_target_pairs={{0,1},{1,2},{2,3},{3,4},{4,5},{5,6},{6,7},{7,0},{8,9},{9,10},{10,1... | collective-permute-start | bytes 786440 | tf_op jit(solution)/shard_map/ppermute | solution.py:602
  49.3 32.7 %all-to-all-start.2 = ((bf16[32,32,1024]{2,1,0:T(8,128)(2,1)}), bf16[32,32,1024]{2,1,0:T(8,128)(2,1)}, u32[]{:S(2)}, u32[]{:S(2)}) async-start(bf16[32,32,1024]{2,1,0:T(8,128)(2,1)} %gather.1), calls=%async_computation.2 | async-start | bytes 4194304 | tf_op jit(solution)/shard_map/all_to_all | solution.py:640
  58.7 16.9 %copy-start.2 = (s32[256]{0:T(256)S(1)}, s32[256]{0:T(256)}, u32[]{:S(2)}) copy-start(s32[256]{0:T(256)} %copy-done.1) | copy-start | bytes 3076
  58.7 16.9 %copy-start.4 = (s32[2]{0:T(128)S(1)}, s32[2]{0:T(128)}, u32[]{:S(2)}) copy-start(s32[2]{0:T(128)} %copy-done.3) | copy-start | bytes 28
  58.7 14.9 %collective-permute-start.4 = (bf16[32,32,128]{2,1,0:T(8,128)(2,1)S(1)}, bf16[32,32,128]{2,1,0:T(8,128)(2,1)S(1)}, u32[]{:S(2)}, u32[]{:S(2)}) collective-permute-start(bf16[32,32,128]{2,1,0:T(8,128)(2,1)S(1)} %get-tuple-element.26.refs_3_), channel_id=1, source_target_pairs={{0,7},{1,0},{2,1},{3,2},{4,3},{5,4},{6,5},{7,6},{8,15},{9,8},{10,9... | collective-permute-start | bytes 786440 | tf_op jit(solution)/shard_map/ppermute | solution.py:602
  59.1 14.5 %collective-permute-start.2 = (bf16[32,32,128]{2,1,0:T(8,128)(2,1)S(1)}, bf16[32,32,128]{2,1,0:T(8,128)(2,1)S(1)}, u32[]{:S(2)}, u32[]{:S(2)}) collective-permute-start(bf16[32,32,128]{2,1,0:T(8,128)(2,1)S(1)} %get-tuple-element.25.before_ref.refs_0_), channel_id=1, source_target_pairs={{0,1},{1,2},{2,3},{3,4},{4,5},{5,6},{6,7},{7,0},{8,9},{9,10},{10,1... | collective-permute-start | bytes 786440 | tf_op jit(solution)/shard_map/ppermute | solution.py:602
  60.8 16.2 %collective-permute-start.6 = (bf16[32,32,128]{2,1,0:T(8,128)(2,1)S(1)}, bf16[32,32,128]{2,1,0:T(8,128)(2,1)S(1)}, u32[]{:S(2)}, u32[]{:S(2)}) collective-permute-start(bf16[32,32,128]{2,1,0:T(8,128)(2,1)S(1)} %broadcast_select_fusion.1), channel_id=1, source_target_pairs={{0,3},{1,4},{2,5},{3,6},{4,7},{5,0},{6,1},{7,2},{8,13},{9,14},{10,... | collective-permute-start | bytes 786440 | tf_op jit(solution)/shard_map/ppermute | solution.py:618
  73.6 6.6 %collective-permute-start.5 = (bf16[32,32,128]{2,1,0:T(8,128)(2,1)S(1)}, bf16[32,32,128]{2,1,0:T(8,128)(2,1)S(1)}, u32[]{:S(2)}, u32[]{:S(2)}) collective-permute-start(bf16[32,32,128]{2,1,0:T(8,128)(2,1)S(1)} %collective-permute-done.4.refs_4_), channel_id=1, source_target_pairs={{0,7},{1,0},{2,1},{3,2},{4,3},{5,4},{6,5},{7,6},{8,15},{9,8},{10,9... | collective-permute-start | bytes 786440 | tf_op jit(solution)/shard_map/ppermute | solution.py:602
  73.6 8.2 %collective-permute-start.3 = (bf16[32,32,128]{2,1,0:T(8,128)(2,1)S(1)}, bf16[32,32,128]{2,1,0:T(8,128)(2,1)S(1)}, u32[]{:S(2)}, u32[]{:S(2)}) collective-permute-start(bf16[32,32,128]{2,1,0:T(8,128)(2,1)S(1)} %collective-permute-done.2.refs_1_), channel_id=1, source_target_pairs={{0,1},{1,2},{2,3},{3,4},{4,5},{5,6},{6,7},{7,0},{8,9},{9,10},{10,1... | collective-permute-start | bytes 786440 | tf_op jit(solution)/shard_map/ppermute | solution.py:602
  107.5 9.3 %collective-permute-start.8 = (bf16[33,32,128]{2,1,0:T(8,128)(2,1)S(1)}, bf16[33,32,128]{2,1,0:T(8,128)(2,1)S(1)}, u32[]{:S(2)}, u32[]{:S(2)}) collective-permute-start(bf16[33,32,128]{2,1,0:T(8,128)(2,1)S(1)} %named.1.refs_0_), channel_id=1, source_target_pairs={{0,7},{1,0},{2,1},{3,2},{4,3},{5,4},{6,5},{7,6},{8,15},{9,8},{10,9... | collective-permute-start | bytes 811016 | tf_op jit(solution)/shard_map/ppermute | solution.py:602
  108.8 9.0 %collective-permute-start.7 = (bf16[33,32,128]{2,1,0:T(8,128)(2,1)S(1)}, bf16[33,32,128]{2,1,0:T(8,128)(2,1)S(1)}, u32[]{:S(2)}, u32[]{:S(2)}) collective-permute-start(bf16[33,32,128]{2,1,0:T(8,128)(2,1)S(1)} %named.1.refs_0_), channel_id=1, source_target_pairs={{0,1},{1,2},{2,3},{3,4},{4,5},{5,6},{6,7},{7,0},{8,9},{9,10},{10,1... | collective-permute-start | bytes 811016 | tf_op jit(solution)/shard_map/ppermute | solution.py:602
  111.2 26.3 %all-to-all-start.4 = ((bf16[32,128,128]{2,1,0:T(8,128)(2,1)}), bf16[32,128,128]{2,1,0:T(8,128)(2,1)}, u32[]{:S(2)}, u32[]{:S(2)}) async-start(bf16[32,128,128]{2,1,0:T(8,128)(2,1)} %deal.1), calls=%async_computation.4 | async-start | bytes 2097152 | tf_op jit(solution)/shard_map/all_to_all | solution.py:640
  117.8 19.7 %copy-start.5 = (s32[2]{0:T(128)S(1)}, s32[2]{0:T(128)}, u32[]{:S(2)}) copy-start(s32[2]{0:T(128)} %copy-done.3) | copy-start | bytes 28
  117.8 8.8 %collective-permute-start.9 = (bf16[33,32,128]{2,1,0:T(8,128)(2,1)S(1)}, bf16[33,32,128]{2,1,0:T(8,128)(2,1)S(1)}, u32[]{:S(2)}, u32[]{:S(2)}) collective-permute-start(bf16[33,32,128]{2,1,0:T(8,128)(2,1)S(1)} %get-tuple-element.34.refs_1_), channel_id=1, source_target_pairs={{0,1},{1,2},{2,3},{3,4},{4,5},{5,6},{6,7},{7,0},{8,9},{9,10},{10,1... | collective-permute-start | bytes 811016 | tf_op jit(solution)/shard_map/ppermute | solution.py:602
  117.8 15.8 %collective-permute-start.11 = (bf16[33,32,128]{2,1,0:T(8,128)(2,1)S(1)}, bf16[33,32,128]{2,1,0:T(8,128)(2,1)S(1)}, u32[]{:S(2)}, u32[]{:S(2)}) collective-permute-start(bf16[33,32,128]{2,1,0:T(8,128)(2,1)S(1)} %get-tuple-element.37.refs_4_), channel_id=1, source_target_pairs={{0,7},{1,0},{2,1},{3,2},{4,3},{5,4},{6,5},{7,6},{8,15},{9,8},{10,9... | collective-permute-start | bytes 811016 | tf_op jit(solution)/shard_map/ppermute | solution.py:602
  121.1 20.7 %collective-permute-start.13 = (bf16[33,32,128]{2,1,0:T(8,128)(2,1)S(1)}, bf16[33,32,128]{2,1,0:T(8,128)(2,1)S(1)}, u32[]{:S(2)}, u32[]{:S(2)}) collective-permute-start(bf16[33,32,128]{2,1,0:T(8,128)(2,1)S(1)} %broadcast_select_fusion), channel_id=1, source_target_pairs={{0,3},{1,4},{2,5},{3,6},{4,7},{5,0},{6,1},{7,2},{8,13},{9,14},{10,... | collective-permute-start | bytes 811016 | tf_op jit(solution)/shard_map/ppermute | solution.py:618
  126.6 15.2 %collective-permute-start.10 = (bf16[33,32,128]{2,1,0:T(8,128)(2,1)S(1)}, bf16[33,32,128]{2,1,0:T(8,128)(2,1)S(1)}, u32[]{:S(2)}, u32[]{:S(2)}) collective-permute-start(bf16[33,32,128]{2,1,0:T(8,128)(2,1)S(1)} %collective-permute-done.9.refs_2_), channel_id=1, source_target_pairs={{0,1},{1,2},{2,3},{3,4},{4,5},{5,6},{6,7},{7,0},{8,9},{9,10},{10,1... | collective-permute-start | bytes 811016 | tf_op jit(solution)/shard_map/ppermute | solution.py:602
  133.6 8.1 %collective-permute-start.12 = (bf16[33,32,128]{2,1,0:T(8,128)(2,1)S(1)}, bf16[33,32,128]{2,1,0:T(8,128)(2,1)S(1)}, u32[]{:S(2)}, u32[]{:S(2)}) collective-permute-start(bf16[33,32,128]{2,1,0:T(8,128)(2,1)S(1)} %collective-permute-done.11.refs_5_), channel_id=1, source_target_pairs={{0,7},{1,0},{2,1},{3,2},{4,3},{5,4},{6,5},{7,6},{8,15},{9,8},{10,9... | collective-permute-start | bytes 811016 | tf_op jit(solution)/shard_map/ppermute | solution.py:602

commit v7 on v6

--- a/solution.py
+++ b/solution.py
@@ -122,7 +122,7 @@
     )(owner, slot)
 
 
-def cut(left_ref, right_ref, slot, out_ref, base):
+def cut(left_ref, slot, out_ref, base):
     for index in range(out_ref.shape[0]):
         row, column = row_piece(index)
         rows = pl.ds(row, TILE)
@@ -130,36 +130,45 @@
         out_ref[index, base + TILE : base + ROWS] = left_ref[
             slot, rows, column + LANES : column + 2 * LANES
         ]
-        out_ref[index, base + ROWS : base + 2 * ROWS] = right_ref[
-            slot, ROWS * index : ROWS * (index + 1)
-        ]
-
-
-def pack_kernel(left_hbm, right_hbm, spare_hbm, left_ref, right_ref, spare_ref, sems):
-    reads, writes = [], []
-    for spare in range(left_ref.shape[0]):
-        pair = (
-            pltpu.make_async_copy(left_hbm.at[spare + 1], left_ref.at[spare], sems.at[0, spare]),
-            pltpu.make_async_copy(right_hbm.at[spare + 1], right_ref.at[spare], sems.at[1, spare]),
+
+
+def pack_kernel(left_hbm, right_hbm, spare_hbm, left_ref, spare_ref, sems):
+    spares = left_ref.shape[0]
+    lefts, rights, writes = [], [], []
+    for spare in range(spares):
+        part = pl.ds(2 * ROWS * spare + ROWS, ROWS)
+        lefts.append(
+            pltpu.make_async_copy(left_hbm.at[spare + 1], left_ref.at[spare], sems.at[0, spare])
         )
-        for copy in pair:
-            copy.start()
-        reads.append(pair)
-    for spare, pair in enumerate(reads):
-        for copy in pair:
-            copy.wait()
-        cut(left_ref, right_ref, spare, spare_ref, 2 * ROWS * spare)
-        part = (slice(None), pl.ds(2 * ROWS * spare, 2 * ROWS))
-        copy = pltpu.make_async_copy(spare_ref.at[part], spare_hbm.at[part], sems.at[2, spare])
+        rights.append(
+            pltpu.make_async_copy(
+                right_hbm.at[spare + 1], spare_ref.at[:, part], sems.at[1, spare]
+            )
+        )
+        lefts[spare].start()
+        rights[spare].start()
+
+    def write(first, kind, spare):
+        part = (slice(None), pl.ds(first, ROWS))
+        copy = pltpu.make_async_copy(spare_ref.at[part], spare_hbm.at[part], sems.at[kind, spare])
         copy.start()
         writes.append(copy)
+
+    for spare in range(spares):
+        base = 2 * ROWS * spare
+        lefts[spare].wait()
+        cut(left_ref, spare, spare_ref, base)
+        write(base, 2, spare)
+        rights[spare].wait()
+        write(base + ROWS, 3, spare)
     for copy in writes:
         copy.wait()
 
 
 def pack(left, right, pieces):
     hbm = pl.BlockSpec(memory_space=pltpu.HBM)
-    spares = left.shape[0] - 1
+    slots = left.shape[0]
+    spares = slots - 1
     shape = (pieces, spares * 2 * ROWS, LANES)
     return pl.pallas_call(
         pack_kernel,
@@ -168,34 +177,34 @@
         out_shape=pltpu.HBM(shape, BF16),
         scratch_shapes=[
             pltpu.VMEM((spares,) + left.shape[1:], BF16),
-            pltpu.VMEM((spares,) + right.shape[1:], BF16),
             pltpu.VMEM(shape, BF16),
-            pltpu.SemaphoreType.DMA((3, spares)),
+            pltpu.SemaphoreType.DMA((4, spares)),
         ],
         compiler_params=params(8),
         name="pack",
-    )(*in_hbm(left, right))
-
-
-def keep_kernel(place_ref, plan_ref, left_hbm, right_hbm, kept_ref, left_ref, right_ref, sems):
+    )(*in_hbm(left, right.reshape(slots, pieces, ROWS, LANES)))
+
+
+def keep_kernel(place_ref, plan_ref, left_hbm, right_hbm, kept_ref, left_ref, sems):
     slots = left_hbm.shape[0]
     first = jnp.int32(slots - 1)
     for slot in reversed(range(slots - 1)):
         first = jnp.where(plan_ref[SOURCE + place_ref[1] * slots + slot] >= 0, slot, first)
     copies = (
         pltpu.make_async_copy(left_hbm.at[first], left_ref.at[0], sems.at[0]),
-        pltpu.make_async_copy(right_hbm.at[first], right_ref.at[0], sems.at[1]),
+        pltpu.make_async_copy(right_hbm.at[first], kept_ref.at[:, pl.ds(ROWS, ROWS)], sems.at[1]),
     )
     for copy in copies:
         copy.start()
-    for copy in copies:
-        copy.wait()
-    cut(left_ref, right_ref, 0, kept_ref, 0)
+    copies[0].wait()
+    cut(left_ref, 0, kept_ref, 0)
+    copies[1].wait()
 
 
 def keep(place, plan, left, right, pieces):
     smem = pl.BlockSpec(memory_space=pltpu.SMEM)
     hbm = pl.BlockSpec(memory_space=pltpu.HBM)
+    slots = left.shape[0]
     return pl.pallas_call(
         keep_kernel,
         in_specs=[smem, smem, hbm, hbm],
@@ -203,12 +212,11 @@
         out_shape=jax.ShapeDtypeStruct((pieces, 2 * ROWS, LANES), BF16),
         scratch_shapes=[
             pltpu.VMEM((1,) + left.shape[1:], BF16),
-            pltpu.VMEM((1,) + right.shape[1:], BF16),
             pltpu.SemaphoreType.DMA((2,)),
         ],
         compiler_params=params(8),
         name="keep",
-    )(place, plan, *in_hbm(left, right))
+    )(place, plan, *in_hbm(left, right.reshape(slots, pieces, ROWS, LANES)))
 
 
 def route_kernel(plan_ref, arrived_ref, out_hbm, out_ref, sems):
@@ -350,21 +358,21 @@
         place(index, both_ref[index, :ROWS], rep * width)
 
     right_root = both_ref[:, ROWS:].reshape(order, width)
+    columns = pl.multiple_of(rep * width, width)
     rooted = []
+    right = jnp.zeros((width, order), F32)
     for part, copy in enumerate(blocks):
         copy.wait()
-        lines = block_ref[part * (pieces // parts) : (part + 1) * (pieces // parts)]
-        rooted.append(
-            jnp.dot(
-                lines.reshape(order // parts, order), right_root, preferred_element_type=F32
-            ).astype(BF16)
-        )
+        first, last = part * (pieces // parts), (part + 1) * (pieces // parts)
+        lines = block_ref[first:last].reshape(order // parts, order)
+        rooted.append(jnp.dot(lines, right_root, preferred_element_type=F32).astype(BF16))
+        own = block_ref[first:last, :, pl.ds(columns, width)].reshape(order // parts, width)
+        right += jnp.dot(own.T, lines, preferred_element_type=F32)
     rooted = jnp.concatenate(rooted, axis=0)
     precond = jnp.dot(left_ref[...], rooted, preferred_element_type=F32)
     out_ref[:, :ROWS, :] = precond.astype(BF16).reshape(pieces, rows, width)
 
     block = block_ref[...].reshape(order, order)
-    columns = pl.multiple_of(rep * width, width)
     own_columns = block_ref[:, :, pl.ds(columns, width)].reshape(order, width)
     own_rows = block_ref[pl.ds(rep * (width // rows), width // rows)].reshape(width, order)
     left = lax.dot_general(

time: 145 us -> 145 us (level)
  no operation moved by 1% of the time
where the time goes in v7:
time: 145 us; the launch traced here: 144 us
  waiting for transfers between devices  53 us (37%)
  starting transfers between devices  43.9 us (30%)
  Pallas kernels  24.9 us (17%)
  blocking collectives  21.1 us (15%)
    ppermute x12, waiting for transfers between devices, shift(): lax.ppermute(value, 'rep', [(i, (i + by) % size) for i in range(size)])  34.3 us
    all_to_all x4, starting transfers between devices, exchange(): lax.all_to_all(value, 'fsdp', split_axis=0, concat_axis=0, tiled=True)  24.1 us
    all_to_all x1, blocking collectives, exchange(): lax.all_to_all(value, 'fsdp', split_axis=0, concat_axis=0, tiled=True)  21.1 us
    ppermute x12, starting transfers between devices, shift(): lax.ppermute(value, 'rep', [(i, (i + by) % size) for i in range(size)])  19.2 us
    all_to_all x4, waiting for transfers between devices, exchange(): lax.all_to_all(value, 'fsdp', split_axis=0, concat_axis=0, tiled=True)  18.6 us
    pallas_call x1, Pallas kernels, factors(): pl.pallas_call(factor_kernel, in_specs=[pl.BlockSpec(memory_space=pltpu.S...  4.26 us
    pallas_call x1, Pallas kernels, block_shares(): pl.pallas_call(block_kernel, in_specs=[pl.BlockSpec(memory_space=pltpu.SM...  4.23 us
    pallas_call x1, Pallas kernels, make_plan(): pl.pallas_call(plan_kernel, in_specs=[smem, smem], out_specs=smem, out_sh...  3.52 us
  transfers between devices with their start and end apart: 18, of which 11 were waited for; matrix products, arithmetic and copies ran while one was open for 0% of the time, Pallas kernels for 10%

profile of v7, /device:TPU:8, one launch (start us, length us, event | category | flops | bytes accessed | tf_op | source)
XLA Modules:
  0.0 144.1 jit_solution(3778497273333973626)
XLA Ops:
  0.6 0.0 copy-start.6
  0.6 0.0 copy-start.7
  0.7 2.0 %pack.1 = bf16[32,128,128]{2,1,0:T(8,128)(2,1)} custom-call(bf16[3,128,1024]{2,1,0:T(8,128)(2,1)} %bitcast.4, bf16[3,32,32,128]{3,2,1,0:T(8,128)(2,1)} %bitcast.6), custom_call_target="tpu_custom_call" | custom-call | tf_op jit(solution)/shard_map/pack/pallas_call | solution.py:173
  2.7 7.5 %all-to-all-start = ((bf16[32,128,128]{2,1,0:T(8,128)(2,1)}), bf16[32,128,128]{2,1,0:T(8,128)(2,1)S(1)}, u32[]{:S(2)}, u32[]{:S(2)}) async-start(bf16[32,128,128]{2,1,0:T(8,128)(2,1)} %pack.1), calls=%async_computation | async-start | bytes 2097152 | tf_op jit(solution)/shard_map/all_to_all | solution.py:648
  10.2 0.0 copy-done.6
  10.3 0.0 copy-done.7
  10.3 3.5 %make_plan.1.plan_ref = s32[256]{0:T(256)S(1)} custom-call(s32[32]{0:T(128)S(1)} %copy-done.6, s32[32]{0:T(128)S(1)} %copy-done.7), custom_call_target="tpu_custom_call" | custom-call | tf_op jit(solution)/shard_map/make_plan/pallas_call | solution.py:114
  13.8 0.0 copy-start.1
  13.8 0.0 copy-start
  13.8 12.0 %all-to-all-done.arrived_ref = bf16[32,128,128]{2,1,0:T(8,128)(2,1)S(1)} async-done(((bf16[32,128,128]{2,1,0:T(8,128)(2,1)}), bf16[32,128,128]{2,1,0:T(8,128)(2,1)S(1)}, u32[]{:S(2)}, u32[]{:S(2)}) %all-to-all-start) | async-done | bytes 1048608 | tf_op jit(solution)/shard_map/all_to_all | solution.py:648
  25.8 1.4 route.1
  27.2 5.3 %all-to-all-start.1 = ((bf16[32,64,128]{2,1,0:T(8,128)(2,1)}), bf16[32,64,128]{2,1,0:T(8,128)(2,1)S(1)}, u32[]{:S(2)}, u32[]{:S(2)}) async-start(bf16[32,64,128]{2,1,0:T(8,128)(2,1)} %route.1), calls=%async_computation.1 | async-start | bytes 1048576 | tf_op jit(solution)/shard_map/all_to_all | solution.py:648
  32.5 0.1 pad_add_fusion.place_ref
  32.6 0.0 copy-start.3
  32.6 1.6 %keep.1.kept_ref = bf16[32,64,128]{2,1,0:T(8,128)(2,1)S(1)} custom-call(s32[2]{0:T(128)S(1)} %pad_add_fusion.place_ref, s32[256]{0:T(256)S(1)} %make_plan.1.plan_ref, bf16[3,128,1024]{2,1,0:T(8,128)(2,1)} %bitcast.5, bf16[3,32,32,128]{3,2,1,0:T(8,128)(2,1)} %bitcast.7), custom_call_target="tpu_custom_call" | custom-call | tf_op jit(solution)/shard_map/keep/pallas_call | solution.py:208
  34.2 0.0 copy-done
  34.2 2.0 %gather.1 = bf16[32,32,1024]{2,1,0:T(8,128)(2,1)} custom-call(s32[256]{0:T(256)S(1)} %make_plan.1.plan_ref, bf16[32,32,1024]{2,1,0:T(8,128)(2,1)S(1)} %copy-done), custom_call_target="tpu_custom_call" | custom-call | tf_op jit(solution)/shard_map/gather/pallas_call | solution.py:316
  36.2 6.4 %all-to-all-done.1.roots_ref = bf16[32,64,128]{2,1,0:T(8,128)(2,1)S(1)} async-done(((bf16[32,64,128]{2,1,0:T(8,128)(2,1)}), bf16[32,64,128]{2,1,0:T(8,128)(2,1)S(1)}, u32[]{:S(2)}, u32[]{:S(2)}) %all-to-all-start.1) | async-done | bytes 524320 | tf_op jit(solution)/shard_map/all_to_all | solution.py:648
  42.7 0.0 copy-done.1
  42.7 0.0 copy-done.3
  42.7 0.6 pick.1
  43.3 5.9 %collective-permute-start.1 = (bf16[32,32,128]{2,1,0:T(8,128)(2,1)S(1)}, bf16[32,32,128]{2,1,0:T(8,128)(2,1)S(1)}, u32[]{:S(2)}, u32[]{:S(2)}) collective-permute-start(bf16[32,32,128]{2,1,0:T(8,128)(2,1)S(1)} %pick.1), channel_id=1, source_target_pairs={{0,7},{1,0},{2,1},{3,2},{4,3},{5,4},{6,5},{7,6},{8,15},{9,8},{10,9... | collective-permute-start | bytes 786440 | tf_op jit(solution)/shard_map/ppermute | solution.py:610
  49.2 0.0 collective-permute-start
  49.2 5.6 %all-to-all-start.2 = ((bf16[32,32,1024]{2,1,0:T(8,128)(2,1)}), bf16[32,32,1024]{2,1,0:T(8,128)(2,1)}, u32[]{:S(2)}, u32[]{:S(2)}) async-start(bf16[32,32,1024]{2,1,0:T(8,128)(2,1)} %gather.1), calls=%async_computation.2 | async-start | bytes 4194304 | tf_op jit(solution)/shard_map/all_to_all | solution.py:648
  54.8 0.4 collective-permute-done.1.refs_1_
  55.2 3.4 %collective-permute-done.refs_0_ = bf16[32,32,128]{2,1,0:T(8,128)(2,1)S(1)} collective-permute-done((bf16[32,32,128]{2,1,0:T(8,128)(2,1)S(1)}, bf16[32,32,128]{2,1,0:T(8,128)(2,1)S(1)}, u32[]{:S(2)}, u32[]{:S(2)}) %collective-permute-start) | collective-permute-done | bytes 262176 | tf_op jit(solution)/shard_map/ppermute | solution.py:610
  58.7 0.0 copy-start.2
  58.7 0.4 collective-permute-start.4
  59.0 1.7 %collective-permute-start.2 = (bf16[32,32,128]{2,1,0:T(8,128)(2,1)S(1)}, bf16[32,32,128]{2,1,0:T(8,128)(2,1)S(1)}, u32[]{:S(2)}, u32[]{:S(2)}) collective-permute-start(bf16[32,32,128]{2,1,0:T(8,128)(2,1)S(1)} %get-tuple-element.25.before_ref.refs_0_), channel_id=1, source_target_pairs={{0,1},{1,2},{2,3},{3,4},{4,5},{5,6},{6,7},{7,0},{8,9},{9,10},{10,1... | collective-permute-start | bytes 786440 | tf_op jit(solution)/shard_map/ppermute | solution.py:610
  60.7 0.6 collective-permute-start.6
  61.3 12.2 %collective-permute-done.4.refs_4_ = bf16[32,32,128]{2,1,0:T(8,128)(2,1)S(1)} collective-permute-done((bf16[32,32,128]{2,1,0:T(8,128)(2,1)S(1)}, bf16[32,32,128]{2,1,0:T(8,128)(2,1)S(1)}, u32[]{:S(2)}, u32[]{:S(2)}) %collective-permute-start.4) | collective-permute-done | bytes 262176 | tf_op jit(solution)/shard_map/ppermute | solution.py:610
  73.5 0.0 collective-permute-start.5
  73.5 0.0 collective-permute-done.2.refs_1_
  73.5 2.0 %collective-permute-start.3 = (bf16[32,32,128]{2,1,0:T(8,128)(2,1)S(1)}, bf16[32,32,128]{2,1,0:T(8,128)(2,1)S(1)}, u32[]{:S(2)}, u32[]{:S(2)}) collective-permute-start(bf16[32,32,128]{2,1,0:T(8,128)(2,1)S(1)} %collective-permute-done.2.refs_1_), channel_id=1, source_target_pairs={{0,1},{1,2},{2,3},{3,4},{4,5},{5,6},{6,7},{7,0},{8,9},{9,10},{10,1... | collective-permute-start | bytes 786440 | tf_op jit(solution)/shard_map/ppermute | solution.py:610
  75.6 0.0 copy-done.2
  75.6 0.0 copy-done.4
  75.6 1.4 hold.1.both_hbm
  76.9 0.0 collective-permute-done.6.refs_6_
  76.9 3.2 %collective-permute-done.5.refs_5_ = bf16[32,32,128]{2,1,0:T(8,128)(2,1)S(1)} collective-permute-done((bf16[32,32,128]{2,1,0:T(8,128)(2,1)S(1)}, bf16[32,32,128]{2,1,0:T(8,128)(2,1)S(1)}, u32[]{:S(2)}, u32[]{:S(2)}) %collective-permute-start.5) | collective-permute-done | bytes 262176 | tf_op jit(solution)/shard_map/ppermute | solution.py:610
  80.1 1.6 %collective-permute-done.3.refs_2_ = bf16[32,32,128]{2,1,0:T(8,128)(2,1)S(1)} collective-permute-done((bf16[32,32,128]{2,1,0:T(8,128)(2,1)S(1)}, bf16[32,32,128]{2,1,0:T(8,128)(2,1)S(1)}, u32[]{:S(2)}, u32[]{:S(2)}) %collective-permute-start.3) | collective-permute-done | bytes 262176 | tf_op jit(solution)/shard_map/ppermute | solution.py:610
  81.7 0.2 all-to-all-done.2.block_hbm
  82.0 4.2 %block_shares.1 = (bf16[32,112,128]{2,1,0:T(8,128)(2,1)S(1)}, bf16[32,64,128]{2,1,0:T(8,128)(2,1)S(1)}) custom-call(s32[1]{0:T(128)} %bitcast.rep_ref, bf16[32,32,1024]{2,1,0:T(8,128)(2,1)} %all-to-all-done.2.block_hbm, bf16[32,64,128]{2,1,0:T(8,128)(2,1)} %hold.1.both_hbm, bf16[32,32,128]{2,1,0:T(8,128)(2,1)S(1)} %get-tuple-element.25.before_ref.refs_0_, ...), custom_call_target="tpu_custom_call" | custom-call | flops 1073741824 | bytes 6291456 | tf_op jit(solution)/shard_map/block_shares/pallas_call | solution.py:407
  86.2 21.1 %all_to_all.25.arrived_ref = bf16[32,112,128]{2,1,0:T(8,128)(2,1)S(1)} all-to-all(bf16[32,112,128]{2,1,0:T(8,128)(2,1)S(1)} %get-tuple-element.27), channel_id=1, replica_groups=mesh['fsdp'=32,'rep'=8] {'fsdp'}, dimensions={0} | all-to-all | bytes 1835008 | tf_op jit(solution)/shard_map/all_to_all | solution.py:648
  107.3 0.1 named.1.refs_0_
  107.4 1.4 collective-permute-start.8
  108.7 0.7 collective-permute-start.7
  109.5 1.6 %deal.1 = bf16[32,128,128]{2,1,0:T(8,128)(2,1)} custom-call(s32[256]{0:T(256)S(1)} %copy-done.2, bf16[32,112,128]{2,1,0:T(8,128)(2,1)S(1)} %all_to_all.25.arrived_ref), custom_call_target="tpu_custom_call" | custom-call | tf_op jit(solution)/shard_map/deal/pallas_call | solution.py:456
  111.1 5.6 %all-to-all-start.4 = ((bf16[32,128,128]{2,1,0:T(8,128)(2,1)}), bf16[32,128,128]{2,1,0:T(8,128)(2,1)}, u32[]{:S(2)}, u32[]{:S(2)}) async-start(bf16[32,128,128]{2,1,0:T(8,128)(2,1)} %deal.1), calls=%async_computation.4 | async-start | bytes 2097152 | tf_op jit(solution)/shard_map/all_to_all | solution.py:648
  116.7 0.0 collective-permute-done.8.refs_1_
  116.7 1.1 collective-permute-done.7.refs_0_
  117.7 0.0 collective-permute-start.9
  117.7 3.2 %collective-permute-start.11 = (bf16[33,32,128]{2,1,0:T(8,128)(2,1)S(1)}, bf16[33,32,128]{2,1,0:T(8,128)(2,1)S(1)}, u32[]{:S(2)}, u32[]{:S(2)}) collective-permute-start(bf16[33,32,128]{2,1,0:T(8,128)(2,1)S(1)} %get-tuple-element.37.refs_4_), channel_id=1, source_target_pairs={{0,7},{1,0},{2,1},{3,2},{4,3},{5,4},{6,5},{7,6},{8,15},{9,8},{10,9... | collective-permute-start | bytes 811016 | tf_op jit(solution)/shard_map/ppermute | solution.py:610
  121.0 0.1 collective-permute-start.13
  121.1 5.4 %collective-permute-done.9.refs_2_ = bf16[33,32,128]{2,1,0:T(8,128)(2,1)S(1)} collective-permute-done((bf16[33,32,128]{2,1,0:T(8,128)(2,1)S(1)}, bf16[33,32,128]{2,1,0:T(8,128)(2,1)S(1)}, u32[]{:S(2)}, u32[]{:S(2)}) %collective-permute-start.9) | collective-permute-done | bytes 270368 | tf_op jit(solution)/shard_map/ppermute | solution.py:610
  126.5 0.0 collective-permute-start.10
  126.5 7.0 %collective-permute-done.11.refs_5_ = bf16[33,32,128]{2,1,0:T(8,128)(2,1)S(1)} collective-permute-done((bf16[33,32,128]{2,1,0:T(8,128)(2,1)S(1)}, bf16[33,32,128]{2,1,0:T(8,128)(2,1)S(1)}, u32[]{:S(2)}, u32[]{:S(2)}) %collective-permute-start.11) | collective-permute-done | bytes 270368 | tf_op jit(solution)/shard_map/ppermute | solution.py:610
  133.6 3.8 %collective-permute-start.12 = (bf16[33,32,128]{2,1,0:T(8,128)(2,1)S(1)}, bf16[33,32,128]{2,1,0:T(8,128)(2,1)S(1)}, u32[]{:S(2)}, u32[]{:S(2)}) collective-permute-start(bf16[33,32,128]{2,1,0:T(8,128)(2,1)S(1)} %collective-permute-done.11.refs_5_), channel_id=1, source_target_pairs={{0,7},{1,0},{2,1},{3,2},{4,3},{5,4},{6,5},{7,6},{8,15},{9,8},{10,9... | collective-permute-start | bytes 811016 | tf_op jit(solution)/shard_map/ppermute | solution.py:610
  137.4 0.0 all-to-all-done.4.products_ref
  137.4 0.0 copy-done.5
  137.4 4.3 %factors.1 = (f32[1,3,128,1024]{3,2,1,0:T(8,128)}, f32[1,3,1024,128]{3,2,1,0:T(8,128)}) custom-call(s32[256]{0:T(256)S(1)} %copy-done.2, s32[2]{0:T(128)S(1)} %copy-done.5, bf16[32,64,128]{2,1,0:T(8,128)(2,1)S(1)} %get-tuple-element.30.own_ref, bf16[32,128,128]{2,1,0:T(8,128)(2,1)} %all-to-all-done.4.products_ref, f32[1,3,128,1024]{3,2,1,0:T(8,128)} %left_hbm.1, ...), custom_call_target="tpu_custom_call" | custom-call | flops 6291456 | bytes 15728640 | tf_op jit(solution)/shard_map/factors/pallas_call | solution.py:576
  141.7 0.0 collective-permute-done.13.refs_7_
  141.7 0.0 collective-permute-done.10.refs_3_
  141.7 0.0 collective-permute-done.12.refs_6_
  141.7 2.2 %finish.1 = bf16[32,32,1024]{2,1,0:T(8,128)(2,1)} custom-call(s32[1]{0:T(128)} %bitcast.rep_ref, s32[256]{0:T(256)S(1)} %copy-done.2, bf16[33,32,128]{2,1,0:T(8,128)(2,1)S(1)} %named.1.refs_0_, bf16[33,32,128]{2,1,0:T(8,128)(2,1)S(1)} %get-tuple-element.34.refs_1_, bf16[33,32,128]{2,1,0:T(8,128)(2,1)S(1)} %collective-permute-done.9.refs_2_, ...), custom_call_target="tpu_custom_call" | custom-call | tf_op jit(solution)/shard_map/finish/pallas_call | solution.py:500
  (6 shorter events, 0.1 us)
Async XLA Ops:
  0.6 9.6 %copy-start.6 = (s32[32]{0:T(128)S(1)}, s32[32]{0:T(128)}, u32[]{:S(2)}) copy-start(s32[32]{0:T(128)} %owner_ref.1) | copy-start | bytes 388
  0.6 9.6 %copy-start.7 = (s32[32]{0:T(128)S(1)}, s32[32]{0:T(128)}, u32[]{:S(2)}) copy-start(s32[32]{0:T(128)} %slot_ref.1) | copy-start | bytes 388
  2.7 23.1 %all-to-all-start = ((bf16[32,128,128]{2,1,0:T(8,128)(2,1)}), bf16[32,128,128]{2,1,0:T(8,128)(2,1)S(1)}, u32[]{:S(2)}, u32[]{:S(2)}) async-start(bf16[32,128,128]{2,1,0:T(8,128)(2,1)} %pack.1), calls=%async_computation | async-start | bytes 2097152 | tf_op jit(solution)/shard_map/all_to_all | solution.py:648
  13.8 28.9 %copy-start.1 = (s32[256]{0:T(256)}, s32[256]{0:T(256)S(1)}, u32[]{:S(2)}) copy-start(s32[256]{0:T(256)S(1)} %make_plan.1.plan_ref) | copy-start | bytes 3076
  13.8 20.4 %copy-start = (bf16[32,32,1024]{2,1,0:T(8,128)(2,1)S(1)}, bf16[32,32,1024]{2,1,0:T(8,128)(2,1)}, u32[]{:S(2)}) copy-start(bf16[32,32,1024]{2,1,0:T(8,128)(2,1)} %gradient_ref.1) | copy-start | bytes 6291460
  27.2 15.5 %all-to-all-start.1 = ((bf16[32,64,128]{2,1,0:T(8,128)(2,1)}), bf16[32,64,128]{2,1,0:T(8,128)(2,1)S(1)}, u32[]{:S(2)}, u32[]{:S(2)}) async-start(bf16[32,64,128]{2,1,0:T(8,128)(2,1)} %route.1), calls=%async_computation.1 | async-start | bytes 1048576 | tf_op jit(solution)/shard_map/all_to_all | solution.py:648
  32.6 10.1 %copy-start.3 = (s32[2]{0:T(128)}, s32[2]{0:T(128)S(1)}, u32[]{:S(2)}) copy-start(s32[2]{0:T(128)S(1)} %pad_add_fusion.place_ref) | copy-start | bytes 28
  43.3 12.0 %collective-permute-start.1 = (bf16[32,32,128]{2,1,0:T(8,128)(2,1)S(1)}, bf16[32,32,128]{2,1,0:T(8,128)(2,1)S(1)}, u32[]{:S(2)}, u32[]{:S(2)}) collective-permute-start(bf16[32,32,128]{2,1,0:T(8,128)(2,1)S(1)} %pick.1), channel_id=1, source_target_pairs={{0,7},{1,0},{2,1},{3,2},{4,3},{5,4},{6,5},{7,6},{8,15},{9,8},{10,9... | collective-permute-start | bytes 786440 | tf_op jit(solution)/shard_map/ppermute | solution.py:610
  49.2 9.5 %collective-permute-start = (bf16[32,32,128]{2,1,0:T(8,128)(2,1)S(1)}, bf16[32,32,128]{2,1,0:T(8,128)(2,1)S(1)}, u32[]{:S(2)}, u32[]{:S(2)}) collective-permute-start(bf16[32,32,128]{2,1,0:T(8,128)(2,1)S(1)} %pick.1), channel_id=1, source_target_pairs={{0,1},{1,2},{2,3},{3,4},{4,5},{5,6},{6,7},{7,0},{8,9},{9,10},{10,1... | collective-permute-start | bytes 786440 | tf_op jit(solution)/shard_map/ppermute | solution.py:610
  49.2 32.7 %all-to-all-start.2 = ((bf16[32,32,1024]{2,1,0:T(8,128)(2,1)}), bf16[32,32,1024]{2,1,0:T(8,128)(2,1)}, u32[]{:S(2)}, u32[]{:S(2)}) async-start(bf16[32,32,1024]{2,1,0:T(8,128)(2,1)} %gather.1), calls=%async_computation.2 | async-start | bytes 4194304 | tf_op jit(solution)/shard_map/all_to_all | solution.py:648
  58.7 16.9 %copy-start.2 = (s32[256]{0:T(256)S(1)}, s32[256]{0:T(256)}, u32[]{:S(2)}) copy-start(s32[256]{0:T(256)} %copy-done.1) | copy-start | bytes 3076
  58.7 16.9 %copy-start.4 = (s32[2]{0:T(128)S(1)}, s32[2]{0:T(128)}, u32[]{:S(2)}) copy-start(s32[2]{0:T(128)} %copy-done.3) | copy-start | bytes 28
  58.7 14.9 %collective-permute-start.4 = (bf16[32,32,128]{2,1,0:T(8,128)(2,1)S(1)}, bf16[32,32,128]{2,1,0:T(8,128)(2,1)S(1)}, u32[]{:S(2)}, u32[]{:S(2)}) collective-permute-start(bf16[32,32,128]{2,1,0:T(8,128)(2,1)S(1)} %get-tuple-element.26.refs_3_), channel_id=1, source_target_pairs={{0,7},{1,0},{2,1},{3,2},{4,3},{5,4},{6,5},{7,6},{8,15},{9,8},{10,9... | collective-permute-start | bytes 786440 | tf_op jit(solution)/shard_map/ppermute | solution.py:610
  59.0 14.5 %collective-permute-start.2 = (bf16[32,32,128]{2,1,0:T(8,128)(2,1)S(1)}, bf16[32,32,128]{2,1,0:T(8,128)(2,1)S(1)}, u32[]{:S(2)}, u32[]{:S(2)}) collective-permute-start(bf16[32,32,128]{2,1,0:T(8,128)(2,1)S(1)} %get-tuple-element.25.before_ref.refs_0_), channel_id=1, source_target_pairs={{0,1},{1,2},{2,3},{3,4},{4,5},{5,6},{6,7},{7,0},{8,9},{9,10},{10,1... | collective-permute-start | bytes 786440 | tf_op jit(solution)/shard_map/ppermute | solution.py:610
  60.7 16.2 %collective-permute-start.6 = (bf16[32,32,128]{2,1,0:T(8,128)(2,1)S(1)}, bf16[32,32,128]{2,1,0:T(8,128)(2,1)S(1)}, u32[]{:S(2)}, u32[]{:S(2)}) collective-permute-start(bf16[32,32,128]{2,1,0:T(8,128)(2,1)S(1)} %broadcast_select_fusion.1), channel_id=1, source_target_pairs={{0,3},{1,4},{2,5},{3,6},{4,7},{5,0},{6,1},{7,2},{8,13},{9,14},{10,... | collective-permute-start | bytes 786440 | tf_op jit(solution)/shard_map/ppermute | solution.py:626
  73.5 6.6 %collective-permute-start.5 = (bf16[32,32,128]{2,1,0:T(8,128)(2,1)S(1)}, bf16[32,32,128]{2,1,0:T(8,128)(2,1)S(1)}, u32[]{:S(2)}, u32[]{:S(2)}) collective-permute-start(bf16[32,32,128]{2,1,0:T(8,128)(2,1)S(1)} %collective-permute-done.4.refs_4_), channel_id=1, source_target_pairs={{0,7},{1,0},{2,1},{3,2},{4,3},{5,4},{6,5},{7,6},{8,15},{9,8},{10,9... | collective-permute-start | bytes 786440 | tf_op jit(solution)/shard_map/ppermute | solution.py:610
  73.5 8.2 %collective-permute-start.3 = (bf16[32,32,128]{2,1,0:T(8,128)(2,1)S(1)}, bf16[32,32,128]{2,1,0:T(8,128)(2,1)S(1)}, u32[]{:S(2)}, u32[]{:S(2)}) collective-permute-start(bf16[32,32,128]{2,1,0:T(8,128)(2,1)S(1)} %collective-permute-done.2.refs_1_), channel_id=1, source_target_pairs={{0,1},{1,2},{2,3},{3,4},{4,5},{5,6},{6,7},{7,0},{8,9},{9,10},{10,1... | collective-permute-start | bytes 786440 | tf_op jit(solution)/shard_map/ppermute | solution.py:610
  107.4 9.3 %collective-permute-start.8 = (bf16[33,32,128]{2,1,0:T(8,128)(2,1)S(1)}, bf16[33,32,128]{2,1,0:T(8,128)(2,1)S(1)}, u32[]{:S(2)}, u32[]{:S(2)}) collective-permute-start(bf16[33,32,128]{2,1,0:T(8,128)(2,1)S(1)} %named.1.refs_0_), channel_id=1, source_target_pairs={{0,7},{1,0},{2,1},{3,2},{4,3},{5,4},{6,5},{7,6},{8,15},{9,8},{10,9... | collective-permute-start | bytes 811016 | tf_op jit(solution)/shard_map/ppermute | solution.py:610
  108.7 9.0 %collective-permute-start.7 = (bf16[33,32,128]{2,1,0:T(8,128)(2,1)S(1)}, bf16[33,32,128]{2,1,0:T(8,128)(2,1)S(1)}, u32[]{:S(2)}, u32[]{:S(2)}) collective-permute-start(bf16[33,32,128]{2,1,0:T(8,128)(2,1)S(1)} %named.1.refs_0_), channel_id=1, source_target_pairs={{0,1},{1,2},{2,3},{3,4},{4,5},{5,6},{6,7},{7,0},{8,9},{9,10},{10,1... | collective-permute-start | bytes 811016 | tf_op jit(solution)/shard_map/ppermute | solution.py:610
  111.1 26.3 %all-to-all-start.4 = ((bf16[32,128,128]{2,1,0:T(8,128)(2,1)}), bf16[32,128,128]{2,1,0:T(8,128)(2,1)}, u32[]{:S(2)}, u32[]{:S(2)}) async-start(bf16[32,128,128]{2,1,0:T(8,128)(2,1)} %deal.1), calls=%async_computation.4 | async-start | bytes 2097152 | tf_op jit(solution)/shard_map/all_to_all | solution.py:648
  117.7 19.7 %copy-start.5 = (s32[2]{0:T(128)S(1)}, s32[2]{0:T(128)}, u32[]{:S(2)}) copy-start(s32[2]{0:T(128)} %copy-done.3) | copy-start | bytes 28
  117.7 8.8 %collective-permute-start.9 = (bf16[33,32,128]{2,1,0:T(8,128)(2,1)S(1)}, bf16[33,32,128]{2,1,0:T(8,128)(2,1)S(1)}, u32[]{:S(2)}, u32[]{:S(2)}) collective-permute-start(bf16[33,32,128]{2,1,0:T(8,128)(2,1)S(1)} %get-tuple-element.34.refs_1_), channel_id=1, source_target_pairs={{0,1},{1,2},{2,3},{3,4},{4,5},{5,6},{6,7},{7,0},{8,9},{9,10},{10,1... | collective-permute-start | bytes 811016 | tf_op jit(solution)/shard_map/ppermute | solution.py:610
  117.7 15.8 %collective-permute-start.11 = (bf16[33,32,128]{2,1,0:T(8,128)(2,1)S(1)}, bf16[33,32,128]{2,1,0:T(8,128)(2,1)S(1)}, u32[]{:S(2)}, u32[]{:S(2)}) collective-permute-start(bf16[33,32,128]{2,1,0:T(8,128)(2,1)S(1)} %get-tuple-element.37.refs_4_), channel_id=1, source_target_pairs={{0,7},{1,0},{2,1},{3,2},{4,3},{5,4},{6,5},{7,6},{8,15},{9,8},{10,9... | collective-permute-start | bytes 811016 | tf_op jit(solution)/shard_map/ppermute | solution.py:610
  121.0 20.7 %collective-permute-start.13 = (bf16[33,32,128]{2,1,0:T(8,128)(2,1)S(1)}, bf16[33,32,128]{2,1,0:T(8,128)(2,1)S(1)}, u32[]{:S(2)}, u32[]{:S(2)}) collective-permute-start(bf16[33,32,128]{2,1,0:T(8,128)(2,1)S(1)} %broadcast_select_fusion), channel_id=1, source_target_pairs={{0,3},{1,4},{2,5},{3,6},{4,7},{5,0},{6,1},{7,2},{8,13},{9,14},{10,... | collective-permute-start | bytes 811016 | tf_op jit(solution)/shard_map/ppermute | solution.py:626
  126.5 15.2 %collective-permute-start.10 = (bf16[33,32,128]{2,1,0:T(8,128)(2,1)S(1)}, bf16[33,32,128]{2,1,0:T(8,128)(2,1)S(1)}, u32[]{:S(2)}, u32[]{:S(2)}) collective-permute-start(bf16[33,32,128]{2,1,0:T(8,128)(2,1)S(1)} %collective-permute-done.9.refs_2_), channel_id=1, source_target_pairs={{0,1},{1,2},{2,3},{3,4},{4,5},{5,6},{6,7},{7,0},{8,9},{9,10},{10,1... | collective-permute-start | bytes 811016 | tf_op jit(solution)/shard_map/ppermute | solution.py:610
  133.6 8.1 %collective-permute-start.12 = (bf16[33,32,128]{2,1,0:T(8,128)(2,1)S(1)}, bf16[33,32,128]{2,1,0:T(8,128)(2,1)S(1)}, u32[]{:S(2)}, u32[]{:S(2)}) collective-permute-start(bf16[33,32,128]{2,1,0:T(8,128)(2,1)S(1)} %collective-permute-done.11.refs_5_), channel_id=1, source_target_pairs={{0,7},{1,0},{2,1},{3,2},{4,3},{5,4},{6,5},{7,6},{8,15},{9,8},{10,9... | collective-permute-start | bytes 811016 | tf_op jit(solution)/shard_map/ppermute | solution.py:610
